TPU v7x, 256 devices: a whole 4x4x8 slice. The times are simulated.
256 devices in a mesh: gx: 8 (over z), gy: 32 (over y, x, core).
Axes of the slice: x: 4, y: 4, z: 8, core: 2. Of those that a mesh axis runs over, the one named last changes fastest.
Arguments:
- background: float32 [16, 128, 256, 128], P(None, 'gx', 'gy'), may hold values from -6 to 6
- conductivity: float32 [128, 256, 128], P('gx', 'gy'), may hold values from 0.5 to 4
- perturbation: float32 [128, 256, 128], P('gx', 'gy'), may hold values from -6 to 6
- electrodes: int32 [16], replicated, may hold values from 0 to 4194303
- pattern: int32 [16, 2], replicated, may hold values from 0 to 15, as said below
Outputs:
- tangent_fields: float32 [16, 128, 256, 128], P(None, 'gx', 'gy')
- sensitivity: float32 [128, 256, 128], P('gx', 'gy')
Inputs may be any that keep to these rules, and one draw needn't show every extreme that they name: `pattern`: each row names two different electrodes, and the first column names every electrode once.
All inputs are finite; a program needn't handle non-finite values.
Results may differ from a plain program's by a relative error of at most 0.00021.
Values sent between devices are 32-bit elements; how exact they have to be, the bound alone decides.
No kernel may reach another device: no remote copies, remote signals or barrier semaphores. Data moves between devices by JAX's collectives and lax.ppermute only.
A program may use at most 64 MiB of HBM per device.

v0:
```python
import math

import jax
import jax.numpy as jnp
from jax import lax
from jax.sharding import PartitionSpec as P

ITERS = 2


def with_halo(block, sides, width):
    for axis, dim in sides:
        count = lax.axis_size(axis)
        forward = [(i, i + 1) for i in range(count - 1)]
        backward = [(target, source) for source, target in forward]
        low = lax.ppermute(
            lax.slice_in_dim(block, block.shape[dim] - width, None, axis=dim), axis, forward
        )
        high = lax.ppermute(lax.slice_in_dim(block, 0, width, axis=dim), axis, backward)
        block = jnp.concatenate([low, block, high], axis=dim)
    return block


def neighbour_views(padded):
    lead = padded.ndim - 3

    def view(dx, dy, dz):
        idx = [slice(None)] * lead
        idx += [
            slice(1 + dx, padded.shape[lead] - 1 + dx),
            slice(1 + dy, padded.shape[lead + 1] - 1 + dy),
            slice(1 + dz, padded.shape[lead + 2] - 1 + dz),
        ]
        return padded[tuple(idx)]

    moves = [(1, 0, 0), (-1, 0, 0), (0, 1, 0), (0, -1, 0), (0, 0, 1), (0, 0, -1)]
    return (view(0, 0, 0), [view(a, b, c) for a, b, c in moves])


def stencil(field_pad, sigma_pad):
    centre, others = neighbour_views(field_pad)
    scent, sothers = neighbour_views(sigma_pad)
    result = 0.05 * centre
    for qj, sj in zip(others, sothers):
        result = result + 0.5 * (scent + sj) * (centre - qj)
    return result


def tangent_source(back_pad, pert_pad):
    centre, others = neighbour_views(back_pad)
    pcent, pothers = neighbour_views(pert_pad)
    result = jnp.zeros_like(centre)
    for qj, pj in zip(others, pothers):
        result = result - 0.5 * (pcent + pj) * (centre - qj)
    return result


def sens_terms(back_pad, adj_pad):
    centre, others = neighbour_views(back_pad)
    acent, aothers = neighbour_views(adj_pad)
    result = jnp.zeros(centre.shape[1:], jnp.float32)
    for qj, aj in zip(others, aothers):
        result = result - 0.5 * jnp.sum((centre - qj) * (acent - aj), axis=0)
    return result


def gram(left, right):
    count = left.shape[0]
    return jnp.dot(
        left.reshape(count, -1), right.reshape(count, -1).T, precision=lax.Precision.HIGHEST
    )


def combine(coeff, fields):
    count = fields.shape[0]
    return jnp.dot(coeff.T, fields.reshape(count, -1), precision=lax.Precision.HIGHEST).reshape(
        fields.shape
    )


def chol_solve(matrix, rhs):
    factor = jnp.linalg.cholesky(matrix)
    return jax.scipy.linalg.cho_solve((factor, True), rhs)


def zpad_depth(padded):
    return jnp.pad(padded, ((0, 0), (0, 0), (0, 0), (1, 1)))


def apply_operator(search, sigma_pad):
    rimmed = with_halo(search, (("gx", 1), ("gy", 2)), 1)
    return stencil(zpad_depth(rimmed), sigma_pad)


def residual_gram(resid):
    return lax.psum(gram(resid, resid), ("gx", "gy"))


def block_solve(rhs, sigma_pad):
    solution = jnp.zeros_like(rhs)
    resid = rhs
    search = rhs
    norms = residual_gram(resid)
    for step in range(ITERS):
        image = apply_operator(search, sigma_pad)
        curv = lax.psum(gram(search, image), ("gx", "gy"))
        alpha = chol_solve(curv, norms)
        solution = solution + combine(alpha, search)
        resid = resid - combine(alpha, image)
        if step + 1 < ITERS:
            fresh = residual_gram(resid)
            beta = chol_solve(norms, fresh)
            search = resid + combine(beta, search)
            norms = fresh
    return solution


def on_device(background, conductivity, perturbation, electrodes, pattern):
    count, size_x, size_y, size_z = background.shape
    coeffs = jnp.stack([conductivity, perturbation], axis=0)
    coeff_pad = zpad_depth(with_halo(coeffs, (("gx", 1), ("gy", 2)), 1))
    sigma_pad = coeff_pad[0]
    pert_pad = coeff_pad[1]
    back_pad = zpad_depth(with_halo(background, (("gx", 1), ("gy", 2)), 1))
    rhs = tangent_source(back_pad, pert_pad)
    tangent = block_solve(rhs, sigma_pad)
    total_x = size_x * lax.axis_size("gx")
    total_y = size_y * lax.axis_size("gy")
    plane = total_y * size_z
    coord_x = electrodes // plane
    remain = electrodes % plane
    coord_y = remain // size_z
    coord_z = remain % size_z
    local_x = coord_x - lax.axis_index("gx") * size_x
    local_y = coord_y - lax.axis_index("gy") * size_y
    inside = (local_x >= 0) & (local_x < size_x) & (local_y >= 0) & (local_y < size_y)
    local_flat = (local_x * size_y + local_y) * size_z + coord_z
    cell_ids = jnp.arange(size_x * size_y * size_z, dtype=jnp.int32)
    onehot = jnp.where(
        inside[:, None] & (local_flat[:, None] == cell_ids[None, :]), 1.0, 0.0
    ).astype(jnp.float32)
    flat = tangent.reshape(count, -1)
    probe = lax.psum(jnp.dot(flat, onehot.T, precision=lax.Precision.HIGHEST), ("gx", "gy"))
    elec_ids = jnp.arange(pattern.shape[0], dtype=jnp.int32)
    pairing = (
        jnp.where(pattern[None, :, 0] == elec_ids[:, None], 1.0, 0.0)
        - jnp.where(pattern[None, :, 1] == elec_ids[:, None], 1.0, 0.0)
    ).astype(jnp.float32)
    measured = jnp.dot(probe, pairing, precision=lax.Precision.HIGHEST)
    weight = jnp.dot(measured, pairing.T, precision=lax.Precision.HIGHEST)
    inject = jnp.dot(weight, onehot, precision=lax.Precision.HIGHEST)
    damping = 80.0 / math.sqrt(total_x * total_y * size_z)
    adj_rhs = damping * tangent + 8.0 * inject.reshape(tangent.shape)
    adjoint = block_solve(adj_rhs, sigma_pad)
    both = jnp.concatenate([background, adjoint], axis=0)
    both_pad = zpad_depth(with_halo(both, (("gx", 1), ("gy", 2)), 1))
    sens = sens_terms(both_pad[:count], both_pad[count:])
    return (tangent, sens)


def solution(mesh):
    in_specs = (P(None, "gx", "gy", None), P("gx", "gy", None), P("gx", "gy", None), P(), P())
    out_specs = (P(None, "gx", "gy", None), P("gx", "gy", None))
    return jax.shard_map(
        on_device, mesh=mesh, in_specs=in_specs, out_specs=out_specs, check_vma=False
    )
```

profile of v0, /device:TPU:2, one launch (start us, length us, event | category | flops | bytes accessed | tf_op | source)
XLA Modules:
  0.0 745.3 jit_solution(8466606743272323611)
XLA Ops:
  0.6 1.9 copy.44
  2.6 3.8 collective-permute-start.5
  9.7 5.2 collective-permute-start
  17.2 1.9 collective-permute-start.3
  19.2 2.4 collective-permute-start.2
  26.3 1.9 collective-permute-start.6
  28.2 2.4 collective-permute-start.7
  30.8 3.8 collective-permute-done.7
  37.6 4.8 collective-permute-start.9
  46.7 2.4 collective-permute-start.11
  50.6 2.6 collective-permute-done.11
  55.4 2.1 convolution_bitcast_fusion.13
  57.8 85.7 %all-reduce.8 = (f32[16,16]{0,1:T(8,128)S(1)}, f32[16,16]{0,1:T(8,128)}) all-reduce(f32[16,16]{0,1:T(8,128)S(1)} %convolution_bitcast_fusion.12, f32[16,16]{0,1:T(8,128)} %convolution_bitcast_fusion.13), channel_id=1, replica_groups=mesh['gx'=8,'gy'=32] {'gx','gy'}, use_global_device_ids=true, to_apply=%region_3.5 | all-reduce | flops 512 | bytes 4096 | tf_op jit(solution)/shard_map/psum | solution.py:96
  146.3 2.1 cholesky.104
  150.5 1.9 custom-call.12
  156.7 75.6 %psum.65 = f32[16,16]{1,0:T(8,128)S(1)} all-reduce(f32[16,16]{1,0:T(8,128)S(1)} %convolution_bitcast_fusion.10), channel_id=1, replica_groups=mesh['gx'=8,'gy'=32] {'gx','gy'}, use_global_device_ids=true, to_apply=%region_4.7 | all-reduce | flops 256 | bytes 2048 | tf_op jit(solution)/shard_map/psum | solution.py:96
  232.3 2.1 cholesky.115
  237.5 2.7 convolution_add_fusion.3
  241.5 4.5 collective-permute-start.13
  248.0 2.9 collective-permute-start.14
  250.9 2.1 collective-permute-start.15
  253.0 2.5 fusion.139
  258.2 2.1 convolution_bitcast_fusion.8
  260.2 75.0 %psum.66 = f32[16,16]{0,1:T(8,128)S(1)} all-reduce(f32[16,16]{0,1:T(8,128)S(1)} %convolution_bitcast_fusion.8), channel_id=1, replica_groups=mesh['gx'=8,'gy'=32] {'gx','gy'}, use_global_device_ids=true, to_apply=%region_5.8 | all-reduce | flops 256 | bytes 2048 | tf_op jit(solution)/shard_map/psum | solution.py:106
  339.8 2.7 convolution_add_fusion.2
  343.8 2.5 fusion.3
  346.4 75.3 %psum.67 = f32[16,16]{1,0:T(8,128)S(1)} all-reduce(f32[16,16]{1,0:T(8,128)S(1)} %fusion.3), channel_id=1, replica_groups=mesh['gx'=8,'gy'=32] {'gx','gy'}, use_global_device_ids=true, to_apply=%region_6.9 | all-reduce | flops 256 | bytes 2048 | tf_op jit(solution)/shard_map/psum | solution.py:143
  425.2 5.0 collective-permute-start.17
  432.4 2.2 collective-permute-start.18
  434.5 2.2 collective-permute-start.19
  438.1 2.9 collective-permute-done.19
  443.2 2.1 convolution_bitcast_fusion.6
  445.6 75.4 %all-reduce.7 = (f32[16,16]{0,1:T(8,128)S(1)}, f32[16,16]{0,1:T(8,128)}) all-reduce(f32[16,16]{0,1:T(8,128)S(1)} %convolution_bitcast_fusion.5, f32[16,16]{0,1:T(8,128)} %convolution_bitcast_fusion.6), channel_id=1, replica_groups=mesh['gx'=8,'gy'=32] {'gx','gy'}, use_global_device_ids=true, to_apply=%region_8.11 | all-reduce | flops 512 | bytes 4096 | tf_op jit(solution)/shard_map/psum | solution.py:96
  523.1 2.1 cholesky.137
  527.1 1.9 custom-call.15
  534.0 74.8 %psum.70 = f32[16,16]{1,0:T(8,128)S(1)} all-reduce(f32[16,16]{1,0:T(8,128)S(1)} %convolution_bitcast_fusion.3), channel_id=1, replica_groups=mesh['gx'=8,'gy'=32] {'gx','gy'}, use_global_device_ids=true, to_apply=%region_9.12 | all-reduce | flops 256 | bytes 2048 | tf_op jit(solution)/shard_map/psum | solution.py:96
  614.0 2.7 convolution_add_fusion.1
  618.0 4.5 collective-permute-start.21
  624.5 2.5 collective-permute-start.22
  630.4 3.3 collective-permute-done.23
  634.6 2.1 convolution_bitcast_fusion.1
  636.6 74.8 %psum.71 = f32[16,16]{0,1:T(8,128)S(1)} all-reduce(f32[16,16]{0,1:T(8,128)S(1)} %convolution_bitcast_fusion.1), channel_id=1, replica_groups=mesh['gx'=8,'gy'=32] {'gx','gy'}, use_global_device_ids=true, to_apply=%region_10.13 | all-reduce | flops 256 | bytes 2048 | tf_op jit(solution)/shard_map/psum | solution.py:106
  718.8 4.6 collective-permute-start.25
  725.9 2.9 collective-permute-start.26
  728.9 2.3 collective-permute-start.27
  731.1 1.9 collective-permute-done.26
  733.1 4.2 collective-permute-done.27
  737.3 4.4 select_maximum_fusion
  (173 shorter events, 89.5 us)
Async XLA Ops:
  0.6 25.0 %copy-start = (f32[16,16,8,128]{3,2,1,0:T(8,128)S(1)}, f32[16,16,8,128]{3,2,1,0:T(8,128)}, u32[]{:S(2)}) copy-start(f32[16,16,8,128]{3,2,1,0:T(8,128)} %param.8) | copy-start | bytes 3145732
  2.6 23.0 %collective-permute-start.5 = (f32[16,1,8,128]{3,0,2,1:T(8,128)S(1)}, f32[16,1,8,128]{3,0,2,1:T(8,128)S(1)}, u32[]{:S(2)}, u32[]{:S(2)}) collective-permute-start(f32[16,1,8,128]{3,0,2,1:T(8,128)S(1)} %get-tuple-element.45), channel_id=1, source_target_pairs={{0,32},{32,64},{64,96},{96,128},{128,160},{160,192},{192,224},{1,3... | collective-permute-start | bytes 196616 | tf_op jit(solution)/shard_map/ppermute | solution.py:16
  6.4 19.8 %collective-permute-start.4 = (f32[16,1,8,128]{3,0,2,1:T(8,128)S(1)}, f32[16,1,8,128]{3,0,2,1:T(8,128)S(1)}, u32[]{:S(2)}, u32[]{:S(2)}) collective-permute-start(f32[16,1,8,128]{3,0,2,1:T(8,128)S(1)} %get-tuple-element.44), channel_id=1, source_target_pairs={{32,0},{64,32},{96,64},{128,96},{160,128},{192,160},{224,192},{33,... | collective-permute-start | bytes 196616 | tf_op jit(solution)/shard_map/ppermute | solution.py:19
  8.5 7.7 %collective-permute-start.1 = (f32[2,1,8,128]{3,2,1,0:T(8,128)S(1)}, f32[2,1,8,128]{3,2,1,0:T(8,128)S(1)}, u32[]{:S(2)}, u32[]{:S(2)}) collective-permute-start(f32[2,1,8,128]{3,2,1,0:T(8,128)S(1)} %get-tuple-element.63), channel_id=1, source_target_pairs={{32,0},{64,32},{96,64},{128,96},{160,128},{192,160},{224,192},{33,... | collective-permute-start | bytes 24584 | tf_op jit(solution)/shard_map/ppermute | solution.py:19
  9.7 6.5 collective-permute-start
  17.2 5.6 collective-permute-start.3
  19.2 5.1 collective-permute-start.2
  26.3 4.6 collective-permute-start.6
  28.2 6.5 collective-permute-start.7
  36.3 8.4 %collective-permute-start.8 = (f32[16,1,8,128]{3,0,2,1:T(8,128)S(1)}, f32[16,1,8,128]{3,0,2,1:T(8,128)S(1)}, u32[]{:S(2)}, u32[]{:S(2)}) collective-permute-start(f32[16,1,8,128]{3,0,2,1:T(8,128)S(1)} %get-tuple-element.43), channel_id=1, source_target_pairs={{32,0},{64,32},{96,64},{128,96},{160,128},{192,160},{224,192},{33,... | collective-permute-start | bytes 196616 | tf_op jit(solution)/shard_map/ppermute | solution.py:19
  37.6 7.2 collective-permute-start.9
  44.8 5.8 collective-permute-start.10
  46.7 6.5 collective-permute-start.11
  155.1 90.9 %copy-start.8 = (s32[16]{0:T(128)S(1)}, s32[16]{0:T(128)}, u32[]{:S(2)}) copy-start(s32[16]{0:T(128)} %get-tuple-element.19) | copy-start | bytes 196
  155.1 90.9 %copy-start.9 = (s32[16]{0:T(128)S(1)}, s32[16]{0:T(128)}, u32[]{:S(2)}) copy-start(s32[16]{0:T(128)} %get-tuple-element.20) | copy-start | bytes 196
  155.2 90.9 %copy-start.10 = (s32[16]{0:T(128)S(1)}, s32[16]{0:T(128)}, u32[]{:S(2)}) copy-start(s32[16]{0:T(128)} %get-tuple-element.21) | copy-start | bytes 196
  240.2 7.7 %collective-permute-start.12 = (f32[16,1,8,128]{3,0,2,1:T(8,128)S(1)}, f32[16,1,8,128]{3,0,2,1:T(8,128)S(1)}, u32[]{:S(2)}, u32[]{:S(2)}) collective-permute-start(f32[16,1,8,128]{3,0,2,1:T(8,128)S(1)} %get-tuple-element.41), channel_id=1, source_target_pairs={{32,0},{64,32},{96,64},{128,96},{160,128},{192,160},{224,192},{33,... | collective-permute-start | bytes 196616 | tf_op jit(solution)/shard_map/ppermute | solution.py:19
  241.5 6.4 collective-permute-start.13
  247.0 6.0 copy-start.2
  248.0 7.5 %collective-permute-start.14 = (f32[16,18,1,128]{3,0,2,1:T(8,128)S(1)}, f32[16,18,1,128]{3,0,2,1:T(8,128)S(1)}, u32[]{:S(2)}, u32[]{:S(2)}) collective-permute-start(f32[16,18,1,128]{3,0,2,1:T(8,128)S(1)} %get-tuple-element.31), channel_id=1, source_target_pairs={{1,0},{2,1},{3,2},{4,3},{5,4},{6,5},{7,6},{8,7},{9,8},{10,9},{11,1... | collective-permute-start | bytes 442376 | tf_op jit(solution)/shard_map/ppermute | solution.py:19
  250.9 6.5 collective-permute-start.15
  339.7 81.9 %copy-start.6 = (s32[16]{0:T(128)S(1)}, s32[16]{0:T(128)}, u32[]{:S(2)}) copy-start(s32[16]{0:T(128)} %get-tuple-element.64) | copy-start | bytes 196
  339.7 81.9 %copy-start.7 = (s32[16]{0:T(128)S(1)}, s32[16]{0:T(128)}, u32[]{:S(2)}) copy-start(s32[16]{0:T(128)} %get-tuple-element.65) | copy-start | bytes 196
  339.8 82.1 %copy-start.11 = (pred[16]{0:T(512)(128)(4,1)S(1)}, pred[16]{0:T(512)(128)(4,1)}, u32[]{:S(2)}) copy-start(pred[16]{0:T(512)(128)(4,1)} %get-tuple-element.18) | copy-start | bytes 52
  339.8 82.1 %copy-start.12 = (s32[16]{0:T(128)S(1)}, s32[16]{0:T(128)}, u32[]{:S(2)}) copy-start(s32[16]{0:T(128)} %fusion.216) | copy-start | bytes 196
  342.8 1.0 copy-start.4
  423.9 8.4 %collective-permute-start.16 = (f32[16,1,8,128]{3,0,2,1:T(8,128)S(1)}, f32[16,1,8,128]{3,0,2,1:T(8,128)S(1)}, u32[]{:S(2)}, u32[]{:S(2)}) collective-permute-start(f32[16,1,8,128]{3,0,2,1:T(8,128)S(1)} %get-tuple-element.39), channel_id=1, source_target_pairs={{32,0},{64,32},{96,64},{128,96},{160,128},{192,160},{224,192},{33,... | collective-permute-start | bytes 196616 | tf_op jit(solution)/shard_map/ppermute | solution.py:19
  425.2 7.1 collective-permute-start.17
  432.4 5.8 collective-permute-start.18
  434.5 6.5 collective-permute-start.19
  521.1 8.7 %copy-start.5 = (f32[16,16]{0,1:T(8,128)}, f32[16,16]{0,1:T(8,128)S(1)}, u32[]{:S(2)}) copy-start(f32[16,16]{0,1:T(8,128)S(1)} %get-tuple-element.14) | copy-start | bytes 3076
  616.7 7.0 collective-permute-start.20
  618.0 6.4 collective-permute-start.21
  622.9 6.0 copy-start.3
  624.5 6.0 collective-permute-start.22
  627.0 6.7 collective-permute-start.23
  717.5 7.1 collective-permute-start.24
  718.8 7.1 collective-permute-start.25
  725.9 7.2 collective-permute-start.26
  728.9 12.9 %copy-start.1 = (f32[16,16,8,128]{3,2,1,0:T(8,128)S(1)}, f32[16,16,8,128]{3,2,1,0:T(8,128)}, u32[]{:S(2)}) copy-start(f32[16,16,8,128]{3,2,1,0:T(8,128)} %param.8) | copy-start | bytes 3145732
  728.9 8.4 %collective-permute-start.27 = (f32[32,18,1,128]{3,0,2,1:T(8,128)S(1)}, f32[32,18,1,128]{3,0,2,1:T(8,128)S(1)}, u32[]{:S(2)}, u32[]{:S(2)}) collective-permute-start(f32[32,18,1,128]{3,0,2,1:T(8,128)S(1)} %get-tuple-element.22), channel_id=1, source_target_pairs={{0,1},{1,2},{2,3},{3,4},{4,5},{5,6},{6,7},{7,8},{8,9},{9,10},{10,1... | collective-permute-start | bytes 884744 | tf_op jit(solution)/shard_map/ppermute | solution.py:16
where the time goes:
time: 757 us; the launch traced here: 745 us
  blocking collectives  537 us (71%)
  starting transfers between devices  73.4 us (10%)
  other arithmetic  53.4 us (7%)
  matrix products  37.2 us (5%)
  waiting for transfers between devices  25.3 us (3%)
  local copies, waits for them, and re-layouts  17.4 us (2%)
    psum x4, blocking collectives, residual_gram(): return lax.psum(gram(resid, resid), ('gx', 'gy'))  312 us
    psum x2, blocking collectives, block_solve(): curv = lax.psum(gram(search, image), ('gx', 'gy'))  150 us
    psum x1, blocking collectives, on_device(): lax.psum(jnp.dot(flat, onehot.T, precision=lax.Precision.HIGHEST), ('gx',...  75.3 us
    ppermute x14, starting transfers between devices, with_halo(): lax.ppermute(lax.slice_in_dim(block, block.shape[dim] - width, None, axis...  48.1 us
    ppermute x14, starting transfers between devices, with_halo(): lax.ppermute(lax.slice_in_dim(block, 0, width, axis=dim), axis, backward)  25.3 us
    ppermute x14, waiting for transfers between devices, with_halo(): lax.ppermute(lax.slice_in_dim(block, block.shape[dim] - width, None, axis...  22 us
    dot_general x8, matrix products, combine(): jnp.dot(coeff.T, fields.reshape(count, -1), precision=lax.Precision.HIGHEST)  16.6 us
  transfers between devices with their start and end apart: 28, of which 14 were waited for; matrix products, arithmetic and copies ran while one was open for 3% of the time, Pallas kernels for 0%

commit v1 on v0

v1 whole, which is shorter than its diff:
```python
import math

import jax
import jax.numpy as jnp
from jax import lax
from jax.experimental import pallas as pl
from jax.experimental.pallas import tpu as pltpu
from jax.sharding import PartitionSpec as P

SHIFT = 12.0
F = 16
LANES = 128
HALO = 4
HIGHEST = lax.Precision.HIGHEST
V0, V1, V2, E0, E1 = range(5)
HALO_ROWS = 48


def tile_at(y):
    return slice(y * F, (y + 1) * F)


def pack_kernel(bg_ref, cond_ref, pert_ref, own_ref, up_ref, down_ref):
    size_x, size_y = cond_ref.shape[0], cond_ref.shape[1]

    def plane(x, carry):
        for y in range(size_y):
            tile = bg_ref[pl.ds(x * size_y + y, F, stride=size_x * size_y), :]
            own_ref[x, tile_at(y), :] = tile
            if y >= size_y - HALO:
                up_ref[x, tile_at(y - size_y + HALO), :] = tile
            if y < HALO:
                down_ref[x, tile_at(y), :] = tile
        cond, pert = cond_ref[x], pert_ref[x]
        own_ref[x, 128:136, :] = cond
        own_ref[x, 136:144, :] = pert
        up_ref[x, 64:72, :] = jnp.concatenate([cond[4:8], pert[4:8]], axis=0)
        down_ref[x, 64:72, :] = jnp.concatenate([cond[0:4], pert[0:4]], axis=0)
        return carry

    lax.fori_loop(0, size_x, plane, 0)


def pack(background, conductivity, perturbation):
    shape = jax.ShapeDtypeStruct
    return pl.pallas_call(
        pack_kernel,
        out_shape=(
            shape((16, 144, LANES), jnp.float32),
            shape((16, 72, LANES), jnp.float32),
            shape((16, 72, LANES), jnp.float32),
        ),
        compiler_params=pltpu.CompilerParams(vmem_limit_bytes=16 * 2**20),
        name="pack_y",
    )(background, conductivity, perturbation)


def run_copies(pairs, sems):
    copies = [pltpu.make_async_copy(s, d, sems.at[i]) for i, (s, d) in enumerate(pairs)]
    for c in copies:
        c.start()
    return copies


def edge_layout():
    low, high, at = [], [], 0
    for k in range(HALO):
        low.append((4 - k, 12 + k, at))
        at += (8 + 2 * k) * F + 32
    at = 0
    for k in range(HALO):
        high.append((1 + k, 15 - k, at))
        at += (14 - 2 * k) * F + 32
    return low, high, at


EDGE_LOW, EDGE_HIGH, EDGE_ROWS = edge_layout()
PACK_COPIES = 46


def pack_x_kernel(own_ref, left_ref, right_ref, up_ref, down_ref, sems):
    pairs = []
    for out, table, base in ((up_ref, EDGE_LOW, 12), (down_ref, EDGE_HIGH, 0)):
        for k, (y0, y1, at) in enumerate(table):
            x = base + k
            pieces = []
            if y0 < 4:
                pieces.append((left_ref, y0 * F, 64))
            pieces.append((own_ref, 0, 128))
            if y1 > 12:
                pieces.append((right_ref, 0, (y1 - 12) * F))
            pieces += [(own_ref, 128, 144), (left_ref, 64, 72), (right_ref, 64, 72)]
            for ref, a, b in pieces:
                pairs.append((ref.at[x, pl.ds(a, b - a)], out.at[pl.ds(at, b - a)]))
                at += b - a
    for c in run_copies(pairs, sems):
        c.wait()


def pack_x(own, left, right):
    shape = jax.ShapeDtypeStruct((EDGE_ROWS, LANES), jnp.float32)
    anywhere = pl.BlockSpec(memory_space=pl.ANY)
    return pl.pallas_call(
        pack_x_kernel,
        out_shape=(shape, shape),
        in_specs=[anywhere] * 3,
        out_specs=(anywhere, anywhere),
        scratch_shapes=[pltpu.SemaphoreType.DMA((PACK_COPIES,))],
        compiler_params=pltpu.CompilerParams(vmem_limit_bytes=2 * 2**20),
        name="pack_x",
    )(own, left, right)


def lane_ids(rows):
    return lax.broadcasted_iota(jnp.int32, (rows, LANES), 1)


def faces(cells, fx, fy, fz, dd, sign, base):
    lane = lane_ids(16)
    edge = (lane == 0) | (lane == LANES - 1)
    half = 0.5 * sign

    def plane(x, carry):
        c = cells[x]
        fx[x] = half * (c + cells[jnp.minimum(x + 1, 23)])
        fy[x] = half * (c + pltpu.roll(c, 15, 0))
        fz[x] = jnp.where(lane == LANES - 1, 0.0, half * (c + pltpu.roll(c, LANES - 1, 1)))
        dd[x] = base + jnp.where(edge, half * c, 0.0)
        return carry

    lax.fori_loop(0, 24, plane, 0)


def stencil_plane(src, coeffs, x, y0, y1, mask_x, mask_y, emit):
    fx, fy, fz, dd = coeffs
    q = src[x, tile_at(y0), :]
    flux = fy[x, y0 - 1 : y0, :] * (q - src[x, tile_at(y0 - 1), :])
    for y in range(y0, y1):
        nxt = src[x, tile_at(y + 1), :]
        row = slice(y, y + 1)
        later = fy[x, row, :] * (nxt - q)
        fz_at = fz[x, row, :] * (pltpu.roll(q, LANES - 1, 1) - q)
        out = dd[x, row, :] * q + (flux - later)
        out = out + fx[x - 1, row, :] * (q - src[x - 1, tile_at(y), :])
        out = out - fx[x, row, :] * (src[x + 1, tile_at(y), :] - q)
        out = out + (pltpu.roll(fz_at, 1, 1) - fz_at)
        mask = mask_x
        if y < 4:
            mask = mask_y[0] if mask is None else mask * mask_y[0]
        elif y >= 12:
            mask = mask_y[1] if mask is None else mask * mask_y[1]
        if mask is not None:
            out = out * mask
        emit(y, out)
        flux, q = later, nxt


def put_split(s_ref, block, lo_base, lane_at, value):
    hi = value.astype(jnp.bfloat16)
    s_ref[block * F : (block + 1) * F, pl.ds(lane_at, LANES)] = hi
    if lo_base is not None:
        lo = (value - hi.astype(jnp.float32)).astype(jnp.bfloat16)
        at = lo_base + block * F
        s_ref[at : at + F, pl.ds(lane_at, LANES)] = lo


def row_of(x, y):
    if isinstance(x, int) and x == 3:
        return 160 + (y - 4)
    if isinstance(x, int) and x == 20:
        return 168 + (y - 4)
    if y == 3:
        return 128 + (x - 4)
    if y == 12:
        return 144 + (x - 4)
    return (x - 4) * 8 + (y - 4)


def lane_of(x, y):
    at = row_of(x, y) * LANES
    return at if isinstance(at, int) else pl.multiple_of(at, LANES)


def kept(x, y):
    if isinstance(x, int) and x in (3, 20):
        return 4 <= y < 12
    if isinstance(x, int):
        return False
    return 3 <= y <= 12


def sweep(src, dst, coeffs, reach, masks, s_ref, block, lo_base):
    mask_x, mask_y = masks

    def emit_at(x):
        def emit(y, out):
            if dst is not None:
                dst[x, tile_at(y), :] = out
            if s_ref is not None and kept(x, y):
                put_split(s_ref, block, lo_base, lane_of(x, y), out)

        return emit

    for step in range(1, reach + 1):
        y0, y1 = 4 - (reach - step), 12 + (reach - step)
        for x, mask in ((4 - step, mask_x[0]), (19 + step, mask_x[1])):
            stencil_plane(src, coeffs, x, y0, y1, mask, mask_y, emit_at(x))

    def plane(x, carry):
        stencil_plane(src, coeffs, x, 4 - reach, 12 + reach, None, mask_y, emit_at(x))
        return carry

    lax.fori_loop(4, 20, plane, 0)


def krylov_kernel(
    elec_ref, own_ref, left_ref, right_ref, low_ref, high_ref, s_ref, pay_ref,
    bext, v0, v1, v2, e0, e1, t_ref, cond, pert, cx, cy, cz, cd, px, py, pz, pd, gram, sems,
):
    pairs = [
        (own_ref.at[:, pl.ds(0, 128)], bext.at[pl.ds(4, 16), pl.ds(64, 128)]),
        (own_ref.at[:, pl.ds(128, 16)], bext.at[pl.ds(4, 16), pl.ds(256, 16)]),
        (left_ref.at[:, pl.ds(0, 64)], bext.at[pl.ds(4, 16), pl.ds(0, 64)]),
        (left_ref.at[:, pl.ds(64, 8)], bext.at[pl.ds(4, 16), pl.ds(272, 8)]),
        (right_ref.at[:, pl.ds(0, 64)], bext.at[pl.ds(4, 16), pl.ds(192, 64)]),
        (right_ref.at[:, pl.ds(64, 8)], bext.at[pl.ds(4, 16), pl.ds(280, 8)]),
    ]
    for ref, table, base in ((low_ref, EDGE_LOW, 0), (high_ref, EDGE_HIGH, 20)):
        for k, (y0, y1, at) in enumerate(table):
            count = (y1 - y0) * F
            pairs.append((ref.at[pl.ds(at, count)], bext.at[base + k, pl.ds(y0 * F, count)]))
            pairs.append((ref.at[pl.ds(at + count, 32)], bext.at[base + k, pl.ds(256, 32)]))
    copies = run_copies(pairs, sems)

    gx, gy = lax.axis_index("gx"), lax.axis_index("gy")
    last_x, last_y = lax.axis_size("gx") - 1, lax.axis_size("gy") - 1
    one, zero = jnp.float32(1), jnp.float32(0)
    mask_x = (jnp.where(gx > 0, one, zero), jnp.where(gx < last_x, one, zero))
    mask_y = (jnp.where(gy > 0, one, zero), jnp.where(gy < last_y, one, zero))
    masks = (mask_x, mask_y)
    total_y = 8 * (last_y + 1)

    sub = lax.broadcasted_iota(jnp.int32, (F, LANES), 0)
    lane = lane_ids(F)
    ids = jnp.zeros((F, LANES), jnp.int32)
    for e in range(F):
        ids = jnp.where(sub == e, elec_ref[e], ids)
    ids = ids - lane

    def unit_plane(x):
        at_x = gx * 16 + x - 4
        good_x = (at_x >= 0) & (at_x < 16 * (last_x + 1))
        for y in range(2, 14):
            at_y = gy * 8 + y - 4
            good = good_x & (at_y >= 0) & (at_y < total_y)
            here = jnp.where(good, (at_x * total_y + at_y) * LANES, -(2**20))
            value = jnp.where(ids == here, 1.0, 0.0)
            e0[x, tile_at(y), :] = value
            if kept(x, y):
                put_split(s_ref, E0, None, lane_of(x, y), value)

    for x in (2, 3, 20, 21):
        unit_plane(x)

    def unit_loop(x, carry):
        unit_plane(x)
        return carry

    lax.fori_loop(4, 20, unit_loop, 0)
    s_ref[80 + E0 * F : 80 + (E0 + 1) * F, :] = jnp.zeros((F, s_ref.shape[1]), jnp.bfloat16)
    for c in copies:
        c.wait()

    def coeff_plane(x, carry):
        own, left, right = bext[x, 256:272, :], bext[x, 272:280, :], bext[x, 280:288, :]
        cond[x] = jnp.concatenate([left[0:4], own[0:8], right[0:4]], axis=0)
        pert[x] = jnp.concatenate([left[4:8], own[8:16], right[4:8]], axis=0)
        return carry

    lax.fori_loop(0, 24, coeff_plane, 0)
    faces(cond, cx, cy, cz, cd, 1.0, 0.05 - SHIFT)
    faces(pert, px, py, pz, pd, -1.0, 0.0)
    ccoef, pcoef = (cx, cy, cz, cd), (px, py, pz, pd)

    sweep(bext, v0, pcoef, 3, masks, s_ref, V0, 80)
    sweep(v0, v1, ccoef, 2, masks, s_ref, V1, 80)
    sweep(v1, v2, ccoef, 1, masks, s_ref, V2, 80)
    sweep(v2, None, ccoef, 0, masks, t_ref, 0, 32)
    sweep(e0, e1, ccoef, 1, masks, s_ref, E1, 80)
    sweep(e1, None, ccoef, 0, masks, t_ref, 1, 32)

    gram[...] = jnp.zeros_like(gram)
    chunk = 1024

    def gram_step(i, carry):
        at = pl.ds(pl.multiple_of(i * chunk, chunk), chunk)
        left = s_ref[:, at]
        right = jnp.concatenate([left, t_ref[:, at]], axis=0)
        gram[...] += lax.dot_general(
            left, right, (((1,), (1,)), ((), ())), preferred_element_type=jnp.float32
        )
        return carry

    lax.fori_loop(0, 128 * LANES // chunk, gram_step, 0)
    both = gram[0:80, :] + gram[80:160, :]

    def block(row, col, lo):
        rows = both[row * F : (row + 1) * F]
        return rows[:, col : col + F] + rows[:, lo : lo + F]

    def pair(row, col):
        return block(row, col * F, 80 + col * F)

    v3, e2 = (160, 192), (176, 208)
    blocks = [
        pair(V0, V0), pair(V0, V1), pair(V1, V1), pair(V1, V2), pair(V2, V2), block(V2, *v3),
        pair(V0, E0), pair(V1, E0), pair(V2, E0), block(E0, *v3), block(E1, *v3),
        pair(E0, E0), pair(E0, E1), pair(E1, E1), block(E1, *e2), jnp.zeros((F, F), jnp.float32),
    ]
    pay_ref[0:16, :] = jnp.concatenate(blocks[:8], axis=1)
    pay_ref[16:32, :] = jnp.concatenate(blocks[8:], axis=1)


CELLS = 176 * LANES


def krylov(electrodes, own, left, right, low, high):
    anywhere = pl.BlockSpec(memory_space=pl.ANY)
    field = pltpu.VMEM((24, 256, LANES), jnp.float32)
    coeff = pltpu.VMEM((24, 16, LANES), jnp.float32)
    return pl.pallas_call(
        krylov_kernel,
        out_shape=(
            jax.ShapeDtypeStruct((160, CELLS), jnp.bfloat16),
            jax.ShapeDtypeStruct((32, LANES), jnp.float32),
        ),
        in_specs=[pl.BlockSpec(memory_space=pltpu.SMEM)] + [anywhere] * 5,
        scratch_shapes=[pltpu.VMEM((24, 288, LANES), jnp.float32)]
        + [field] * 5
        + [pltpu.VMEM((64, 128 * LANES), jnp.bfloat16)]
        + [coeff] * 10
        + [pltpu.VMEM((160, 224), jnp.float32), pltpu.SemaphoreType.DMA((22,))],
        compiler_params=pltpu.CompilerParams(vmem_limit_bytes=48 * 2**20),
        name="krylov",
    )(electrodes, own, left, right, low, high)


def matmul(a, b, dims=((1,), (0,))):
    return lax.dot_general(
        a, b, (dims, ((), ())), precision=HIGHEST, preferred_element_type=jnp.float32
    )


def galerkin(m0, m1, m2, m3):
    a12 = m2 + SHIFT * m1
    work = jnp.concatenate(
        [
            jnp.concatenate([m1 + SHIFT * m0, a12, m0], axis=1),
            jnp.concatenate([a12, m3 + SHIFT * m2, m1], axis=1),
        ],
        axis=0,
    )
    sub = lax.broadcasted_iota(jnp.int32, work.shape, 0)
    for k in range(2 * F):
        row = work[k : k + 1, :]
        row = row / row[:, k : k + 1]
        work = jnp.where(sub == k, row, work - work[:, k : k + 1] * row)
    return work[:, 2 * F :]


def final_kernel(
    pattern_ref, parts_ref, own_ref, left_ref, right_ref, low_ref, high_ref, s_hbm,
    out_ref, sens_ref, bg, adj, s_ref, sems, *, damping,
):
    pairs = [
        (own_ref.at[:, pl.ds(0, 128)], bg.at[pl.ds(1, 16), pl.ds(16, 128)]),
        (left_ref.at[:, pl.ds(48, 16)], bg.at[pl.ds(1, 16), pl.ds(0, 16)]),
        (right_ref.at[:, pl.ds(0, 16)], bg.at[pl.ds(1, 16), pl.ds(144, 16)]),
        (low_ref.at[pl.ds(EDGE_LOW[3][2] + 3 * F, 128)], bg.at[0, pl.ds(16, 128)]),
        (high_ref.at[pl.ds(EDGE_HIGH[0][2] + 3 * F, 128)], bg.at[17, pl.ds(16, 128)]),
        (s_hbm, s_ref),
    ]
    copies = run_copies(pairs, sems)

    total = jnp.sum(parts_ref[...], axis=0)

    def part(k):
        r, c = (k // 8) * F, (k % 8) * F
        return total[r : r + F, c : c + F]

    m = [part(k) for k in range(6)]
    p = [part(6), part(7), part(8), part(9).T, part(10).T]
    e = [part(k) for k in range(11, 15)]
    y = galerkin(*m[:4])
    y0, y1 = y[0:F], y[F:]
    probe = matmul(y0, p[0], ((0,), (0,))) + matmul(y1, p[1], ((0,), (0,)))
    lane = lax.broadcasted_iota(jnp.int32, (F, F), 1)
    sub = lax.broadcasted_iota(jnp.int32, (F, F), 0)
    first, second = jnp.zeros((F, F), jnp.int32), jnp.zeros((F, F), jnp.int32)
    for i in range(F):
        first = jnp.where(sub == i, pattern_ref[i, 0], first)
        second = jnp.where(sub == i, pattern_ref[i, 1], second)
    pairing = jnp.where(lane == first, 1.0, 0.0) - jnp.where(lane == second, 1.0, 0.0)
    measured = matmul(probe, pairing, ((1,), (1,)))
    weight = 8.0 * matmul(measured, pairing)
    z = jnp.concatenate([damping * y0, damping * y1, weight.T], axis=0)
    rows = []
    for k in range(4):
        rows.append(jnp.concatenate([m[k], m[k + 1], p[k]], axis=1))
        rows.append(jnp.concatenate([m[k + 1], m[k + 2], p[k + 1]], axis=1))
        rows.append(jnp.concatenate([p[k].T, p[k + 1].T, e[k]], axis=1))
    nz = matmul(jnp.concatenate(rows, axis=0), z)
    moments = [matmul(z, nz[48 * k : 48 * (k + 1)], ((0,), (0,))) for k in range(4)]
    q = galerkin(*moments)
    z0, z1 = matmul(z, q[0:F]), matmul(z, q[F:])
    mix = jnp.concatenate(
        [z0[0:F], z0[F : 2 * F] + z1[0:F], z1[F : 2 * F], z0[2 * F :], z1[2 * F :]], axis=0
    )
    mix = jnp.concatenate(
        [jnp.concatenate([y, jnp.zeros((48, F), jnp.float32)], axis=0), mix], axis=1
    ).T
    hi = mix.astype(jnp.bfloat16)
    lo = (mix - hi.astype(jnp.float32)).astype(jnp.bfloat16)
    both = jnp.concatenate([hi, lo], axis=0)
    both = jnp.concatenate([both, both], axis=1)
    for c in copies:
        c.wait()

    def combine(at, count):
        out = jnp.dot(both, s_ref[:, pl.ds(at, count)], preferred_element_type=jnp.float32)
        return out[0:32] + out[32:64]

    def plane(x, carry):
        out = combine(pl.multiple_of(x * 8 * LANES, 8 * LANES), 8 * LANES)
        for k in range(8):
            cols = slice(k * LANES, (k + 1) * LANES)
            out_ref[pl.ds(x * 8 + k, F, stride=128), :] = out[0:F, cols]
            adj[x + 1, tile_at(k + 1), :] = out[F:, cols]
        return carry

    lax.fori_loop(0, 16, plane, 0)
    for part_at in range(6):
        out = combine((128 + 8 * part_at) * LANES, 8 * LANES)
        for k in range(8):
            value = out[F:, k * LANES : (k + 1) * LANES]
            if part_at < 2:
                adj[1 + 8 * part_at + k, tile_at(0), :] = value
            elif part_at < 4:
                adj[1 + 8 * (part_at - 2) + k, tile_at(9), :] = value
            else:
                adj[17 * (part_at - 4), tile_at(k + 1), :] = value

    lane = lane_ids(F)

    def sens_plane(x, carry):
        b, a = bg[x, tile_at(1), :], adj[x, tile_at(1), :]
        before = (b - bg[x, tile_at(0), :]) * (a - adj[x, tile_at(0), :])
        for k in range(1, 9):
            bn, an = bg[x, tile_at(k + 1), :], adj[x, tile_at(k + 1), :]
            after = (bn - b) * (an - a)
            total = before + after
            for s in (x - 1, x + 1):
                total = total + (bg[s, tile_at(k), :] - b) * (adj[s, tile_at(k), :] - a)
            own = b * a
            up = (pltpu.roll(b, LANES - 1, 1) - b) * (pltpu.roll(a, LANES - 1, 1) - a)
            up = jnp.where(lane == LANES - 1, own, up)
            down = jnp.where(lane == 0, own, pltpu.roll(up, 1, 1))
            total = total + (up + down)
            sens_ref[x - 1, k - 1 : k, :] = -0.5 * jnp.sum(total, axis=0, keepdims=True)
            before, b, a = after, bn, an
        return carry

    lax.fori_loop(1, 17, sens_plane, 0)


def final(pattern, parts, own, left, right, low, high, s, damping):
    anywhere = pl.BlockSpec(memory_space=pl.ANY)
    vmem = pl.BlockSpec(memory_space=pltpu.VMEM)

    def kernel(*refs):
        final_kernel(*refs, damping=damping)

    return pl.pallas_call(
        kernel,
        out_shape=(
            jax.ShapeDtypeStruct((2048, LANES), jnp.float32),
            jax.ShapeDtypeStruct((16, 8, LANES), jnp.float32),
        ),
        in_specs=[pl.BlockSpec(memory_space=pltpu.SMEM), vmem] + [anywhere] * 6,
        scratch_shapes=[
            pltpu.VMEM((18, 160, LANES), jnp.float32),
            pltpu.VMEM((18, 160, LANES), jnp.float32),
            pltpu.VMEM((160, CELLS), jnp.bfloat16),
            pltpu.SemaphoreType.DMA((6,)),
        ],
        compiler_params=pltpu.CompilerParams(vmem_limit_bytes=40 * 2**20),
        name="final",
    )(pattern, parts, own, left, right, low, high, s)


def spread(block, axis, count, groups=None):
    copies = jnp.broadcast_to(block[None], (count,) + block.shape)
    return lax.all_to_all(copies, axis, 0, 0, axis_index_groups=groups)


def on_device(background, conductivity, perturbation, electrodes, pattern):
    size_x, size_y, size_z = conductivity.shape
    count_x, count_y = lax.axis_size("gx"), lax.axis_size("gy")
    up_y = [(i, i + 1) for i in range(count_y - 1)]
    up_x = [(i, i + 1) for i in range(count_x - 1)]
    down_y, down_x = [(j, i) for i, j in up_y], [(j, i) for i, j in up_x]
    own, up, down = pack(background.reshape(-1, size_z), conductivity, perturbation)
    left = lax.ppermute(up, "gy", up_y)
    right = lax.ppermute(down, "gy", down_y)
    up, down = pack_x(own, left, right)
    low = lax.ppermute(up, "gx", up_x)
    high = lax.ppermute(down, "gx", down_x)
    s, pay = krylov(electrodes, own, left, right, low, high)
    pay = pay + lax.ppermute(pay, "gy", [(i, i ^ 1) for i in range(count_y)])
    pay = jnp.sum(spread(pay, "gx", count_x), axis=0)
    chips = count_y // 2
    groups = [[2 * i + core for i in range(chips)] for core in range(2)]
    parts = spread(pay, "gy", chips, groups)
    cells = size_x * size_y * size_z * count_x * count_y
    tangent, sens = final(
        pattern, parts, own, left, right, low, high, s, 80.0 / math.sqrt(cells)
    )
    return tangent.reshape(background.shape), sens


def solution(mesh):
    in_specs = (P(None, "gx", "gy", None), P("gx", "gy", None), P("gx", "gy", None), P(), P())
    out_specs = (P(None, "gx", "gy", None), P("gx", "gy", None))
    return jax.shard_map(
        on_device, mesh=mesh, in_specs=in_specs, out_specs=out_specs, check_vma=False
    )
```

time: 757 us -> 125 us (0.17); the launches traced: 745 us -> 124 us
  blocking collectives: 537 us -> 17.7 us
  starting transfers between devices: 73.4 us -> 18.8 us
  other arithmetic: 53.4 us -> 0.02 us
  Pallas kernels: 0 us -> 51.6 us
  matrix products: 37.2 us -> 0 us
  local copies, waits for them, and re-layouts: 17.4 us -> 7.43 us
    psum x7 -> x0, blocking collectives: 537 us -> none  [the longest x4 312 us: residual_gram(): return lax.psum(gram(resid, resid), ('gx', 'gy'))]
    ppermute x28 -> x5, starting transfers between devices: 73.4 us -> 11.2 us  [the longest x1 3.85 us: on_device(): low = lax.ppermute(up, 'gx', up_x)]
    pallas_call x0 -> x4, Pallas kernels: none -> 51.6 us  [the longest x1 33 us: krylov(): pl.pallas_call(krylov_kernel, out_shape=(jax.ShapeDtypeStruct((160, CELLS...]
    dot_general x20 -> x0, matrix products: 34.8 us -> none  [the longest x8 16.6 us: combine(): jnp.dot(coeff.T, fields.reshape(count, -1), precision=lax.Precision.HIGHEST)]
    another operation x30 -> x0, other arithmetic: 28.7 us -> none  [the longest x18 14.9 us: chol_solve(): factor = jnp.linalg.cholesky(matrix)]
    all_to_all x0 -> x1, blocking collectives: none -> 17.7 us  [spread(): return lax.all_to_all(copies, axis, 0, 0, axis_index_groups=groups)]
    concatenate x13 -> x0, other arithmetic: 9.98 us -> none  [the longest x12 9.96 us: with_halo(): block = jnp.concatenate([low, block, high], axis=dim)]
    all_to_all x0 -> x1, starting transfers between devices: none -> 7.6 us  [spread(): return lax.all_to_all(copies, axis, 0, 0, axis_index_groups=groups)]
  transfers between devices with their start and end apart: 28 -> 6, of which waited for: 14 -> 6; matrix products, arithmetic and copies ran while one was open for 3% -> 0% of each run, Pallas kernels for 0% -> 0%
where the time goes in v1:
time: 125 us; the launch traced here: 124 us
  Pallas kernels  51.6 us (41%)
  waiting for transfers between devices  28.1 us (22%)
  starting transfers between devices  18.8 us (15%)
  blocking collectives  17.7 us (14%)
  local copies, waits for them, and re-layouts  7.43 us (6%)
    pallas_call x1, Pallas kernels, krylov(): pl.pallas_call(krylov_kernel, out_shape=(jax.ShapeDtypeStruct((160, CELLS...  33 us
    all_to_all x1, blocking collectives, spread(): return lax.all_to_all(copies, axis, 0, 0, axis_index_groups=groups)  17.7 us
    pallas_call x1, Pallas kernels, final(): pl.pallas_call(kernel, out_shape=(jax.ShapeDtypeStruct((2048, LANES), jnp...  16.4 us
    ppermute x1, waiting for transfers between devices, on_device(): low = lax.ppermute(up, 'gx', up_x)  8.09 us
    all_to_all x1, starting transfers between devices, spread(): return lax.all_to_all(copies, axis, 0, 0, axis_index_groups=groups)  7.6 us
    all_to_all x1, waiting for transfers between devices, spread(): return lax.all_to_all(copies, axis, 0, 0, axis_index_groups=groups)  7.24 us
    unnamed x13, local copies, waits for them, and re-layouts  6.69 us
    ppermute x1, waiting for transfers between devices, on_device(): left = lax.ppermute(up, 'gy', up_y)  5.62 us
  transfers between devices with their start and end apart: 6, of which 6 were waited for; matrix products, arithmetic and copies ran while one was open for 0% of the time, Pallas kernels for 0%

profile of v1, /device:TPU:2, one launch (start us, length us, event | category | flops | bytes accessed | tf_op | source)
XLA Modules:
  0.0 124.4 jit_solution(8691740780846190171)
XLA Ops:
  0.6 0.0 copy-start.5
  0.6 0.0 copy-start.1
  0.7 1.2 copy-done.1
  1.9 0.0 copy-start.2
  1.9 0.8 copy-done.2
  2.7 0.0 copy-start.3
  2.7 0.8 copy-done.3
  3.6 0.7 pack_y.1
  4.3 1.9 %collective-permute-start = (f32[16,72,128]{2,1,0:T(8,128)S(1)}, f32[16,72,128]{2,1,0:T(8,128)S(1)}, u32[]{:S(2)}, u32[]{:S(2)}) collective-permute-start(f32[16,72,128]{2,1,0:T(8,128)S(1)} %get-tuple-element.12), channel_id=1, source_target_pairs={{0,1},{1,2},{2,3},{3,4},{4,5},{5,6},{6,7},{7,8},{8,9},{9,10},{10,1... | collective-permute-start | bytes 1769480 | tf_op jit(solution)/shard_map/ppermute | solution.py:513
  6.2 3.6 %collective-permute-start.1 = (f32[16,72,128]{2,1,0:T(8,128)S(1)}, f32[16,72,128]{2,1,0:T(8,128)S(1)}, u32[]{:S(2)}, u32[]{:S(2)}) collective-permute-start(f32[16,72,128]{2,1,0:T(8,128)S(1)} %get-tuple-element.13), channel_id=1, source_target_pairs={{1,0},{2,1},{3,2},{4,3},{5,4},{6,5},{7,6},{8,7},{9,8},{10,9},{11,1... | collective-permute-start | bytes 1769480 | tf_op jit(solution)/shard_map/ppermute | solution.py:514
  9.8 5.6 %collective-permute-done.left_ref.refs_3_ = f32[16,72,128]{2,1,0:T(8,128)S(1)} collective-permute-done((f32[16,72,128]{2,1,0:T(8,128)S(1)}, f32[16,72,128]{2,1,0:T(8,128)S(1)}, u32[]{:S(2)}, u32[]{:S(2)}) %collective-permute-start) | collective-permute-done | bytes 589856 | tf_op jit(solution)/shard_map/ppermute | solution.py:513
  15.5 1.8 %collective-permute-done.1.right_ref.refs_4_ = f32[16,72,128]{2,1,0:T(8,128)S(1)} collective-permute-done((f32[16,72,128]{2,1,0:T(8,128)S(1)}, f32[16,72,128]{2,1,0:T(8,128)S(1)}, u32[]{:S(2)}, u32[]{:S(2)}) %collective-permute-start.1) | collective-permute-done | bytes 589856 | tf_op jit(solution)/shard_map/ppermute | solution.py:514
  17.2 1.6 %pack_x.1 = (f32[832,128]{1,0:T(8,128)S(1)}, f32[832,128]{1,0:T(8,128)S(1)}) custom-call(f32[16,144,128]{2,1,0:T(8,128)S(1)} %get-tuple-element.11.own_ref.refs_2_, f32[16,72,128]{2,1,0:T(8,128)S(1)} %collective-permute-done.left_ref.refs_3_, f32[16,72,128]{2,1,0:T(8,128)S(1)} %collective-permute-done.1.right_ref.refs_4_), custom_call_target="tpu_custom_call" | custom-call | tf_op jit(solution)/shard_map/pack_x/pallas_call | solution.py:103
  18.8 3.8 %collective-permute-start.2 = (f32[832,128]{1,0:T(8,128)S(1)}, f32[832,128]{1,0:T(8,128)S(1)}, u32[]{:S(2)}, u32[]{:S(2)}) collective-permute-start(f32[832,128]{1,0:T(8,128)S(1)} %get-tuple-element.14), channel_id=1, source_target_pairs={{0,32},{32,64},{64,96},{96,128},{128,160},{160,192},{192,224},{1,3... | collective-permute-start | bytes 1277960 | tf_op jit(solution)/shard_map/ppermute | solution.py:516
  22.6 1.3 %collective-permute-start.3 = (f32[832,128]{1,0:T(8,128)S(1)}, f32[832,128]{1,0:T(8,128)S(1)}, u32[]{:S(2)}, u32[]{:S(2)}) collective-permute-start(f32[832,128]{1,0:T(8,128)S(1)} %get-tuple-element.15), channel_id=1, source_target_pairs={{32,0},{64,32},{96,64},{128,96},{160,128},{192,160},{224,192},{33,... | collective-permute-start | bytes 1277960 | tf_op jit(solution)/shard_map/ppermute | solution.py:517
  23.9 8.1 %collective-permute-done.2.low_ref.refs_5_ = f32[832,128]{1,0:T(8,128)S(1)} collective-permute-done((f32[832,128]{1,0:T(8,128)S(1)}, f32[832,128]{1,0:T(8,128)S(1)}, u32[]{:S(2)}, u32[]{:S(2)}) %collective-permute-start.2) | collective-permute-done | bytes 426016 | tf_op jit(solution)/shard_map/ppermute | solution.py:516
  32.0 4.6 %collective-permute-done.3.high_ref.refs_6_ = f32[832,128]{1,0:T(8,128)S(1)} collective-permute-done((f32[832,128]{1,0:T(8,128)S(1)}, f32[832,128]{1,0:T(8,128)S(1)}, u32[]{:S(2)}, u32[]{:S(2)}) %collective-permute-start.3) | collective-permute-done | bytes 426016 | tf_op jit(solution)/shard_map/ppermute | solution.py:517
  36.6 0.0 copy-start.4
  36.6 0.7 copy-done.4
  37.2 33.0 %krylov.1 = (bf16[160,22528]{1,0:T(8,128)(2,1)}, f32[32,128]{1,0:T(8,128)S(1)}) custom-call(s32[16]{0:T(128)S(1)} %copy-done.4, f32[16,144,128]{2,1,0:T(8,128)S(1)} %get-tuple-element.11.own_ref.refs_2_, f32[16,72,128]{2,1,0:T(8,128)S(1)} %collective-permute-done.left_ref.refs_3_, f32[16,72,128]{2,1,0:T(8,128)S(1)} %collective-permute-done.1.right_ref.refs_4_, ...), custom_call_target="tpu_custom_call" | custom-call | tf_op jit(solution)/shard_map/krylov/pallas_call | solution.py:331
  70.2 0.5 collective-permute-start.4
  70.8 0.8 collective-permute-done.4
  71.6 17.7 %all_to_all.10 = f32[8,32,128]{2,1,0:T(8,128)S(1)} all-to-all(f32[8,32,128]{2,1,0:T(8,128)S(1)} %broadcast_in_dim.4), channel_id=1, replica_groups=mesh['gx'=8,'gy'=32] {'gx'}, dimensions={0} | all-to-all | bytes 262144 | tf_op jit(solution)/shard_map/all_to_all | solution.py:503
  89.3 0.7 broadcast_in_dim.5
  90.1 7.6 %all-to-all-start.1 = ((f32[16,32,128]{2,1,0:T(8,128)}), f32[16,32,128]{2,1,0:T(8,128)S(1)}, u32[]{:S(2)}, u32[]{:S(2)}) async-start(f32[16,32,128]{2,1,0:T(8,128)} %broadcast_in_dim.5), calls=%async_computation.1 | async-start | bytes 524288 | tf_op jit(solution)/shard_map/all_to_all | solution.py:503
  97.7 0.0 copy-done.5
  97.7 0.1 copy.8.refs_0_
  97.7 7.2 %all-to-all-done.1.refs_1_ = f32[16,32,128]{2,1,0:T(8,128)S(1)} async-done(((f32[16,32,128]{2,1,0:T(8,128)}), f32[16,32,128]{2,1,0:T(8,128)S(1)}, u32[]{:S(2)}, u32[]{:S(2)}) %all-to-all-start.1) | async-done | bytes 262176 | tf_op jit(solution)/shard_map/all_to_all | solution.py:503
  105.0 0.0 copy-start
  105.0 3.0 %copy-done = bf16[160,22528]{1,0:T(8,128)(2,1)S(1)} copy-done((bf16[160,22528]{1,0:T(8,128)(2,1)S(1)}, bf16[160,22528]{1,0:T(8,128)(2,1)}, u32[]{:S(2)}) %copy-start) | copy-done | bytes 7208984
  108.0 16.4 %final.1 = (f32[2048,128]{1,0:T(8,128)}, f32[16,8,128]{2,1,0:T(8,128)}) custom-call(s32[16,2]{1,0:T(8,128)S(1)} %copy.8.refs_0_, f32[16,32,128]{2,1,0:T(8,128)S(1)} %all-to-all-done.1.refs_1_, f32[16,144,128]{2,1,0:T(8,128)S(1)} %get-tuple-element.11.own_ref.refs_2_, f32[16,72,128]{2,1,0:T(8,128)S(1)} %collective-permute-done.left_ref.refs_3_, ...), custom_call_target="tpu_custom_call" | custom-call | tf_op jit(solution)/shard_map/final/pallas_call | solution.py:483
  (3 shorter events, 0.0 us)
Async XLA Ops:
  0.6 97.0 %copy-start.5 = (s32[16,2]{0,1:T(2,128)S(1)}, s32[16,2]{0,1:T(2,128)}, u32[]{:S(2)}) copy-start(s32[16,2]{0,1:T(2,128)} %param.9) | copy-start | bytes 388
  0.6 1.2 copy-start.1
  1.9 0.8 copy-start.2
  2.7 0.8 copy-start.3
  4.3 11.2 %collective-permute-start = (f32[16,72,128]{2,1,0:T(8,128)S(1)}, f32[16,72,128]{2,1,0:T(8,128)S(1)}, u32[]{:S(2)}, u32[]{:S(2)}) collective-permute-start(f32[16,72,128]{2,1,0:T(8,128)S(1)} %get-tuple-element.12), channel_id=1, source_target_pairs={{0,1},{1,2},{2,3},{3,4},{4,5},{5,6},{6,7},{7,8},{8,9},{9,10},{10,1... | collective-permute-start | bytes 1769480 | tf_op jit(solution)/shard_map/ppermute | solution.py:513
  6.2 11.0 %collective-permute-start.1 = (f32[16,72,128]{2,1,0:T(8,128)S(1)}, f32[16,72,128]{2,1,0:T(8,128)S(1)}, u32[]{:S(2)}, u32[]{:S(2)}) collective-permute-start(f32[16,72,128]{2,1,0:T(8,128)S(1)} %get-tuple-element.13), channel_id=1, source_target_pairs={{1,0},{2,1},{3,2},{4,3},{5,4},{6,5},{7,6},{8,7},{9,8},{10,9},{11,1... | collective-permute-start | bytes 1769480 | tf_op jit(solution)/shard_map/ppermute | solution.py:514
  18.8 13.2 %collective-permute-start.2 = (f32[832,128]{1,0:T(8,128)S(1)}, f32[832,128]{1,0:T(8,128)S(1)}, u32[]{:S(2)}, u32[]{:S(2)}) collective-permute-start(f32[832,128]{1,0:T(8,128)S(1)} %get-tuple-element.14), channel_id=1, source_target_pairs={{0,32},{32,64},{64,96},{96,128},{128,160},{160,192},{192,224},{1,3... | collective-permute-start | bytes 1277960 | tf_op jit(solution)/shard_map/ppermute | solution.py:516
  22.6 13.9 %collective-permute-start.3 = (f32[832,128]{1,0:T(8,128)S(1)}, f32[832,128]{1,0:T(8,128)S(1)}, u32[]{:S(2)}, u32[]{:S(2)}) collective-permute-start(f32[832,128]{1,0:T(8,128)S(1)} %get-tuple-element.15), channel_id=1, source_target_pairs={{32,0},{64,32},{96,64},{128,96},{160,128},{192,160},{224,192},{33,... | collective-permute-start | bytes 1277960 | tf_op jit(solution)/shard_map/ppermute | solution.py:517
  36.6 0.7 copy-start.4
  70.2 1.4 %collective-permute-start.4 = (f32[32,128]{1,0:T(8,128)S(1)}, f32[32,128]{1,0:T(8,128)S(1)}, u32[]{:S(2)}, u32[]{:S(2)}) collective-permute-start(f32[32,128]{1,0:T(8,128)S(1)} %get-tuple-element.16), channel_id=1, source_target_pairs={{0,1},{1,0},{2,3},{3,2},{4,5},{5,4},{6,7},{7,6},{8,9},{9,8},{10,11... | collective-permute-start | bytes 49160 | tf_op jit(solution)/shard_map/ppermute | solution.py:519
  90.1 14.9 %all-to-all-start.1 = ((f32[16,32,128]{2,1,0:T(8,128)}), f32[16,32,128]{2,1,0:T(8,128)S(1)}, u32[]{:S(2)}, u32[]{:S(2)}) async-start(f32[16,32,128]{2,1,0:T(8,128)} %broadcast_in_dim.5), calls=%async_computation.1 | async-start | bytes 524288 | tf_op jit(solution)/shard_map/all_to_all | solution.py:503
  105.0 3.0 %copy-start = (bf16[160,22528]{1,0:T(8,128)(2,1)S(1)}, bf16[160,22528]{1,0:T(8,128)(2,1)}, u32[]{:S(2)}) copy-start(bf16[160,22528]{1,0:T(8,128)(2,1)} %get-tuple-element.17.refs_7_) | copy-start | bytes 21626884

commit v2 on v1

v2 whole, which is shorter than its diff:
```python
import math

import jax
import jax.numpy as jnp
from jax import lax
from jax.experimental import pallas as pl
from jax.experimental.pallas import tpu as pltpu
from jax.sharding import PartitionSpec as P

SHIFT = 12.0
F = 16
LANES = 128
HALO = 4
HIGHEST = lax.Precision.HIGHEST
V0, V1, V2, E0, E1, V3, E2 = 0, 32, 64, 96, 112, 144, 176
KEPT, ALL_ROWS = 144, 208
WIDE = 10 * LANES
MB = 2**20


def tile_at(y):
    return slice(y * F, (y + 1) * F)


def run_copies(pairs, sems, first=0):
    copies = [
        pltpu.make_async_copy(s, d, sems.at[first + i]) for i, (s, d) in enumerate(pairs)
    ]
    for c in copies:
        c.start()
    return copies


def wait_all(copies):
    for c in copies:
        c.wait()


def odd(axis):
    return lax.rem(lax.axis_index(axis), 2) == 1


def pack_kernel(bg_hbm, cond_hbm, pert_hbm, own_ref, core_ref, chip_ref, bg, cond_v, pert_v, sems):
    size_x, size_y = cond_v.shape[0], cond_v.shape[1]
    pairs = [(cond_hbm, cond_v), (pert_hbm, pert_v), (bg_hbm, bg)]
    wait_all(run_copies(pairs, sems))

    def fill(top_ref, bottom_ref):
        def plane(x, carry):
            for y in range(size_y):
                tile = bg[pl.ds(x * size_y + y, F, stride=size_x * size_y), :]
                own_ref[x, tile_at(y), :] = tile
                if y >= size_y - HALO:
                    top_ref[x, tile_at(y - size_y + HALO), :] = tile
                if y < HALO:
                    bottom_ref[x, tile_at(y), :] = tile
            cond, pert = cond_v[x], pert_v[x]
            own_ref[x, 128:136, :] = cond
            own_ref[x, 136:144, :] = pert
            top_ref[x, 64:72, :] = jnp.concatenate([cond[4:8], pert[4:8]], axis=0)
            bottom_ref[x, 64:72, :] = jnp.concatenate([cond[0:4], pert[0:4]], axis=0)
            return carry

        lax.fori_loop(0, size_x, plane, 0, unroll=4)

    @pl.when(odd("gy"))
    def _():
        fill(chip_ref, core_ref)

    @pl.when(jnp.logical_not(odd("gy")))
    def _():
        fill(core_ref, chip_ref)


def pack(background, conductivity, perturbation):
    shape = jax.ShapeDtypeStruct
    anywhere = pl.BlockSpec(memory_space=pl.ANY)
    return pl.pallas_call(
        pack_kernel,
        out_shape=(
            shape((16, 144, LANES), jnp.float32),
            shape((16, 72, LANES), jnp.float32),
            shape((16, 72, LANES), jnp.float32),
        ),
        in_specs=[anywhere] * 3,
        scratch_shapes=[
            pltpu.VMEM((2048, LANES), jnp.float32),
            pltpu.VMEM((16, 8, LANES), jnp.float32),
            pltpu.VMEM((16, 8, LANES), jnp.float32),
            pltpu.SemaphoreType.DMA((3,)),
        ],
        compiler_params=pltpu.CompilerParams(vmem_limit_bytes=16 * MB),
        name="pack_y",
    )(background, conductivity, perturbation)


def edge_layout():
    table, at = [], 0
    for dx in range(1, HALO + 1):
        table.append((dx, 16 - dx, at))
        at += (16 - 2 * dx) * F + 32
    return table, at


EDGE, EDGE_ROWS = edge_layout()


def pack_x_kernel(own_ref, core_ref, chip_ref, a_ref, b_ref, sems):
    odd_x = odd("gx")

    def send(left_ref, right_ref):
        pairs = []
        for out, up in ((a_ref, jnp.logical_not(odd_x)), (b_ref, odd_x)):
            for y0, y1, at in EDGE:
                x = jnp.where(up, 16 - y0, y0 - 1)
                pieces = []
                if y0 < 4:
                    pieces.append((left_ref, y0 * F, 64))
                pieces.append((own_ref, 0, 128))
                if y1 > 12:
                    pieces.append((right_ref, 0, (y1 - 12) * F))
                pieces += [(own_ref, 128, 144), (left_ref, 64, 72), (right_ref, 64, 72)]
                for ref, a, b in pieces:
                    pairs.append((ref.at[x, pl.ds(a, b - a)], out.at[pl.ds(at, b - a)]))
                    at += b - a
        wait_all(run_copies(pairs, sems))

    @pl.when(odd("gy"))
    def _():
        send(core_ref, chip_ref)

    @pl.when(jnp.logical_not(odd("gy")))
    def _():
        send(chip_ref, core_ref)


def pack_x(own, core, chip):
    shape = jax.ShapeDtypeStruct((EDGE_ROWS, LANES), jnp.float32)
    anywhere = pl.BlockSpec(memory_space=pl.ANY)
    return pl.pallas_call(
        pack_x_kernel,
        out_shape=(shape, shape),
        in_specs=[anywhere] * 3,
        out_specs=(anywhere, anywhere),
        scratch_shapes=[pltpu.SemaphoreType.DMA((44,))],
        compiler_params=pltpu.CompilerParams(vmem_limit_bytes=2 * MB),
        name="pack_x",
    )(own, core, chip)


def lane_ids(rows):
    return lax.broadcasted_iota(jnp.int32, (rows, LANES), 1)


def own_copies(own_ref, core_ref, chip_ref, bext, ranges):
    odd_y = odd("gy")
    core_at = pl.multiple_of(jnp.where(odd_y, 0, 192), 8)
    chip_at = pl.multiple_of(jnp.where(odd_y, 192, 0), 8)
    core_c = pl.multiple_of(jnp.where(odd_y, 272, 280), 8)
    chip_c = pl.multiple_of(jnp.where(odd_y, 280, 272), 8)
    pairs = []
    for first, count, place in ranges:
        src, dst = pl.ds(first, count), pl.ds(place, count)
        pairs += [
            (own_ref.at[src, pl.ds(128, 16)], bext.at[dst, pl.ds(256, 16)]),
            (core_ref.at[src, pl.ds(64, 8)], bext.at[dst, pl.ds(core_c, 8)]),
            (chip_ref.at[src, pl.ds(64, 8)], bext.at[dst, pl.ds(chip_c, 8)]),
            (own_ref.at[src, pl.ds(0, 128)], bext.at[dst, pl.ds(64, 128)]),
            (core_ref.at[src, pl.ds(0, 64)], bext.at[dst, pl.ds(core_at, 64)]),
            (chip_ref.at[src, pl.ds(0, 64)], bext.at[dst, pl.ds(chip_at, 64)]),
        ]
    return pairs


def faces(bext, planes, ccoef, pcoef):
    lane = lane_ids(16)
    last = lane == LANES - 1
    edge = (lane == 0) | last

    def cells(x):
        own, left, right = bext[x, 256:272, :], bext[x, 272:280, :], bext[x, 280:288, :]
        return (
            jnp.concatenate([left[0:4], own[0:8], right[0:4]], axis=0),
            jnp.concatenate([left[4:8], own[8:16], right[4:8]], axis=0),
        )

    def plane(x):
        now, then = cells(x), cells(x + 1)
        for coef, c, n, half, base in (
            (ccoef, now[0], then[0], 0.5, 0.05 - SHIFT),
            (pcoef, now[1], then[1], -0.5, 0.0),
        ):
            fx, fy, fu, fd, dd = coef
            fx[x] = half * (c + n)
            fy[x] = half * (c + pltpu.roll(c, 15, 0))
            up = jnp.where(last, 0.0, half * (c + pltpu.roll(c, LANES - 1, 1)))
            fu[x] = up
            fd[x] = pltpu.roll(up, 1, 1)
            dd[x] = base + jnp.where(edge, half * c, 0.0)

    for x in planes:
        plane(x)


def stencil_plane(src, coeffs, x, y0, y1, mask_x, mask_y, emit):
    fx, fy, fu, fd, dd = coeffs
    q = src[x, tile_at(y0), :]
    flux = fy[x, y0 - 1 : y0, :] * (q - src[x, tile_at(y0 - 1), :])
    for y in range(y0, y1):
        nxt = src[x, tile_at(y + 1), :]
        row = slice(y, y + 1)
        later = fy[x, row, :] * (nxt - q)
        out = dd[x, row, :] * q + (flux - later)
        out = out + fx[x - 1, row, :] * (q - src[x - 1, tile_at(y), :])
        out = out - fx[x, row, :] * (src[x + 1, tile_at(y), :] - q)
        out = out + fd[x, row, :] * (q - pltpu.roll(q, 1, 1))
        out = out - fu[x, row, :] * (pltpu.roll(q, LANES - 1, 1) - q)
        mask = mask_x
        if y < 4:
            mask = mask_y[0] if mask is None else mask * mask_y[0]
        elif y >= 12:
            mask = mask_y[1] if mask is None else mask * mask_y[1]
        if mask is not None:
            out = out * mask
        emit(y, out)
        flux, q = later, nxt


def put_split(s_ref, i, row, y, value, exact=False):
    lanes = slice((y - 3) * LANES, (y - 2) * LANES)
    hi = value.astype(jnp.bfloat16)
    s_ref[i, row : row + F, lanes] = hi
    if not exact:
        lo = (value - hi.astype(jnp.float32)).astype(jnp.bfloat16)
        s_ref[i, row + F : row + 2 * F, lanes] = lo


def electrode_ids(elec_ref):
    sub = lax.broadcasted_iota(jnp.int32, (F, LANES), 0)
    ids = jnp.zeros((F, LANES), jnp.int32)
    for e in range(F):
        ids = jnp.where(sub == e, elec_ref[e], ids)
    return ids - lane_ids(F)


def grid_masks():
    one, zero = jnp.float32(1), jnp.float32(0)
    masks = []
    for axis in ("gx", "gy"):
        i = lax.axis_index(axis)
        low, high = i > 0, i < lax.axis_size(axis) - 1
        masks.append((jnp.where(low, one, zero), jnp.where(high, one, zero)))
    return masks


def unit_plane(ids, at_x, e0, i, s_ref, s_at, y_kept):
    size_x, size_y = 16 * lax.axis_size("gx"), 8 * lax.axis_size("gy")
    good_x = (at_x >= 0) & (at_x < size_x)
    for y in range(2, 14):
        at_y = lax.axis_index("gy") * 8 + y - 4
        good = good_x & (at_y >= 0) & (at_y < size_y)
        here = jnp.where(good, (at_x * size_y + at_y) * LANES, -(2**20))
        value = jnp.where(ids == here, 1.0, 0.0)
        e0[i, tile_at(y), :] = value
        if y_kept[0] <= y < y_kept[1]:
            put_split(s_ref, s_at, E0, y, value, exact=True)


def gram_of(s_ref, i):
    return lax.dot_general(
        s_ref[i, 0:KEPT, LANES : 9 * LANES],
        s_ref[i, :, LANES : 9 * LANES],
        (((1,), (1,)), ((), ())),
        preferred_element_type=jnp.float32,
    )


def inner_kernel(
    elec_ref, own_ref, core_ref, chip_ref, s_hbm, band_hbm, gram_ref,
    bext, v0, v1, v2, e0, e1, s_ref, cx, cy, cu, cd, cr, px, py, pu, pd, pr, sems, out_sems,
):
    copies = run_copies(own_copies(own_ref, core_ref, chip_ref, bext, [(0, 16, 0)]), sems)
    gx = lax.axis_index("gx")
    _, mask_y = grid_masks()
    ids = electrode_ids(elec_ref)

    def units(x, carry):
        unit_plane(ids, gx * 16 + x, e0, x, s_ref, x, (3, 13))
        return carry

    lax.fori_loop(2, 14, units, 0)
    wait_all(copies[:3])
    ccoef, pcoef = (cx, cy, cu, cd, cr), (px, py, pu, pd, pr)
    faces(bext, range(15), ccoef, pcoef)
    wait_all(copies[3:])

    def sweep(src, dst, coeffs, first, reach, row, keep):
        def plane(x, carry):
            def emit(y, out):
                if dst is not None:
                    dst[x, tile_at(y), :] = out
                if keep[0] <= y < keep[1]:
                    put_split(s_ref, x, row, y, out)

            stencil_plane(src, coeffs, x, 4 - reach, 12 + reach, None, mask_y, emit)
            return carry

        lax.fori_loop(first, 16 - first, plane, 0, unroll=2)

    def save(first, row, rows, at):
        count = 16 - 2 * first
        pair = (
            s_ref.at[pl.ds(first, count), pl.ds(row, rows)],
            s_hbm.at[pl.ds(first + 1, count), pl.ds(row, rows)],
        )
        return run_copies([pair], out_sems, at)

    def save_band(src, first, at):
        pairs = [
            (src.at[pl.ds(x, 2)], band_hbm.at[pl.ds(2 * at + 2 * k, 2)])
            for k, x in enumerate((first, 14 - first))
        ]
        return run_copies(pairs, out_sems, 4 + at)

    sweep(bext, v0, pcoef, 1, 3, V0, (3, 13))
    outs = save(1, V0, 32, 0) + save_band(v0, 1, 0)
    sweep(v0, v1, ccoef, 2, 2, V1, (3, 13))
    outs += save(2, V1, 32, 1) + save_band(v1, 2, 2)
    sweep(v1, v2, ccoef, 3, 1, V2, (3, 13))
    outs += save(3, V2, 32, 2) + save_band(v2, 3, 4)
    sweep(e0, e1, ccoef, 3, 1, E1, (3, 13))
    outs += save(4, E0, 48, 3)
    sweep(v2, None, ccoef, 4, 0, V3, (4, 12))
    sweep(e1, None, ccoef, 4, 0, E2, (4, 12))

    gram_ref[...] = gram_of(s_ref, 4)

    def gram_step(x, carry):
        gram_ref[...] += gram_of(s_ref, x)
        return carry

    lax.fori_loop(5, 12, gram_step, 0)
    wait_all(outs)


def inner(electrodes, own, core, chip):
    anywhere = pl.BlockSpec(memory_space=pl.ANY)
    vmem = pl.BlockSpec(memory_space=pltpu.VMEM)
    field = pltpu.VMEM((16, 256, LANES), jnp.float32)
    coeff = pltpu.VMEM((16, 16, LANES), jnp.float32)
    return pl.pallas_call(
        inner_kernel,
        out_shape=(
            jax.ShapeDtypeStruct((18, KEPT, WIDE), jnp.bfloat16),
            jax.ShapeDtypeStruct((12, 256, LANES), jnp.float32),
            jax.ShapeDtypeStruct((KEPT, ALL_ROWS), jnp.float32),
        ),
        in_specs=[pl.BlockSpec(memory_space=pltpu.SMEM)] + [anywhere] * 3,
        out_specs=(anywhere, anywhere, vmem),
        scratch_shapes=[pltpu.VMEM((16, 288, LANES), jnp.float32)]
        + [field] * 5
        + [pltpu.VMEM((16, ALL_ROWS, WIDE), jnp.bfloat16)]
        + [coeff] * 10
        + [pltpu.SemaphoreType.DMA((6,)), pltpu.SemaphoreType.DMA((10,))],
        compiler_params=pltpu.CompilerParams(vmem_limit_bytes=32 * MB),
        cost_estimate=pl.CostEstimate(
            flops=4 * 10**9, bytes_accessed=16 * 10**6, transcendentals=0
        ),
        name="inner",
    )(electrodes, own, core, chip)


def edge_kernel(
    elec_ref, own_ref, core_ref, chip_ref, a_ref, b_ref, band_ref, first_gram, s_in,
    s_hbm, pay_ref,
    bext, v0, v1, v2, e0, e1, s_ref, gram, cx, cy, cu, cd, cr, px, py, pu, pd, pr, sems, out_sems,
):
    odd_x = odd("gx")
    pairs = own_copies(own_ref, core_ref, chip_ref, bext, [(0, 6, 4), (10, 6, 10)])
    coef_pairs, field_pairs = pairs[0:3] + pairs[6:9], pairs[3:6] + pairs[9:12]
    for ref, high in ((a_ref, jnp.logical_not(odd_x)), (b_ref, odd_x)):
        for y0, y1, at in EDGE:
            count = (y1 - y0) * F
            to = jnp.where(high, 15 + y0, 4 - y0)
            coef_pairs.append((ref.at[pl.ds(at + count, 32)], bext.at[to, pl.ds(256, 32)]))
            field_pairs.append((ref.at[pl.ds(at, count)], bext.at[to, pl.ds(y0 * F, count)]))
    band_pairs = [
        (band_ref.at[pl.ds(2 * k, 2)], dst.at[pl.ds(to, 2)])
        for k, (dst, to) in enumerate(((v0, 5), (v0, 13), (v1, 6), (v1, 12), (v2, 7), (v2, 11)))
    ]
    s_pairs = []
    for row, count in ((V0, 3), (V1, 2), (V2, 1)):
        rows = pl.ds(row, 32)
        for src, to in ((5 - count, 5 - count), (13, 5)):
            s_pairs.append(
                (s_in.at[pl.ds(src, count), rows], s_ref.at[pl.ds(to, count), rows])
            )
    coef_copies = run_copies(coef_pairs, sems)
    at = len(coef_pairs)
    field_copies = run_copies(field_pairs, sems, at)
    at += len(field_pairs)
    band_copies = run_copies(band_pairs, sems, at)
    at += len(band_pairs)
    s_copies = run_copies(s_pairs, sems, at)

    gx = lax.axis_index("gx")
    mask_x, mask_y = grid_masks()
    ids = electrode_ids(elec_ref)

    def x_of(l):
        return l - 4 if l < 10 else l

    def keep_of(l):
        x = x_of(l)
        i = x + 1 if l < 10 else x - 7
        if x in (-1, 16):
            return i, (4, 12)
        if -1 < x < 4 or 11 < x < 16:
            return i, (3, 13)
        return 0, (99, 99)

    for l in list(range(2, 10)) + list(range(10, 18)):
        i, keep = keep_of(l)
        unit_plane(ids, gx * 16 + x_of(l), e0, l, s_ref, i, keep)
    wait_all(coef_copies)
    ccoef, pcoef = (cx, cy, cu, cd, cr), (px, py, pu, pd, pr)
    faces(bext, list(range(9)) + list(range(10, 19)), ccoef, pcoef)
    wait_all(field_copies)

    def sweep(src, dst, coeffs, reach, planes, row, rows_kept=None):
        for l in planes:
            x = x_of(l)
            out_by = max(0, -x, x - 15)
            mask = mask_x[0] if x < 0 else mask_x[1] if x > 15 else None
            i, keep = keep_of(l)
            keep = rows_kept or keep

            def emit(y, out, l=l, i=i, keep=keep):
                if dst is not None:
                    dst[l, tile_at(y), :] = out
                if keep[0] <= y < keep[1]:
                    put_split(s_ref, i, row, y, out)

            near = reach - out_by
            stencil_plane(src, coeffs, l, 4 - near, 12 + near, mask, mask_y, emit)

    def sides(low, count):
        return [x + 4 for x in range(low, low + count)] + [15 - x for x in range(low, low + count)]

    def save(row, rows, count, at):
        pairs = [
            (s_ref.at[pl.ds(i, count), pl.ds(row, rows)], s_hbm.at[pl.ds(o, count), pl.ds(row, rows)])
            for i, o in ((0, 0), (10 - count, 18 - count))
        ]
        return run_copies(pairs, out_sems, at)

    sweep(bext, v0, pcoef, 3, sides(-3, 4), V0)
    outs = save(V0, 32, 2, 0)
    wait_all(band_copies)
    sweep(v0, v1, ccoef, 2, sides(-2, 4), V1)
    outs += save(V1, 32, 3, 2)
    sweep(v1, v2, ccoef, 1, sides(-1, 4), V2)
    outs += save(V2, 32, 4, 4)
    sweep(e0, e1, ccoef, 1, sides(-1, 6), E1)
    outs += save(E0, 48, 5, 6)
    sweep(v2, None, ccoef, 0, sides(0, 4), V3, (4, 12))
    sweep(e1, None, ccoef, 0, sides(0, 4), E2, (4, 12))
    wait_all(s_copies)

    gram[...] = first_gram[...]

    def gram_step(i, carry):
        gram[...] += gram_of(s_ref, i)
        return carry

    lax.fori_loop(1, 9, gram_step, 0)

    def rows_of(row):
        if row == E0:
            return gram[row : row + F, :]
        return gram[row : row + F, :] + gram[row + F : row + 2 * F, :]

    summed = {row: rows_of(row) for row in (V0, V1, V2, E0, E1)}

    def block(row, col):
        rows = summed[row]
        if col == E0:
            return rows[:, col : col + F]
        return rows[:, col : col + F] + rows[:, col + F : col + 2 * F]

    order = [
        (V0, V0), (V0, V1), (V1, V1), (V1, V2), (V2, V2), (V2, V3), (V0, E0), (V1, E0),
        (V2, E0), (E0, V3), (E1, V3), (E0, E0), (E0, E1), (E1, E1), (E1, E2),
    ]
    blocks = [block(r, c) for r, c in order] + [jnp.zeros((F, F), jnp.float32)]
    pay_ref[0:16, :] = jnp.concatenate(blocks[:8], axis=1)
    pay_ref[16:32, :] = jnp.concatenate(blocks[8:], axis=1)
    wait_all(outs)


def edge(electrodes, own, core, chip, a, b, band, gram, s):
    anywhere = pl.BlockSpec(memory_space=pl.ANY)
    vmem = pl.BlockSpec(memory_space=pltpu.VMEM)
    field = pltpu.VMEM((20, 256, LANES), jnp.float32)
    coeff = pltpu.VMEM((20, 16, LANES), jnp.float32)
    return pl.pallas_call(
        edge_kernel,
        out_shape=(
            jax.ShapeDtypeStruct((18, KEPT, WIDE), jnp.bfloat16),
            jax.ShapeDtypeStruct((32, LANES), jnp.float32),
        ),
        in_specs=[pl.BlockSpec(memory_space=pltpu.SMEM)] + [anywhere] * 6 + [vmem, anywhere],
        out_specs=(anywhere, vmem),
        scratch_shapes=[pltpu.VMEM((20, 288, LANES), jnp.float32)]
        + [field] * 5
        + [
            pltpu.VMEM((10, ALL_ROWS, WIDE), jnp.bfloat16),
            pltpu.VMEM((KEPT, ALL_ROWS), jnp.float32),
        ]
        + [coeff] * 10
        + [pltpu.SemaphoreType.DMA((40,)), pltpu.SemaphoreType.DMA((8,))],
        input_output_aliases={8: 0},
        compiler_params=pltpu.CompilerParams(vmem_limit_bytes=32 * MB),
        name="edge",
    )(electrodes, own, core, chip, a, b, band, gram, s)


def matmul(a, b, dims=((1,), (0,))):
    return lax.dot_general(
        a, b, (dims, ((), ())), precision=HIGHEST, preferred_element_type=jnp.float32
    )


def galerkin(m0, m1, m2, m3):
    a12 = m2 + SHIFT * m1
    work = jnp.concatenate(
        [
            jnp.concatenate([m1 + SHIFT * m0, a12, m0], axis=1),
            jnp.concatenate([a12, m3 + SHIFT * m2, m1], axis=1),
        ],
        axis=0,
    )
    sub = lax.broadcasted_iota(jnp.int32, work.shape, 0)
    for k in range(2 * F):
        row = work[k : k + 1, :]
        row = row / row[:, k : k + 1]
        work = jnp.where(sub == k, row, work - work[:, k : k + 1] * row)
    return work[:, 2 * F :]


def final_kernel(
    pattern_ref, parts_ref, own_ref, core_ref, chip_ref, a_ref, b_ref, s_hbm,
    out_ref, sens_ref, bg, adj, s_ref, sems, *, damping,
):
    odd_x, odd_y = odd("gx"), odd("gy")

    def y_rows(is_left):
        src = pl.multiple_of(jnp.where(is_left, 48, 0), 8)
        dst = pl.multiple_of(jnp.where(is_left, 0, 144), 8)
        return pl.ds(src, 16), pl.ds(dst, 16)

    planes = pl.ds(1, 16)
    core_src, core_dst = y_rows(odd_y)
    chip_src, chip_dst = y_rows(jnp.logical_not(odd_y))
    near = pl.ds(3 * F, 128)
    pairs = [
        (s_hbm, s_ref),
        (own_ref.at[:, pl.ds(0, 128)], bg.at[planes, pl.ds(16, 128)]),
        (core_ref.at[:, core_src], bg.at[planes, core_dst]),
        (chip_ref.at[:, chip_src], bg.at[planes, chip_dst]),
        (a_ref.at[near], bg.at[jnp.where(odd_x, 0, 17), pl.ds(16, 128)]),
        (b_ref.at[near], bg.at[jnp.where(odd_x, 17, 0), pl.ds(16, 128)]),
    ]
    copies = run_copies(pairs, sems)

    total = jnp.sum(parts_ref[...], axis=0)

    def part(k):
        r, c = (k // 8) * F, (k % 8) * F
        return total[r : r + F, c : c + F]

    m = [part(k) for k in range(6)]
    p = [part(6), part(7), part(8), part(9).T, part(10).T]
    e = [part(k) for k in range(11, 15)]
    y = galerkin(*m[:4])
    y0, y1 = y[0:F], y[F:]
    probe = matmul(y0, p[0], ((0,), (0,))) + matmul(y1, p[1], ((0,), (0,)))
    lane = lax.broadcasted_iota(jnp.int32, (F, F), 1)
    sub = lax.broadcasted_iota(jnp.int32, (F, F), 0)
    first, second = jnp.zeros((F, F), jnp.int32), jnp.zeros((F, F), jnp.int32)
    for i in range(F):
        first = jnp.where(sub == i, pattern_ref[i, 0], first)
        second = jnp.where(sub == i, pattern_ref[i, 1], second)
    pairing = jnp.where(lane == first, 1.0, 0.0) - jnp.where(lane == second, 1.0, 0.0)
    measured = matmul(probe, pairing, ((1,), (1,)))
    weight = 8.0 * matmul(measured, pairing)
    z = jnp.concatenate([damping * y0, damping * y1, weight.T], axis=0)
    rows = []
    for k in range(4):
        rows.append(jnp.concatenate([m[k], m[k + 1], p[k]], axis=1))
        rows.append(jnp.concatenate([m[k + 1], m[k + 2], p[k + 1]], axis=1))
        rows.append(jnp.concatenate([p[k].T, p[k + 1].T, e[k]], axis=1))
    nz = matmul(jnp.concatenate(rows, axis=0), z)
    moments = [matmul(z, nz[48 * k : 48 * (k + 1)], ((0,), (0,))) for k in range(4)]
    q = galerkin(*moments)
    z0, z1 = matmul(z, q[0:F]), matmul(z, q[F:])
    none = jnp.zeros((F, F), jnp.float32)
    mix = [
        jnp.concatenate([y0, z0[0:F]], axis=1),
        jnp.concatenate([y1, z0[F : 2 * F] + z1[0:F]], axis=1),
        jnp.concatenate([none, z1[F : 2 * F]], axis=1),
        jnp.concatenate([none, z0[2 * F :]], axis=1),
        jnp.concatenate([none, z1[2 * F :]], axis=1),
    ]
    mix = [mix[i] for i in (0, 0, 1, 1, 2, 2, 3, 4, 4)]
    mix = jnp.concatenate(mix, axis=0).T
    hi = mix.astype(jnp.bfloat16)
    lo = (mix - hi.astype(jnp.float32)).astype(jnp.bfloat16)
    both = jnp.concatenate([hi, lo], axis=0)
    wait_all(copies)

    def combine(x, lanes):
        out = jnp.dot(both, s_ref[x, :, lanes], preferred_element_type=jnp.float32)
        return out[0:32] + out[32:64]

    def plane(x, carry):
        out = combine(x, slice(0, WIDE))
        for k in range(10):
            cols = slice(k * LANES, (k + 1) * LANES)
            if 0 < k < 9:
                out_ref[pl.ds(x * 8 + k - 9, F, stride=128), :] = out[0:F, cols]
            adj[x, tile_at(k), :] = out[F:, cols]
        return carry

    lax.fori_loop(1, 17, plane, 0)
    for x in (0, 17):
        out = combine(x, slice(LANES, 9 * LANES))
        for k in range(8):
            adj[x, tile_at(k + 1), :] = out[F:, k * LANES : (k + 1) * LANES]

    lane = lane_ids(F)

    def sens_plane(x, carry):
        b, a = bg[x, tile_at(1), :], adj[x, tile_at(1), :]
        before = (b - bg[x, tile_at(0), :]) * (a - adj[x, tile_at(0), :])
        for k in range(1, 9):
            bn, an = bg[x, tile_at(k + 1), :], adj[x, tile_at(k + 1), :]
            after = (bn - b) * (an - a)
            total = before + after
            for s in (x - 1, x + 1):
                total = total + (bg[s, tile_at(k), :] - b) * (adj[s, tile_at(k), :] - a)
            bu = jnp.where(lane == LANES - 1, 0.0, pltpu.roll(b, LANES - 1, 1))
            au = jnp.where(lane == LANES - 1, 0.0, pltpu.roll(a, LANES - 1, 1))
            bd = jnp.where(lane == 0, 0.0, pltpu.roll(b, 1, 1))
            ad = jnp.where(lane == 0, 0.0, pltpu.roll(a, 1, 1))
            total = total + (bu - b) * (au - a) + (bd - b) * (ad - a)
            sens_ref[x - 1, k - 1 : k, :] = -0.5 * jnp.sum(total, axis=0, keepdims=True)
            before, b, a = after, bn, an
        return carry

    lax.fori_loop(1, 17, sens_plane, 0, unroll=2)


def final(pattern, parts, own, core, chip, a, b, s, damping):
    anywhere = pl.BlockSpec(memory_space=pl.ANY)
    vmem = pl.BlockSpec(memory_space=pltpu.VMEM)

    def kernel(*refs):
        final_kernel(*refs, damping=damping)

    return pl.pallas_call(
        kernel,
        out_shape=(
            jax.ShapeDtypeStruct((2048, LANES), jnp.float32),
            jax.ShapeDtypeStruct((16, 8, LANES), jnp.float32),
        ),
        in_specs=[pl.BlockSpec(memory_space=pltpu.SMEM), vmem] + [anywhere] * 6,
        scratch_shapes=[
            pltpu.VMEM((18, 160, LANES), jnp.float32),
            pltpu.VMEM((18, 160, LANES), jnp.float32),
            pltpu.VMEM((18, KEPT, WIDE), jnp.bfloat16),
            pltpu.SemaphoreType.DMA((6,)),
        ],
        compiler_params=pltpu.CompilerParams(vmem_limit_bytes=56 * MB),
        name="final",
    )(pattern, parts, own, core, chip, a, b, s)


def spread(block, axis, count, groups=None):
    copies = jnp.broadcast_to(block[None], (count,) + block.shape)
    return lax.all_to_all(copies, axis, 0, 0, axis_index_groups=groups)


def swaps(first, count):
    lows = range(first, count - 1, 2)
    return [(i, i + 1) for i in lows] + [(i + 1, i) for i in lows]


def on_device(background, conductivity, perturbation, electrodes, pattern):
    size_x, size_y, size_z = conductivity.shape
    count_x, count_y = lax.axis_size("gx"), lax.axis_size("gy")
    flat = background.reshape(-1, size_z)
    own, core, chip = pack(flat, conductivity, perturbation)
    chip = lax.ppermute(chip, "gy", swaps(1, count_y))
    core = lax.ppermute(core, "gy", swaps(0, count_y))
    a, b = pack_x(own, core, chip)
    a = lax.ppermute(a, "gx", swaps(0, count_x))
    b = lax.ppermute(b, "gx", swaps(1, count_x))
    s, band, gram = inner(electrodes, own, core, chip)
    s, pay = edge(electrodes, own, core, chip, a, b, band, gram, s)
    pay = pay + lax.ppermute(pay, "gy", swaps(0, count_y))
    pay = jnp.sum(spread(pay, "gx", count_x), axis=0)
    chips = count_y // 2
    groups = [[2 * i + c for i in range(chips)] for c in range(2)]
    parts = spread(pay, "gy", chips, groups)
    cells = size_x * size_y * size_z * count_x * count_y
    damping = 80.0 / math.sqrt(cells)
    tangent, sens = final(pattern, parts, own, core, chip, a, b, s, damping)
    return tangent.reshape(background.shape), sens


def solution(mesh):
    in_specs = (P(None, "gx", "gy", None), P("gx", "gy", None), P("gx", "gy", None), P(), P())
    out_specs = (P(None, "gx", "gy", None), P("gx", "gy", None))
    return jax.shard_map(
        on_device, mesh=mesh, in_specs=in_specs, out_specs=out_specs, check_vma=False
    )
```

time: 125 us -> 99.4 us (0.80)
  waiting for transfers between devices: 28.1 us -> 15.2 us
  Pallas kernels: 51.6 us -> 39.8 us
  starting transfers between devices: 18.8 us -> 14.3 us
  blocking collectives: 17.7 us -> 20.4 us
    pallas_call x1 -> x2, Pallas kernels: 33 us -> 20.3 us  [the longest x1 10.3 us: edge(): pl.pallas_call(edge_kernel, out_shape=(jax.ShapeDtypeStruct((18, KEPT, WI...]
    ppermute x5, waiting for transfers between devices: 20.9 us -> 8.52 us  [the longest x1 7.53 us: on_device(): chip = lax.ppermute(chip, 'gy', swaps(1, count_y))]
    ppermute x5, starting transfers between devices: 11.2 us -> 6.62 us  [the longest x1 4.27 us: on_device(): chip = lax.ppermute(chip, 'gy', swaps(1, count_y))]
    all_to_all x1, blocking collectives: 17.7 us -> 20.4 us  [spread(): return lax.all_to_all(copies, axis, 0, 0, axis_index_groups=groups)]
    unnamed x13 -> x27, local copies, waits for them, and re-layouts: 6.69 us -> 7.71 us
  transfers between devices with their start and end apart: 6 -> 6, of which waited for: 6 -> 3; matrix products, arithmetic and copies ran while one was open for 0% -> 1% of each run, Pallas kernels for 0% -> 10%
where the time goes in v2:
time: 99.4 us; the launch traced here: 99 us
  Pallas kernels  39.8 us (40%)
  blocking collectives  20.4 us (21%)
  waiting for transfers between devices  15.2 us (15%)
  starting transfers between devices  14.3 us (14%)
  local copies, waits for them, and re-layouts  8.45 us (9%)
    all_to_all x1, blocking collectives, spread(): return lax.all_to_all(copies, axis, 0, 0, axis_index_groups=groups)  20.4 us
    pallas_call x1, Pallas kernels, final(): pl.pallas_call(kernel, out_shape=(jax.ShapeDtypeStruct((2048, LANES), jnp...  17.1 us
    pallas_call x1, Pallas kernels, edge(): pl.pallas_call(edge_kernel, out_shape=(jax.ShapeDtypeStruct((18, KEPT, WI...  10.3 us
    pallas_call x1, Pallas kernels, inner(): pl.pallas_call(inner_kernel, out_shape=(jax.ShapeDtypeStruct((18, KEPT, W...  9.92 us
    unnamed x27, local copies, waits for them, and re-layouts  7.71 us
    all_to_all x1, starting transfers between devices, spread(): return lax.all_to_all(copies, axis, 0, 0, axis_index_groups=groups)  7.64 us
    ppermute x1, waiting for transfers between devices, on_device(): chip = lax.ppermute(chip, 'gy', swaps(1, count_y))  7.53 us
    all_to_all x1, waiting for transfers between devices, spread(): return lax.all_to_all(copies, axis, 0, 0, axis_index_groups=groups)  6.65 us
  transfers between devices with their start and end apart: 6, of which 3 were waited for; matrix products, arithmetic and copies ran while one was open for 1% of the time, Pallas kernels for 10%

profile of v2, /device:TPU:2, one launch (start us, length us, event | category | flops | bytes accessed | tf_op | source)
XLA Modules:
  0.0 99.0 jit_solution(6477005770868885434)
XLA Ops:
  0.6 0.0 copy-start.6
  0.6 1.2 %copy-done.6 = f32[16,16,8,128]{3,2,1,0:T(8,128)S(1)} copy-done((f32[16,16,8,128]{3,2,1,0:T(8,128)S(1)}, f32[16,16,8,128]{3,2,1,0:T(8,128)}, u32[]{:S(2)}) %copy-start.6) | copy-done | bytes 1048600
  1.9 0.0 copy-start.7
  1.9 0.8 copy-done.7
  2.7 0.0 copy-start.8
  2.7 0.8 copy-done.8
  3.5 0.9 pack_y.1
  4.4 0.0 copy-start.1
  4.4 0.1 collective-permute-start
  4.5 4.3 %collective-permute-start.1 = (f32[16,72,128]{2,1,0:T(8,128)S(1)}, f32[16,72,128]{2,1,0:T(8,128)S(1)}, u32[]{:S(2)}, u32[]{:S(2)}) collective-permute-start(f32[16,72,128]{2,1,0:T(8,128)S(1)} %get-tuple-element.16), channel_id=1, source_target_pairs={{1,2},{3,4},{5,6},{7,8},{9,10},{11,12},{13,14},{15,16},{17,18},{19... | collective-permute-start | bytes 1769480 | tf_op jit(solution)/shard_map/ppermute | solution.py:704
  8.8 0.0 collective-permute-done.core_ref.refs_3_
  8.8 0.0 copy-start.2
  8.8 7.5 %collective-permute-done.1.chip_ref.refs_4_ = f32[16,72,128]{2,1,0:T(8,128)S(1)} collective-permute-done((f32[16,72,128]{2,1,0:T(8,128)S(1)}, f32[16,72,128]{2,1,0:T(8,128)S(1)}, u32[]{:S(2)}, u32[]{:S(2)}) %collective-permute-start.1) | collective-permute-done | bytes 589856 | tf_op jit(solution)/shard_map/ppermute | solution.py:704
  16.4 0.0 copy-start.3
  16.4 1.6 %pack_x.1 = (f32[832,128]{1,0:T(8,128)S(1)}, f32[832,128]{1,0:T(8,128)S(1)}) custom-call(f32[16,144,128]{2,1,0:T(8,128)S(1)} %get-tuple-element.14.own_ref.refs_2_, f32[16,72,128]{2,1,0:T(8,128)S(1)} %collective-permute-done.core_ref.refs_3_, f32[16,72,128]{2,1,0:T(8,128)S(1)} %collective-permute-done.1.chip_ref.refs_4_), custom_call_target="tpu_custom_call" | custom-call | tf_op jit(solution)/shard_map/pack_x/pallas_call | solution.py:140
  18.0 1.4 %collective-permute-start.2 = (f32[832,128]{1,0:T(8,128)S(1)}, f32[832,128]{1,0:T(8,128)S(1)}, u32[]{:S(2)}, u32[]{:S(2)}) collective-permute-start(f32[832,128]{1,0:T(8,128)S(1)} %get-tuple-element.17), channel_id=1, source_target_pairs={{0,32},{64,96},{128,160},{192,224},{32,0},{96,64},{160,128},{224,1... | collective-permute-start | bytes 1277960 | tf_op jit(solution)/shard_map/ppermute | solution.py:707
  19.3 0.7 collective-permute-start.3
  20.0 0.0 copy-start.9
  20.0 0.6 copy-done.9
  20.7 0.0 copy-start.10
  20.7 9.9 %inner.1 = (bf16[18,144,1280]{2,1,0:T(8,128)(2,1)S(1)}, f32[12,256,128]{2,1,0:T(8,128)S(1)}, f32[144,208]{1,0:T(8,128)S(1)}) custom-call(s32[16]{0:T(128)S(1)} %copy-done.9, f32[16,144,128]{2,1,0:T(8,128)S(1)} %get-tuple-element.14.own_ref.refs_2_, f32[16,72,128]{2,1,0:T(8,128)S(1)} %collective-permute-done.core_ref.refs_3_, ...), custom_call_target="tpu_custom_call" | custom-call | flops 4000000000 | bytes 16000000 | tf_op jit(solution)/shard_map/inner/pallas_call | solution.py:351
  30.6 0.0 copy-start.12
  30.6 0.0 collective-permute-done.2.a_ref.refs_5_
  30.6 0.0 copy-start.4
  30.6 0.0 collective-permute-done.3.b_ref.refs_6_
  30.6 0.0 copy-start.5
  30.7 0.0 copy-done.1
  30.7 0.0 copy-done.2
  30.7 0.0 copy-done.3
  30.7 0.0 copy-done.10
  30.7 10.3 %edge.1 = (bf16[18,144,1280]{2,1,0:T(8,128)(2,1)S(1)}, f32[32,128]{1,0:T(8,128)S(1)}) custom-call(s32[16]{0:T(128)S(1)} %copy-done.10, f32[16,144,128]{2,1,0:T(8,128)S(1)} %get-tuple-element.14.own_ref.refs_2_, f32[16,72,128]{2,1,0:T(8,128)S(1)} %collective-permute-done.core_ref.refs_3_, ...), custom_call_target="tpu_custom_call", output_to_operand_aliasing={{0}: (8, {})} | custom-call | tf_op jit(solution)/shard_map/edge/pallas_call | solution.py:506
  41.0 0.0 copy-start
  41.1 2.8 %copy-done = bf16[18,144,1280]{2,1,0:T(8,128)(2,1)} copy-done((bf16[18,144,1280]{2,1,0:T(8,128)(2,1)}, bf16[18,144,1280]{2,1,0:T(8,128)(2,1)S(1)}, u32[]{:S(2)}) %copy-start) | copy-done | bytes 6635544
  43.8 0.2 collective-permute-start.4
  44.0 1.0 collective-permute-done.4
  45.0 20.4 %all_to_all.10 = f32[8,32,128]{2,1,0:T(8,128)S(1)} all-to-all(f32[8,32,128]{2,1,0:T(8,128)S(1)} %broadcast_in_dim.4), channel_id=1, replica_groups=mesh['gx'=8,'gy'=32] {'gx'}, dimensions={0} | all-to-all | bytes 262144 | tf_op jit(solution)/shard_map/all_to_all | solution.py:691
  65.5 0.7 broadcast_in_dim.5
  66.2 7.6 %all-to-all-start.1 = ((f32[16,32,128]{2,1,0:T(8,128)}), f32[16,32,128]{2,1,0:T(8,128)S(1)}, u32[]{:S(2)}, u32[]{:S(2)}) async-start(f32[16,32,128]{2,1,0:T(8,128)} %broadcast_in_dim.5), calls=%async_computation.1 | async-start | bytes 524288 | tf_op jit(solution)/shard_map/all_to_all | solution.py:691
  73.8 0.0 copy-done.12
  73.8 0.7 copy.9.refs_0_
  74.5 6.7 %all-to-all-done.1.refs_1_ = f32[16,32,128]{2,1,0:T(8,128)S(1)} async-done(((f32[16,32,128]{2,1,0:T(8,128)}), f32[16,32,128]{2,1,0:T(8,128)S(1)}, u32[]{:S(2)}, u32[]{:S(2)}) %all-to-all-start.1) | async-done | bytes 262176 | tf_op jit(solution)/shard_map/all_to_all | solution.py:691
  81.2 0.0 copy-start.11
  81.2 0.0 copy-done.4
  81.2 0.0 copy-done.5
  81.2 0.7 copy-done.11
  81.9 17.1 %final.1 = (f32[2048,128]{1,0:T(8,128)}, f32[16,8,128]{2,1,0:T(8,128)}) custom-call(s32[16,2]{1,0:T(8,128)} %copy.9.refs_0_, f32[16,32,128]{2,1,0:T(8,128)} %copy-done.11, f32[16,144,128]{2,1,0:T(8,128)} %copy-done.1, f32[16,72,128]{2,1,0:T(8,128)} %copy-done.2, f32[16,72,128]{2,1,0:T(8,128)} %copy-done.3, f32[832,128]{1,0:T(8,128)} %copy-done.4, ...), custom_call_target="tpu_custom_call" | custom-call | tf_op jit(solution)/shard_map/final/pallas_call | solution.py:671
  (3 shorter events, 0.0 us)
Async XLA Ops:
  0.6 1.2 %copy-start.6 = (f32[16,16,8,128]{3,2,1,0:T(8,128)S(1)}, f32[16,16,8,128]{3,2,1,0:T(8,128)}, u32[]{:S(2)}) copy-start(f32[16,16,8,128]{3,2,1,0:T(8,128)} %param.5) | copy-start | bytes 3145732
  1.9 0.8 copy-start.7
  2.7 0.8 copy-start.8
  4.4 26.2 %copy-start.1 = (f32[16,144,128]{2,1,0:T(8,128)}, f32[16,144,128]{2,1,0:T(8,128)S(1)}, u32[]{:S(2)}) copy-start(f32[16,144,128]{2,1,0:T(8,128)S(1)} %get-tuple-element.14.own_ref.refs_2_) | copy-start | bytes 3538948
  4.4 4.4 %collective-permute-start = (f32[16,72,128]{2,1,0:T(8,128)S(1)}, f32[16,72,128]{2,1,0:T(8,128)S(1)}, u32[]{:S(2)}, u32[]{:S(2)}) collective-permute-start(f32[16,72,128]{2,1,0:T(8,128)S(1)} %get-tuple-element.15), channel_id=1, source_target_pairs={{0,1},{2,3},{4,5},{6,7},{8,9},{10,11},{12,13},{14,15},{16,17},{18,... | collective-permute-start | bytes 1769480 | tf_op jit(solution)/shard_map/ppermute | solution.py:705
  4.5 11.8 %collective-permute-start.1 = (f32[16,72,128]{2,1,0:T(8,128)S(1)}, f32[16,72,128]{2,1,0:T(8,128)S(1)}, u32[]{:S(2)}, u32[]{:S(2)}) collective-permute-start(f32[16,72,128]{2,1,0:T(8,128)S(1)} %get-tuple-element.16), channel_id=1, source_target_pairs={{1,2},{3,4},{5,6},{7,8},{9,10},{11,12},{13,14},{15,16},{17,18},{19... | collective-permute-start | bytes 1769480 | tf_op jit(solution)/shard_map/ppermute | solution.py:704
  8.8 21.8 %copy-start.2 = (f32[16,72,128]{2,1,0:T(8,128)}, f32[16,72,128]{2,1,0:T(8,128)S(1)}, u32[]{:S(2)}) copy-start(f32[16,72,128]{2,1,0:T(8,128)S(1)} %collective-permute-done.core_ref.refs_3_) | copy-start | bytes 1769476
  16.4 14.3 %copy-start.3 = (f32[16,72,128]{2,1,0:T(8,128)}, f32[16,72,128]{2,1,0:T(8,128)S(1)}, u32[]{:S(2)}) copy-start(f32[16,72,128]{2,1,0:T(8,128)S(1)} %collective-permute-done.1.chip_ref.refs_4_) | copy-start | bytes 1769476
  18.0 12.7 %collective-permute-start.2 = (f32[832,128]{1,0:T(8,128)S(1)}, f32[832,128]{1,0:T(8,128)S(1)}, u32[]{:S(2)}, u32[]{:S(2)}) collective-permute-start(f32[832,128]{1,0:T(8,128)S(1)} %get-tuple-element.17), channel_id=1, source_target_pairs={{0,32},{64,96},{128,160},{192,224},{32,0},{96,64},{160,128},{224,1... | collective-permute-start | bytes 1277960 | tf_op jit(solution)/shard_map/ppermute | solution.py:707
  19.3 11.3 %collective-permute-start.3 = (f32[832,128]{1,0:T(8,128)S(1)}, f32[832,128]{1,0:T(8,128)S(1)}, u32[]{:S(2)}, u32[]{:S(2)}) collective-permute-start(f32[832,128]{1,0:T(8,128)S(1)} %get-tuple-element.18), channel_id=1, source_target_pairs={{32,64},{96,128},{160,192},{64,32},{128,96},{192,160},{33,65},{97,... | collective-permute-start | bytes 1277960 | tf_op jit(solution)/shard_map/ppermute | solution.py:708
  20.0 0.7 copy-start.9
  20.7 10.0 %copy-start.10 = (s32[16]{0:T(128)S(1)}, s32[16]{0:T(128)}, u32[]{:S(2)}) copy-start(s32[16]{0:T(128)} %elec_ref.3) | copy-start | bytes 196
  30.6 43.2 %copy-start.12 = (s32[16,2]{0,1:T(2,128)S(1)}, s32[16,2]{0,1:T(2,128)}, u32[]{:S(2)}) copy-start(s32[16,2]{0,1:T(2,128)} %param.9) | copy-start | bytes 388
  30.6 50.5 %copy-start.4 = (f32[832,128]{1,0:T(8,128)}, f32[832,128]{1,0:T(8,128)S(1)}, u32[]{:S(2)}) copy-start(f32[832,128]{1,0:T(8,128)S(1)} %collective-permute-done.2.a_ref.refs_5_) | copy-start | bytes 1277956
  30.6 50.5 %copy-start.5 = (f32[832,128]{1,0:T(8,128)}, f32[832,128]{1,0:T(8,128)S(1)}, u32[]{:S(2)}) copy-start(f32[832,128]{1,0:T(8,128)S(1)} %collective-permute-done.3.b_ref.refs_6_) | copy-start | bytes 1277956
  41.0 2.8 %copy-start = (bf16[18,144,1280]{2,1,0:T(8,128)(2,1)}, bf16[18,144,1280]{2,1,0:T(8,128)(2,1)S(1)}, u32[]{:S(2)}) copy-start(bf16[18,144,1280]{2,1,0:T(8,128)(2,1)S(1)} %get-tuple-element.23.refs_7_) | copy-start | bytes 19906564
  43.8 1.2 %collective-permute-start.4 = (f32[32,128]{1,0:T(8,128)S(1)}, f32[32,128]{1,0:T(8,128)S(1)}, u32[]{:S(2)}, u32[]{:S(2)}) collective-permute-start(f32[32,128]{1,0:T(8,128)S(1)} %get-tuple-element.22), channel_id=1, source_target_pairs={{0,1},{2,3},{4,5},{6,7},{8,9},{10,11},{12,13},{14,15},{16,17},{18,... | collective-permute-start | bytes 49160 | tf_op jit(solution)/shard_map/ppermute | solution.py:711
  66.2 15.0 %all-to-all-start.1 = ((f32[16,32,128]{2,1,0:T(8,128)}), f32[16,32,128]{2,1,0:T(8,128)S(1)}, u32[]{:S(2)}, u32[]{:S(2)}) async-start(f32[16,32,128]{2,1,0:T(8,128)} %broadcast_in_dim.5), calls=%async_computation.1 | async-start | bytes 524288 | tf_op jit(solution)/shard_map/all_to_all | solution.py:691
  81.2 0.7 copy-start.11

commit v3 on v2

v3 whole, which is shorter than its diff:
```python
import math

import jax
import jax.numpy as jnp
from jax import lax
from jax.experimental import pallas as pl
from jax.experimental.pallas import tpu as pltpu
from jax.sharding import PartitionSpec as P

SHIFT = 12.0
F = 16
LANES = 128
HALO = 4
HIGHEST = lax.Precision.HIGHEST
V0, V1, V2, E0, E1, V3, E2 = 0, 32, 64, 96, 112, 144, 176
KEPT, ALL_ROWS = 144, 208
WIDE = 10 * LANES
MB = 2**20


def tile_at(y):
    return slice(y * F, (y + 1) * F)


def run_copies(pairs, sems, first=0):
    copies = [
        pltpu.make_async_copy(s, d, sems.at[first + i]) for i, (s, d) in enumerate(pairs)
    ]
    for c in copies:
        c.start()
    return copies


def wait_all(copies):
    for c in copies:
        c.wait()


def odd(axis):
    return lax.rem(lax.axis_index(axis), 2) == 1


PARTS = 4


def pack_kernel(
    bg_hbm, cond_hbm, pert_hbm, own_ref, core_ref, chip_ref, a_ref, b_ref,
    bg, cond_v, pert_v, sems,
):
    size_x, size_y = cond_v.shape[0], cond_v.shape[1]
    each = size_x // PARTS
    pairs = [(cond_hbm, cond_v), (pert_hbm, pert_v)]
    for i in range(PARTS):
        planes = pl.ds(i * each, each)
        pairs.append((bg_hbm.at[:, planes], bg.at[:, planes]))
    copies = run_copies(pairs, sems)

    def fill(top_ref, bottom_ref):
        wait_all(copies[:2])

        def plane(x, carry):
            for y in range(size_y):
                tile = bg[:, x, y, :]
                own_ref[x, tile_at(y), :] = tile
                if y >= size_y - HALO:
                    top_ref[x, tile_at(y - size_y + HALO), :] = tile
                if y < HALO:
                    bottom_ref[x, tile_at(y), :] = tile
            cond, pert = cond_v[x], pert_v[x]
            own_ref[x, 128:136, :] = cond
            own_ref[x, 136:144, :] = pert
            top_ref[x, 64:72, :] = jnp.concatenate([cond[4:8], pert[4:8]], axis=0)
            bottom_ref[x, 64:72, :] = jnp.concatenate([cond[0:4], pert[0:4]], axis=0)
            return carry

        for i in range(PARTS):
            copies[2 + i].wait()
            lax.fori_loop(i * each, (i + 1) * each, plane, 0, unroll=each)

    @pl.when(odd("gy"))
    def _():
        fill(chip_ref, core_ref)

    @pl.when(jnp.logical_not(odd("gy")))
    def _():
        fill(core_ref, chip_ref)

    for out, up in ((a_ref, jnp.logical_not(odd("gx"))), (b_ref, odd("gx"))):
        for dx in range(1, HALO + 1):
            out[dx - 1] = own_ref[jnp.where(up, size_x - dx, dx - 1)]


def pack(background, conductivity, perturbation):
    shape = jax.ShapeDtypeStruct
    inputs = [
        pltpu.with_memory_space_constraint(v, pltpu.HBM)
        for v in (background, conductivity, perturbation)
    ]
    return pl.pallas_call(
        pack_kernel,
        out_shape=(
            shape((16, 144, LANES), jnp.float32),
            shape((16, 72, LANES), jnp.float32),
            shape((16, 72, LANES), jnp.float32),
            shape((HALO, 144, LANES), jnp.float32),
            shape((HALO, 144, LANES), jnp.float32),
        ),
        in_specs=[pl.BlockSpec(memory_space=pltpu.HBM)] * 3,
        scratch_shapes=[
            pltpu.VMEM((16, 16, 8, LANES), jnp.float32),
            pltpu.VMEM((16, 8, LANES), jnp.float32),
            pltpu.VMEM((16, 8, LANES), jnp.float32),
            pltpu.SemaphoreType.DMA((2 + PARTS,)),
        ],
        compiler_params=pltpu.CompilerParams(vmem_limit_bytes=16 * MB),
        name="pack_y",
    )(*inputs)


def corner_layout():
    table, at = [], 0
    for dx in range(1, HALO):
        rows = (HALO - dx) * F
        table.append((dx, rows, at))
        at += 2 * rows + 16
    return table, at


CORNERS, CORNER_ROWS = corner_layout()


def pack_x_kernel(core_ref, chip_ref, a_ref, b_ref):
    def send(left_ref, right_ref):
        for out, up in ((a_ref, jnp.logical_not(odd("gx"))), (b_ref, odd("gx"))):
            for dx, rows, at in CORNERS:
                x = jnp.where(up, left_ref.shape[0] - dx, dx - 1)
                out[at : at + rows, :] = left_ref[x, 64 - rows : 64, :]
                out[at + rows : at + 2 * rows, :] = right_ref[x, 0:rows, :]
                at += 2 * rows
                out[at : at + 8, :] = left_ref[x, 64:72, :]
                out[at + 8 : at + 16, :] = right_ref[x, 64:72, :]

    @pl.when(odd("gy"))
    def _():
        send(core_ref, chip_ref)

    @pl.when(jnp.logical_not(odd("gy")))
    def _():
        send(chip_ref, core_ref)


def pack_x(core, chip):
    shape = jax.ShapeDtypeStruct((CORNER_ROWS, LANES), jnp.float32)
    return pl.pallas_call(
        pack_x_kernel,
        out_shape=(shape, shape),
        compiler_params=pltpu.CompilerParams(vmem_limit_bytes=16 * MB),
        name="pack_x",
    )(core, chip)


def lane_ids(rows):
    return lax.broadcasted_iota(jnp.int32, (rows, LANES), 1)


def own_copies(own_ref, core_ref, chip_ref, bext):
    odd_y = odd("gy")
    core_at = pl.multiple_of(jnp.where(odd_y, 0, 192), 8)
    chip_at = pl.multiple_of(jnp.where(odd_y, 192, 0), 8)
    core_c = pl.multiple_of(jnp.where(odd_y, 272, 280), 8)
    chip_c = pl.multiple_of(jnp.where(odd_y, 280, 272), 8)
    return [
        (own_ref.at[:, pl.ds(128, 16)], bext.at[:, pl.ds(256, 16)]),
        (core_ref.at[:, pl.ds(64, 8)], bext.at[:, pl.ds(core_c, 8)]),
        (chip_ref.at[:, pl.ds(64, 8)], bext.at[:, pl.ds(chip_c, 8)]),
        (own_ref.at[:, pl.ds(0, 128)], bext.at[:, pl.ds(64, 128)]),
        (core_ref.at[:, pl.ds(0, 64)], bext.at[:, pl.ds(core_at, 64)]),
        (chip_ref.at[:, pl.ds(0, 64)], bext.at[:, pl.ds(chip_at, 64)]),
    ]


def faces(rows_of, planes, ccoef, pcoef):
    lane = lane_ids(16)
    last = lane == LANES - 1
    edge = (lane == 0) | last

    def cells(x):
        own, left, right = rows_of(x)
        return (
            jnp.concatenate([left[0:4], own[0:8], right[0:4]], axis=0),
            jnp.concatenate([left[4:8], own[8:16], right[4:8]], axis=0),
        )

    for x in planes:
        now, then = cells(x), cells(x + 1)
        for coef, c, n, half, base in (
            (ccoef, now[0], then[0], 0.5, 0.05 - SHIFT),
            (pcoef, now[1], then[1], -0.5, 0.0),
        ):
            fx, fy, fu, fd, dd = coef
            fx[x] = half * (c + n)
            fy[x] = half * (c + pltpu.roll(c, 15, 0))
            up = jnp.where(last, 0.0, half * (c + pltpu.roll(c, LANES - 1, 1)))
            fu[x] = up
            fd[x] = pltpu.roll(up, 1, 1)
            dd[x] = base + jnp.where(edge, half * c, 0.0)


def stencil_plane(get, coeffs, x, y0, y1, mask_x, mask_y, emit):
    fx, fy, fu, fd, dd = coeffs
    q = get(x, y0)
    flux = fy[x, y0 - 1 : y0, :] * (q - get(x, y0 - 1))
    for y in range(y0, y1):
        nxt = get(x, y + 1)
        row = slice(y, y + 1)
        later = fy[x, row, :] * (nxt - q)
        out = dd[x, row, :] * q + (flux - later)
        out = out + fx[x - 1, row, :] * (q - get(x - 1, y))
        out = out - fx[x, row, :] * (get(x + 1, y) - q)
        out = out + fd[x, row, :] * (q - pltpu.roll(q, 1, 1))
        out = out - fu[x, row, :] * (pltpu.roll(q, LANES - 1, 1) - q)
        mask = mask_x
        if y < 4:
            mask = mask_y[0] if mask is None else mask * mask_y[0]
        elif y >= 12:
            mask = mask_y[1] if mask is None else mask * mask_y[1]
        if mask is not None:
            out = out * mask
        emit(y, out)
        flux, q = later, nxt


def tiles(ref):
    return lambda x, y: ref[x, tile_at(y), :]


def put_split(s_ref, i, row, y, value, exact=False):
    lanes = slice((y - 3) * LANES, (y - 2) * LANES)
    hi = value.astype(jnp.bfloat16)
    s_ref[i, row : row + F, lanes] = hi
    if not exact:
        lo = (value - hi.astype(jnp.float32)).astype(jnp.bfloat16)
        s_ref[i, row + F : row + 2 * F, lanes] = lo


def electrode_ids(elec_ref):
    sub = lax.broadcasted_iota(jnp.int32, (F, LANES), 0)
    ids = jnp.zeros((F, LANES), jnp.int32)
    for e in range(F):
        ids = jnp.where(sub == e, elec_ref[e], ids)
    return ids - lane_ids(F)


def grid_masks():
    one, zero = jnp.float32(1), jnp.float32(0)
    masks = []
    for axis in ("gx", "gy"):
        i = lax.axis_index(axis)
        low, high = i > 0, i < lax.axis_size(axis) - 1
        masks.append((jnp.where(low, one, zero), jnp.where(high, one, zero)))
    return masks


def unit_plane(ids, at_x, e0, i, s_ref, s_at, y_kept):
    size_x, size_y = 16 * lax.axis_size("gx"), 8 * lax.axis_size("gy")
    good_x = (at_x >= 0) & (at_x < size_x)
    for y in range(2, 14):
        at_y = lax.axis_index("gy") * 8 + y - 4
        good = good_x & (at_y >= 0) & (at_y < size_y)
        here = jnp.where(good, (at_x * size_y + at_y) * LANES, -(2**20))
        value = jnp.where(ids == here, 1.0, 0.0)
        e0[i, tile_at(y), :] = value
        if y_kept[0] <= y < y_kept[1]:
            put_split(s_ref, s_at, E0, y, value, exact=True)


def gram_of(s_ref, i):
    return lax.dot_general(
        s_ref[i, 0:KEPT, LANES : 9 * LANES],
        s_ref[i, :, LANES : 9 * LANES],
        (((1,), (1,)), ((), ())),
        preferred_element_type=jnp.float32,
    )


def inner_kernel(
    elec_ref, own_ref, core_ref, chip_ref, s_hbm, wide_ref, band_ref, side_ref, gram_ref,
    bext, v0, v1, v2, e0, e1, s_ref, cx, cy, cu, cd, cr, px, py, pu, pd, pr, sems, out_sems,
):
    copies = run_copies(own_copies(own_ref, core_ref, chip_ref, bext), sems)
    gx = lax.axis_index("gx")
    _, mask_y = grid_masks()
    ids = electrode_ids(elec_ref)

    def units(x, carry):
        unit_plane(ids, gx * 16 + x, e0, x, s_ref, x, (3, 13))
        return carry

    lax.fori_loop(2, 14, units, 0)
    wait_all(copies[:3])
    ccoef, pcoef = (cx, cy, cu, cd, cr), (px, py, pu, pd, pr)
    faces(
        lambda x: (bext[x, 256:272, :], bext[x, 272:280, :], bext[x, 280:288, :]),
        range(15), ccoef, pcoef,
    )
    wait_all(copies[3:])
    outs = []

    def hand_on(src, dst):
        outs.extend(run_copies([(src, dst)], out_sems, len(outs)))

    def sweep(src, dst, coeffs, first, reach, row, keep):
        def plane(x, carry):
            def emit(y, out):
                if dst is not None:
                    dst[x, tile_at(y), :] = out
                if keep[0] <= y < keep[1]:
                    put_split(s_ref, x, row, y, out)

            stencil_plane(tiles(src), coeffs, x, 4 - reach, 12 + reach, None, mask_y, emit)
            return carry

        lax.fori_loop(first, 16 - first, plane, 0, unroll=2)

    def hand_band(src, first, at):
        for k, x in enumerate((first, 14 - first)):
            hand_on(src.at[pl.ds(x, 2)], band_ref.at[pl.ds(at + 2 * k, 2)])

    hand_on(bext.at[pl.ds(0, 6)], wide_ref.at[pl.ds(0, 6)])
    hand_on(bext.at[pl.ds(10, 6)], wide_ref.at[pl.ds(6, 6)])
    sweep(bext, v0, pcoef, 1, 3, V0, (3, 13))
    hand_band(v0, 1, 0)
    sweep(v0, v1, ccoef, 2, 2, V1, (3, 13))
    hand_band(v1, 2, 4)
    sweep(v1, v2, ccoef, 3, 1, V2, (3, 13))
    hand_band(v2, 3, 8)
    hand_on(s_ref.at[pl.ds(1, 3), pl.ds(0, 96)], side_ref.at[pl.ds(0, 3)])
    hand_on(s_ref.at[pl.ds(12, 3), pl.ds(0, 96)], side_ref.at[pl.ds(3, 3)])
    sweep(e0, e1, ccoef, 3, 1, E1, (3, 13))
    hand_on(s_ref.at[pl.ds(4, 8), pl.ds(0, KEPT)], s_hbm)
    sweep(v2, None, ccoef, 4, 0, V3, (4, 12))
    sweep(e1, None, ccoef, 4, 0, E2, (4, 12))

    gram_ref[...] = gram_of(s_ref, 4)

    def gram_step(x, carry):
        gram_ref[...] += gram_of(s_ref, x)
        return carry

    lax.fori_loop(5, 12, gram_step, 0, unroll=7)
    wait_all(outs)


def inner(electrodes, own, core, chip):
    anywhere = pl.BlockSpec(memory_space=pl.ANY)
    vmem = pl.BlockSpec(memory_space=pltpu.VMEM)
    field = pltpu.VMEM((16, 256, LANES), jnp.float32)
    coeff = pltpu.VMEM((16, 16, LANES), jnp.float32)
    shape = jax.ShapeDtypeStruct
    return pl.pallas_call(
        inner_kernel,
        out_shape=(
            pltpu.HBM((8, KEPT, WIDE), jnp.bfloat16),
            shape((12, 288, LANES), jnp.float32),
            shape((12, 256, LANES), jnp.float32),
            shape((6, 96, WIDE), jnp.bfloat16),
            shape((KEPT, ALL_ROWS), jnp.float32),
        ),
        in_specs=[pl.BlockSpec(memory_space=pltpu.SMEM)] + [anywhere] * 3,
        out_specs=(pl.BlockSpec(memory_space=pltpu.HBM), vmem, vmem, vmem, vmem),
        scratch_shapes=[pltpu.VMEM((16, 288, LANES), jnp.float32)]
        + [field] * 5
        + [pltpu.VMEM((16, ALL_ROWS, WIDE), jnp.bfloat16)]
        + [coeff] * 10
        + [pltpu.SemaphoreType.DMA((6,)), pltpu.SemaphoreType.DMA((11,))],
        compiler_params=pltpu.CompilerParams(vmem_limit_bytes=36 * MB),
        cost_estimate=pl.CostEstimate(
            flops=4 * 10**9, bytes_accessed=16 * 10**6, transcendentals=0
        ),
        name="inner",
    )(electrodes, own, core, chip)


def edge_kernel(
    elec_ref, a_ref, b_ref, a_corner, b_corner, wide_ref, band_ref, side_ref, first_gram,
    s_hbm, pay_ref, halo, v0, v1, v2, e0, e1, s_ref, gram, cx, cy, cu, cd, cr, px, py, pu, pd, pr, out_sems,
):
    gx = lax.axis_index("gx")
    mask_x, mask_y = grid_masks()
    ids = electrode_ids(elec_ref)

    def x_of(l):
        return l - 4 if l < 10 else l

    def place(ref, corner, first):
        for dx in range(1, HALO + 1):
            k = first + dx - 1
            halo[k, 64:192, :] = ref[dx - 1, 0:128, :]
            halo[k, 256:272, :] = ref[dx - 1, 128:144, :]
        for dx, rows, at in CORNERS:
            k = first + dx - 1
            halo[k, 64 - rows : 64, :] = corner[at : at + rows, :]
            halo[k, 192 : 192 + rows, :] = corner[at + rows : at + 2 * rows, :]
            halo[k, 272:288, :] = corner[at + 2 * rows : at + 2 * rows + 16, :]

    @pl.when(odd("gx"))
    def _():
        place(a_ref, a_corner, 0)
        place(b_ref, b_corner, HALO)

    @pl.when(jnp.logical_not(odd("gx")))
    def _():
        place(b_ref, b_corner, 0)
        place(a_ref, a_corner, HALO)

    def plane_of(l):
        x = x_of(l)
        if 0 <= x < 16:
            return wide_ref, x if x < 6 else x - 4
        return halo, (-x - 1 if x < 0 else HALO + x - 16)

    def coeff_rows(l):
        ref, k = plane_of(l)
        return tuple(ref[k, a:b, :] for a, b in ((256, 272), (272, 280), (280, 288)))

    def background(l, y):
        ref, k = plane_of(l)
        return ref[k, tile_at(y), :]

    def banded(ref, first, at):
        def get(l, y):
            x = x_of(l)
            for k, start in enumerate((first, 14 - first)):
                if x in (start, start + 1):
                    return band_ref[at + 2 * k + x - start, tile_at(y), :]
            return ref[l, tile_at(y), :]

        return get

    def keep_of(l):
        x = x_of(l)
        i = x + 1 if l < 10 else x - 7
        if x in (-1, 16):
            return i, (4, 12)
        if -1 < x < 4 or 11 < x < 16:
            return i, (3, 13)
        return 0, (99, 99)

    for i in range(3):
        rows = 96 - 32 * (2 - i)
        s_ref[2 + i, 0:rows, :] = side_ref[i, 0:rows, :]
        s_ref[7 - i, 0:rows, :] = side_ref[5 - i, 0:rows, :]
    for l in list(range(2, 10)) + list(range(10, 18)):
        i, keep = keep_of(l)
        unit_plane(ids, gx * 16 + x_of(l), e0, l, s_ref, i, keep)
    ccoef, pcoef = (cx, cy, cu, cd, cr), (px, py, pu, pd, pr)
    faces(coeff_rows, list(range(9)) + list(range(10, 19)), ccoef, pcoef)

    def sweep(get, dst, coeffs, reach, planes, row, rows_kept=None):
        for l in planes:
            x = x_of(l)
            out_by = max(0, -x, x - 15)
            mask = mask_x[0] if x < 0 else mask_x[1] if x > 15 else None
            i, keep = keep_of(l)
            keep = rows_kept or keep

            def emit(y, out, l=l, i=i, keep=keep):
                if dst is not None:
                    dst[l, tile_at(y), :] = out
                if keep[0] <= y < keep[1]:
                    put_split(s_ref, i, row, y, out)

            near = reach - out_by
            stencil_plane(get, coeffs, l, 4 - near, 12 + near, mask, mask_y, emit)

    def sides(low, count):
        return [x + 4 for x in range(low, low + count)] + [15 - x for x in range(low, low + count)]

    sweep(background, v0, pcoef, 3, sides(-3, 4), V0)
    sweep(banded(v0, 1, 0), v1, ccoef, 2, sides(-2, 4), V1)
    sweep(banded(v1, 2, 4), v2, ccoef, 1, sides(-1, 4), V2)
    sweep(tiles(e0), e1, ccoef, 1, sides(-1, 6), E1)
    outs = run_copies([(s_ref.at[:, pl.ds(0, KEPT)], s_hbm)], out_sems)
    sweep(banded(v2, 3, 8), None, ccoef, 0, sides(0, 4), V3, (4, 12))
    sweep(tiles(e1), None, ccoef, 0, sides(0, 4), E2, (4, 12))

    gram[...] = first_gram[...]

    def gram_step(i, carry):
        gram[...] += gram_of(s_ref, i)
        return carry

    lax.fori_loop(1, 9, gram_step, 0, unroll=8)

    def rows_of(row):
        if row == E0:
            return gram[row : row + F, :]
        return gram[row : row + F, :] + gram[row + F : row + 2 * F, :]

    summed = {row: rows_of(row) for row in (V0, V1, V2, E0, E1)}

    def block(row, col):
        rows = summed[row]
        if col == E0:
            return rows[:, col : col + F]
        return rows[:, col : col + F] + rows[:, col + F : col + 2 * F]

    order = [
        (V0, V0), (V0, V1), (V1, V1), (V1, V2), (V2, V2), (V2, V3), (V0, E0), (V1, E0),
        (V2, E0), (E0, V3), (E1, V3), (E0, E0), (E0, E1), (E1, E1), (E1, E2),
    ]
    blocks = [block(r, c) for r, c in order] + [jnp.zeros((F, F), jnp.float32)]
    pay_ref[0:16, :] = jnp.concatenate(blocks[:8], axis=1)
    pay_ref[16:32, :] = jnp.concatenate(blocks[8:], axis=1)
    wait_all(outs)


def edge(electrodes, a, b, a_corner, b_corner, wide, band, side, gram):
    vmem = pl.BlockSpec(memory_space=pltpu.VMEM)
    field = pltpu.VMEM((20, 256, LANES), jnp.float32)
    coeff = pltpu.VMEM((20, 16, LANES), jnp.float32)
    return pl.pallas_call(
        edge_kernel,
        out_shape=(
            pltpu.HBM((10, KEPT, WIDE), jnp.bfloat16),
            jax.ShapeDtypeStruct((32, LANES), jnp.float32),
        ),
        in_specs=[pl.BlockSpec(memory_space=pltpu.SMEM)] + [vmem] * 8,
        out_specs=(pl.BlockSpec(memory_space=pltpu.HBM), vmem),
        scratch_shapes=[pltpu.VMEM((2 * HALO, 288, LANES), jnp.float32)]
        + [field] * 5
        + [
            pltpu.VMEM((10, ALL_ROWS, WIDE), jnp.bfloat16),
            pltpu.VMEM((KEPT, ALL_ROWS), jnp.float32),
        ]
        + [coeff] * 10
        + [pltpu.SemaphoreType.DMA((1,))],
        compiler_params=pltpu.CompilerParams(vmem_limit_bytes=36 * MB),
        name="edge",
    )(electrodes, a, b, a_corner, b_corner, wide, band, side, gram)


def matmul(a, b, dims=((1,), (0,))):
    return lax.dot_general(
        a, b, (dims, ((), ())), precision=HIGHEST, preferred_element_type=jnp.float32
    )


def galerkin(m0, m1, m2, m3):
    a12 = m2 + SHIFT * m1
    work = jnp.concatenate(
        [
            jnp.concatenate([m1 + SHIFT * m0, a12, m0], axis=1),
            jnp.concatenate([a12, m3 + SHIFT * m2, m1], axis=1),
        ],
        axis=0,
    )
    work = jnp.concatenate([work, jnp.zeros((2 * F, LANES - 3 * F), jnp.float32)], axis=1)
    return eliminate(work)[:, 2 * F : 3 * F]


def eliminate(work, size=8):
    count = work.shape[0]
    sub = lax.broadcasted_iota(jnp.int32, work.shape, 0)

    def column(k):
        return jnp.take_along_axis(work, jnp.full(work.shape, k, jnp.int32), axis=1)

    def row(v, k):
        return jnp.broadcast_to(v[k : k + 1, :], (8, LANES))

    def tall(v):
        return jnp.concatenate([v] * (count // 8), axis=0)

    for k in range(0, count, size):
        cols = [column(k + j) for j in range(size)]
        rows = [row(work, k + i) for i in range(size)]
        p = [[row(cols[j], k + i) for j in range(size)] for i in range(size)]
        for s in range(0, size, 2):
            a, b, c, d = p[s][s], p[s][s + 1], p[s + 1][s], p[s + 1][s + 1]
            inverse = 1.0 / (a * d - b * c)
            a, b, c, d = d * inverse, -(b * inverse), -(c * inverse), a * inverse
            rows[s], rows[s + 1] = a * rows[s] + b * rows[s + 1], c * rows[s] + d * rows[s + 1]
            for j in range(s + 2, size):
                u, v = p[s][j], p[s + 1][j]
                p[s][j], p[s + 1][j] = a * u + b * v, c * u + d * v
            for i in range(size):
                if i in (s, s + 1):
                    continue
                u, v = p[i][s], p[i][s + 1]
                rows[i] = rows[i] - u * rows[s] - v * rows[s + 1]
                for j in range(s + 2, size):
                    p[i][j] = p[i][j] - u * p[s][j] - v * p[s + 1][j]
        for j in range(size):
            work = work - cols[j] * tall(rows[j])
        for j in range(size):
            work = jnp.where(sub == k + j, tall(rows[j]), work)
    return work


def final_kernel(
    pattern_ref, parts_ref, own_ref, core_ref, chip_ref, a_ref, b_ref, mid_hbm, edge_hbm,
    out_ref, sens_ref, bg, adj, s_ref, mix_ref, sems, *, damping,
):
    odd_y = odd("gy")

    def y_rows(is_left):
        src = pl.multiple_of(jnp.where(is_left, 48, 0), 8)
        dst = pl.multiple_of(jnp.where(is_left, 0, 144), 8)
        return pl.ds(src, 16), pl.ds(dst, 16)

    planes = pl.ds(1, 16)
    core_src, core_dst = y_rows(odd_y)
    chip_src, chip_dst = y_rows(jnp.logical_not(odd_y))
    near = pl.ds(0, 128)
    odd_x = odd("gx")
    pairs = [
        (edge_hbm.at[pl.ds(0, 5)], s_ref.at[pl.ds(0, 5)]),
        (mid_hbm, s_ref.at[pl.ds(5, 8)]),
        (edge_hbm.at[pl.ds(5, 5)], s_ref.at[pl.ds(13, 5)]),
        (own_ref.at[:, pl.ds(0, 128)], bg.at[planes, pl.ds(16, 128)]),
        (core_ref.at[:, core_src], bg.at[planes, core_dst]),
        (chip_ref.at[:, chip_src], bg.at[planes, chip_dst]),
        (a_ref.at[0, near], bg.at[jnp.where(odd_x, 0, 17), pl.ds(16, 128)]),
        (b_ref.at[0, near], bg.at[jnp.where(odd_x, 17, 0), pl.ds(16, 128)]),
    ]
    copies = [pltpu.make_async_copy(s, d, sems.at[i]) for i, (s, d) in enumerate(pairs)]

    @pl.when(lax.axis_index("gx") >= 0)
    def _():
        for c in copies:
            c.start()

    total = jnp.sum(parts_ref[...], axis=0)

    def part(k):
        r, c = (k // 8) * F, (k % 8) * F
        return total[r : r + F, c : c + F]

    m = [part(k) for k in range(6)]
    p = [part(6), part(7), part(8), part(9).T, part(10).T]
    e = [part(k) for k in range(11, 15)]
    y = galerkin(*m[:4])

    lane = lax.broadcasted_iota(jnp.int32, (F, F), 1)
    sub = lax.broadcasted_iota(jnp.int32, (F, F), 0)
    first, second = jnp.zeros((F, F), jnp.int32), jnp.zeros((F, F), jnp.int32)
    for i in range(F):
        first = jnp.where(sub == i, pattern_ref[i, 0], first)
        second = jnp.where(sub == i, pattern_ref[i, 1], second)
    pairing = jnp.where(lane == first, 1.0, 0.0) - jnp.where(lane == second, 1.0, 0.0)
    w = matmul(8.0 * matmul(pairing, pairing, ((0,), (0,))), jnp.concatenate(p[:2], axis=0), ((1,), (1,)))
    forms = []
    for k in range(4):
        inside = jnp.concatenate(
            [
                jnp.concatenate([m[k], m[k + 1]], axis=1),
                jnp.concatenate([m[k + 1], m[k + 2]], axis=1),
            ],
            axis=0,
        )
        across = matmul(jnp.concatenate([p[k], p[k + 1]], axis=0), w)
        local = matmul(w, matmul(e[k], w), ((0,), (0,)))
        forms.append(damping * (damping * inside + across + across.T) + local)
    hy = matmul(jnp.concatenate(forms, axis=0), y)
    moments = [matmul(y, hy[32 * k : 32 * (k + 1)], ((0,), (0,))) for k in range(4)]
    z = jnp.concatenate([damping * y, matmul(w, y)], axis=0)
    q = galerkin(*moments)
    z0, z1 = matmul(z, q[0:F]), matmul(z, q[F:])
    none = jnp.zeros((F, F), jnp.float32)
    mix = [
        jnp.concatenate([y[0:F], z0[0:F]], axis=1),
        jnp.concatenate([y[F:], z0[F : 2 * F] + z1[0:F]], axis=1),
        jnp.concatenate([none, z1[F : 2 * F]], axis=1),
        jnp.concatenate([none, z0[2 * F :]], axis=1),
        jnp.concatenate([none, z1[2 * F :]], axis=1),
    ]
    mix = [mix[i] for i in (0, 0, 1, 1, 2, 2, 3, 4, 4)]
    mix = jnp.concatenate(mix, axis=0).T
    hi = mix.astype(jnp.bfloat16)
    mix_ref[0:32, :] = hi
    mix_ref[32:64, :] = (mix - hi.astype(jnp.float32)).astype(jnp.bfloat16)
    wait_all(copies)
    both = mix_ref[...]

    def combine(x, lanes):
        out = jnp.dot(both, s_ref[x, :, lanes], preferred_element_type=jnp.float32)
        return out[0:32] + out[32:64]

    def store(x, out):
        for k in range(10):
            cols = slice(k * LANES, (k + 1) * LANES)
            if 0 < k < 9:
                out_ref[pl.ds(x * 8 + k - 9, F, stride=128), :] = out[0:F, cols]
            adj[x, tile_at(k), :] = out[F:, cols]

    def store_end(x, out):
        for k in range(8):
            adj[x, tile_at(k + 1), :] = out[F:, k * LANES : (k + 1) * LANES]

    lane = lane_ids(F)

    def sens_plane(x):
        b, a = bg[x, tile_at(1), :], adj[x, tile_at(1), :]
        before = (b - bg[x, tile_at(0), :]) * (a - adj[x, tile_at(0), :])
        for k in range(1, 9):
            bn, an = bg[x, tile_at(k + 1), :], adj[x, tile_at(k + 1), :]
            after = (bn - b) * (an - a)
            total = before + after
            for s in (x - 1, x + 1):
                total = total + (bg[s, tile_at(k), :] - b) * (adj[s, tile_at(k), :] - a)
            bu = jnp.where(lane == LANES - 1, 0.0, pltpu.roll(b, LANES - 1, 1))
            au = jnp.where(lane == LANES - 1, 0.0, pltpu.roll(a, LANES - 1, 1))
            bd = jnp.where(lane == 0, 0.0, pltpu.roll(b, 1, 1))
            ad = jnp.where(lane == 0, 0.0, pltpu.roll(a, 1, 1))
            total = total + (bu - b) * (au - a) + (bd - b) * (ad - a)
            sens_ref[x - 1, k - 1 : k, :] = -0.5 * jnp.sum(total, axis=0, keepdims=True)
            before, b, a = after, bn, an

    ends = slice(LANES, 9 * LANES)
    store_end(0, combine(0, ends))
    store(1, combine(1, slice(0, WIDE)))
    store(2, combine(2, slice(0, WIDE)))

    def plane(x, carry):
        out = combine(x + 2, slice(0, WIDE))
        sens_plane(x)
        store(x + 2, out)
        return carry

    lax.fori_loop(1, 15, plane, 0, unroll=2)
    out = combine(17, ends)
    sens_plane(15)
    store_end(17, out)
    sens_plane(16)


def final(pattern, parts, own, core, chip, a, b, mid, edges, damping):
    anywhere = pl.BlockSpec(memory_space=pl.ANY)
    vmem = pl.BlockSpec(memory_space=pltpu.VMEM)
    hbm = pl.BlockSpec(memory_space=pltpu.HBM)

    def kernel(*refs):
        final_kernel(*refs, damping=damping)

    return pl.pallas_call(
        kernel,
        out_shape=(
            jax.ShapeDtypeStruct((2048, LANES), jnp.float32),
            jax.ShapeDtypeStruct((16, 8, LANES), jnp.float32),
        ),
        in_specs=[pl.BlockSpec(memory_space=pltpu.SMEM), vmem] + [anywhere] * 5 + [hbm] * 2,
        scratch_shapes=[
            pltpu.VMEM((18, 160, LANES), jnp.float32),
            pltpu.VMEM((18, 160, LANES), jnp.float32),
            pltpu.VMEM((18, KEPT, WIDE), jnp.bfloat16),
            pltpu.VMEM((64, KEPT), jnp.bfloat16),
            pltpu.SemaphoreType.DMA((8,)),
        ],
        compiler_params=pltpu.CompilerParams(vmem_limit_bytes=56 * MB),
        name="final",
    )(pattern, parts, own, core, chip, a, b, mid, edges)


def spread(block, axis, count, groups=None):
    copies = jnp.broadcast_to(block[None], (count,) + block.shape)
    return lax.all_to_all(copies, axis, 0, 0, axis_index_groups=groups)


def swaps(first, count):
    lows = range(first, count - 1, 2)
    return [(i, i + 1) for i in lows] + [(i + 1, i) for i in lows]


def on_device(background, conductivity, perturbation, electrodes, pattern):
    size_x, size_y, size_z = conductivity.shape
    count_x, count_y = lax.axis_size("gx"), lax.axis_size("gy")
    own, core, chip, a, b = pack(background, conductivity, perturbation)
    a = lax.ppermute(a, "gx", swaps(0, count_x))
    b = lax.ppermute(b, "gx", swaps(1, count_x))
    chip = lax.ppermute(chip, "gy", swaps(1, count_y))
    core = lax.ppermute(core, "gy", swaps(0, count_y))
    a_corner, b_corner = pack_x(core, chip)
    a_corner = lax.ppermute(a_corner, "gx", swaps(0, count_x))
    b_corner = lax.ppermute(b_corner, "gx", swaps(1, count_x))
    mid, wide, band, side, gram = inner(electrodes, own, core, chip)
    edges, pay = edge(electrodes, a, b, a_corner, b_corner, wide, band, side, gram)
    pay = pay + lax.ppermute(pay, "gy", swaps(0, count_y))
    pay = jnp.sum(spread(pay, "gx", count_x), axis=0)
    chips = count_y // 2
    groups = [[2 * i + c for i in range(chips)] for c in range(2)]
    parts = spread(pay, "gy", chips, groups)
    cells = size_x * size_y * size_z * count_x * count_y
    damping = 80.0 / math.sqrt(cells)
    tangent, sens = final(pattern, parts, own, core, chip, a, b, mid, edges, damping)
    return tangent.reshape(background.shape), sens


def solution(mesh):
    in_specs = (P(None, "gx", "gy", None), P("gx", "gy", None), P("gx", "gy", None), P(), P())
    out_specs = (P(None, "gx", "gy", None), P("gx", "gy", None))
    return jax.shard_map(
        on_device, mesh=mesh, in_specs=in_specs, out_specs=out_specs, check_vma=False
    )
```

time: 99.4 us -> 80.8 us (0.81)
  Pallas kernels: 39.8 us -> 27.7 us
  local copies, waits for them, and re-layouts: 8.45 us -> 2.16 us
  starting transfers between devices: 14.3 us -> 16.9 us
  blocking collectives: 20.4 us -> 18.5 us
  waiting for transfers between devices: 15.2 us -> 14.1 us
    pallas_call x1, Pallas kernels: 17.1 us -> 10.5 us  [final(): pl.pallas_call(kernel, out_shape=(jax.ShapeDtypeStruct((2048, LANES), jnp...]
    pallas_call x3, Pallas kernels: 21.8 us -> 15.4 us  [the longest x1 9.18 us: inner(): pl.pallas_call(inner_kernel, out_shape=(pltpu.HBM((8, KEPT, WIDE), jnp.bf...]
    unnamed x27 -> x17, local copies, waits for them, and re-layouts: 7.71 us -> 1.42 us
    ppermute x0 -> x2, starting transfers between devices: none -> 2.03 us  [the longest x1 1.38 us: on_device(): a_corner = lax.ppermute(a_corner, 'gx', swaps(0, count_x))]
    all_to_all x1, blocking collectives: 20.4 us -> 18.5 us  [spread(): return lax.all_to_all(copies, axis, 0, 0, axis_index_groups=groups)]
    all_to_all x1, starting transfers between devices: 7.64 us -> 8.99 us  [spread(): return lax.all_to_all(copies, axis, 0, 0, axis_index_groups=groups)]
    ppermute x1, starting transfers between devices: 1.38 us -> 0.27 us  [on_device(): a = lax.ppermute(a, 'gx', swaps(0, count_x))]
  transfers between devices with their start and end apart: 6 -> 8, of which waited for: 3 -> 3; matrix products, arithmetic and copies ran while one was open for 1% -> 1% of each run, Pallas kernels for 10% -> 11%
where the time goes in v3:
time: 80.8 us; the launch traced here: 80.4 us
  Pallas kernels  27.7 us (34%)
  blocking collectives  18.5 us (23%)
  starting transfers between devices  16.9 us (21%)
  waiting for transfers between devices  14.1 us (17%)
  local copies, waits for them, and re-layouts  2.16 us (3%)
  between operations  1 us (1%)
    all_to_all x1, blocking collectives, spread(): return lax.all_to_all(copies, axis, 0, 0, axis_index_groups=groups)  18.5 us
    pallas_call x1, Pallas kernels, final(): pl.pallas_call(kernel, out_shape=(jax.ShapeDtypeStruct((2048, LANES), jnp...  10.5 us
    pallas_call x1, Pallas kernels, inner(): pl.pallas_call(inner_kernel, out_shape=(pltpu.HBM((8, KEPT, WIDE), jnp.bf...  9.18 us
    all_to_all x1, starting transfers between devices, spread(): return lax.all_to_all(copies, axis, 0, 0, axis_index_groups=groups)  8.99 us
    all_to_all x1, waiting for transfers between devices, spread(): return lax.all_to_all(copies, axis, 0, 0, axis_index_groups=groups)  6.65 us
    ppermute x1, waiting for transfers between devices, on_device(): chip = lax.ppermute(chip, 'gy', swaps(1, count_y))  6.59 us
    pallas_call x1, Pallas kernels, edge(): pl.pallas_call(edge_kernel, out_shape=(pltpu.HBM((10, KEPT, WIDE), jnp.bf...  6.24 us
    ppermute x1, starting transfers between devices, on_device(): chip = lax.ppermute(chip, 'gy', swaps(1, count_y))  4.27 us
  transfers between devices with their start and end apart: 8, of which 3 were waited for; matrix products, arithmetic and copies ran while one was open for 1% of the time, Pallas kernels for 11%

profile of v3, /device:TPU:2, one launch (start us, length us, event | category | flops | bytes accessed | tf_op | source)
XLA Modules:
  0.0 80.4 jit_solution(280881986495981012)
XLA Ops:
  0.6 0.0 copy-start.5
  0.6 1.8 %pack_y.1 = (f32[16,144,128]{2,1,0:T(8,128)S(1)}, f32[16,72,128]{2,1,0:T(8,128)S(1)}, f32[16,72,128]{2,1,0:T(8,128)S(1)}, f32[4,144,128]{2,1,0:T(8,128)S(1)}, f32[4,144,128]{2,1,0:T(8,128)S(1)}) custom-call(f32[16,16,8,128]{3,2,1,0:T(8,128)} %bg_hbm.1, f32[16,8,128]{2,1,0:T(8,128)} %cond_hbm.1, f32[16,8,128]{2,1,0:T(8,128)} %pert_hbm.1), custom_call_target="tpu_custom_call" | custom-call | tf_op jit(solution)/shard_map/pack_y/pallas_call | solution.py:99
  2.4 0.0 copy-start.4
  2.4 0.1 collective-permute-start.2
  2.5 4.3 %collective-permute-start.3 = (f32[16,72,128]{2,1,0:T(8,128)S(1)}, f32[16,72,128]{2,1,0:T(8,128)S(1)}, u32[]{:S(2)}, u32[]{:S(2)}) collective-permute-start(f32[16,72,128]{2,1,0:T(8,128)S(1)} %get-tuple-element.21), channel_id=1, source_target_pairs={{1,2},{3,4},{5,6},{7,8},{9,10},{11,12},{13,14},{15,16},{17,18},{19... | collective-permute-start | bytes 1769480 | tf_op jit(solution)/shard_map/ppermute | solution.py:781
  6.8 0.3 collective-permute-start
  7.1 0.7 collective-permute-start.1
  7.7 0.0 collective-permute-done.2.core_ref.refs_3_
  7.7 0.0 copy-start
  7.8 6.6 %collective-permute-done.3.chip_ref.refs_4_ = f32[16,72,128]{2,1,0:T(8,128)S(1)} collective-permute-done((f32[16,72,128]{2,1,0:T(8,128)S(1)}, f32[16,72,128]{2,1,0:T(8,128)S(1)}, u32[]{:S(2)}, u32[]{:S(2)}) %collective-permute-start.3) | collective-permute-done | bytes 589856 | tf_op jit(solution)/shard_map/ppermute | solution.py:781
  14.3 0.0 copy-start.1
  14.4 1.4 %collective-permute-start.4 = (f32[240,128]{1,0:T(8,128)S(1)}, f32[240,128]{1,0:T(8,128)S(1)}, u32[]{:S(2)}, u32[]{:S(2)}) collective-permute-start(f32[240,128]{1,0:T(8,128)S(1)} %get-tuple-element.22), channel_id=1, source_target_pairs={{0,32},{64,96},{128,160},{192,224},{32,0},{96,64},{160,128},{224,1... | collective-permute-start | bytes 368648 | tf_op jit(solution)/shard_map/ppermute | solution.py:784
  15.7 0.7 collective-permute-start.5
  16.4 0.0 copy-done.5
  16.4 9.2 %inner.1 = (bf16[8,144,1280]{2,1,0:T(8,128)(2,1)}, f32[12,288,128]{2,1,0:T(8,128)S(1)}, f32[12,256,128]{2,1,0:T(8,128)S(1)}, bf16[6,96,1280]{2,1,0:T(8,128)(2,1)S(1)}, f32[144,208]{1,0:T(8,128)S(1)}) custom-call(s32[16]{0:T(128)S(1)} %copy-done.5, f32[16,144,128]{2,1,0:T(8,128)S(1)} %get-tuple-element.24.own_ref.refs_2_, ...), custom_call_target="tpu_custom_call" | custom-call | flops 4000000000 | bytes 16000000 | tf_op jit(solution)/shard_map/inner/pallas_call | solution.py:360
  25.6 0.0 copy-done.4
  25.6 0.0 copy-done
  25.6 0.0 copy-done.1
  25.6 0.0 collective-permute-done.a_ref.refs_5_
  25.6 0.0 copy-start.2
  25.7 0.0 collective-permute-done.1.b_ref.refs_6_
  25.7 0.0 copy-start.3
  25.7 0.0 collective-permute-done.4.a_corner
  25.7 0.0 collective-permute-done.5.b_corner
  25.7 0.0 copy-start.7
  25.7 6.2 %edge.1 = (bf16[10,144,1280]{2,1,0:T(8,128)(2,1)}, f32[32,128]{1,0:T(8,128)S(1)}) custom-call(s32[16]{0:T(128)S(1)} %copy-done.5, f32[4,144,128]{2,1,0:T(8,128)S(1)} %collective-permute-done.a_ref.refs_5_, f32[4,144,128]{2,1,0:T(8,128)S(1)} %collective-permute-done.1.b_ref.refs_6_, f32[240,128]{1,0:T(8,128)S(1)} %collective-permute-done.4.a_corner, ...), custom_call_target="tpu_custom_call" | custom-call | tf_op jit(solution)/shard_map/edge/pallas_call | solution.py:522
  32.0 0.0 copy-done.2
  32.0 0.0 copy-done.3
  32.0 0.6 collective-permute-start.6
  32.6 0.8 %collective-permute-done.6 = f32[32,128]{1,0:T(8,128)S(1)} collective-permute-done((f32[32,128]{1,0:T(8,128)S(1)}, f32[32,128]{1,0:T(8,128)S(1)}, u32[]{:S(2)}, u32[]{:S(2)}) %collective-permute-start.6) | collective-permute-done | bytes 16416 | tf_op jit(solution)/shard_map/ppermute | solution.py:788
  33.4 18.5 %all_to_all.10 = f32[8,32,128]{2,1,0:T(8,128)S(1)} all-to-all(f32[8,32,128]{2,1,0:T(8,128)S(1)} %broadcast_in_dim.4), channel_id=1, replica_groups=mesh['gx'=8,'gy'=32] {'gx'}, dimensions={0} | all-to-all | bytes 262144 | tf_op jit(solution)/shard_map/all_to_all | solution.py:767
  52.0 0.7 broadcast_in_dim.5
  52.7 9.0 %all-to-all-start.1 = ((f32[16,32,128]{2,1,0:T(8,128)}), f32[16,32,128]{2,1,0:T(8,128)S(1)}, u32[]{:S(2)}, u32[]{:S(2)}) async-start(f32[16,32,128]{2,1,0:T(8,128)} %broadcast_in_dim.5), calls=%async_computation.1 | async-start | bytes 524288 | tf_op jit(solution)/shard_map/all_to_all | solution.py:767
  61.7 0.0 copy-done.7
  61.7 0.7 copy.8.refs_0_
  62.4 6.7 %all-to-all-done.1.refs_1_ = f32[16,32,128]{2,1,0:T(8,128)S(1)} async-done(((f32[16,32,128]{2,1,0:T(8,128)}), f32[16,32,128]{2,1,0:T(8,128)S(1)}, u32[]{:S(2)}, u32[]{:S(2)}) %all-to-all-start.1) | async-done | bytes 262176 | tf_op jit(solution)/shard_map/all_to_all | solution.py:767
  69.0 0.0 copy-start.6
  69.0 0.7 copy-done.6
  69.7 10.5 %final.1 = (f32[2048,128]{1,0:T(8,128)}, f32[16,8,128]{2,1,0:T(8,128)}) custom-call(s32[16,2]{1,0:T(8,128)} %copy.8.refs_0_, f32[16,32,128]{2,1,0:T(8,128)} %copy-done.6, f32[16,144,128]{2,1,0:T(8,128)} %copy-done.4, f32[16,72,128]{2,1,0:T(8,128)} %copy-done, f32[16,72,128]{2,1,0:T(8,128)} %copy-done.1, f32[4,144,128]{2,1,0:T(8,128)} %copy-done.2, ...), custom_call_target="tpu_custom_call" | custom-call | tf_op jit(solution)/shard_map/final/pallas_call | solution.py:746
  (4 shorter events, 0.0 us)
Async XLA Ops:
  0.6 15.8 %copy-start.5 = (s32[16]{0:T(128)S(1)}, s32[16]{0:T(128)}, u32[]{:S(2)}) copy-start(s32[16]{0:T(128)} %elec_ref.3) | copy-start | bytes 196
  2.4 23.2 %copy-start.4 = (f32[16,144,128]{2,1,0:T(8,128)}, f32[16,144,128]{2,1,0:T(8,128)S(1)}, u32[]{:S(2)}) copy-start(f32[16,144,128]{2,1,0:T(8,128)S(1)} %get-tuple-element.24.own_ref.refs_2_) | copy-start | bytes 3538948
  2.4 5.3 %collective-permute-start.2 = (f32[16,72,128]{2,1,0:T(8,128)S(1)}, f32[16,72,128]{2,1,0:T(8,128)S(1)}, u32[]{:S(2)}, u32[]{:S(2)}) collective-permute-start(f32[16,72,128]{2,1,0:T(8,128)S(1)} %get-tuple-element.20), channel_id=1, source_target_pairs={{0,1},{2,3},{4,5},{6,7},{8,9},{10,11},{12,13},{14,15},{16,17},{18,... | collective-permute-start | bytes 1769480 | tf_op jit(solution)/shard_map/ppermute | solution.py:782
  2.5 11.8 %collective-permute-start.3 = (f32[16,72,128]{2,1,0:T(8,128)S(1)}, f32[16,72,128]{2,1,0:T(8,128)S(1)}, u32[]{:S(2)}, u32[]{:S(2)}) collective-permute-start(f32[16,72,128]{2,1,0:T(8,128)S(1)} %get-tuple-element.21), channel_id=1, source_target_pairs={{1,2},{3,4},{5,6},{7,8},{9,10},{11,12},{13,14},{15,16},{17,18},{19... | collective-permute-start | bytes 1769480 | tf_op jit(solution)/shard_map/ppermute | solution.py:781
  6.8 18.8 %collective-permute-start = (f32[4,144,128]{2,1,0:T(8,128)S(1)}, f32[4,144,128]{2,1,0:T(8,128)S(1)}, u32[]{:S(2)}, u32[]{:S(2)}) collective-permute-start(f32[4,144,128]{2,1,0:T(8,128)S(1)} %get-tuple-element.18), channel_id=1, source_target_pairs={{0,32},{64,96},{128,160},{192,224},{32,0},{96,64},{160,128},{224,1... | collective-permute-start | bytes 884744 | tf_op jit(solution)/shard_map/ppermute | solution.py:779
  7.1 18.6 %collective-permute-start.1 = (f32[4,144,128]{2,1,0:T(8,128)S(1)}, f32[4,144,128]{2,1,0:T(8,128)S(1)}, u32[]{:S(2)}, u32[]{:S(2)}) collective-permute-start(f32[4,144,128]{2,1,0:T(8,128)S(1)} %get-tuple-element.19), channel_id=1, source_target_pairs={{32,64},{96,128},{160,192},{64,32},{128,96},{192,160},{33,65},{97,... | collective-permute-start | bytes 884744 | tf_op jit(solution)/shard_map/ppermute | solution.py:780
  7.7 17.9 %copy-start = (f32[16,72,128]{2,1,0:T(8,128)}, f32[16,72,128]{2,1,0:T(8,128)S(1)}, u32[]{:S(2)}) copy-start(f32[16,72,128]{2,1,0:T(8,128)S(1)} %collective-permute-done.2.core_ref.refs_3_) | copy-start | bytes 1769476
  14.3 11.3 %copy-start.1 = (f32[16,72,128]{2,1,0:T(8,128)}, f32[16,72,128]{2,1,0:T(8,128)S(1)}, u32[]{:S(2)}) copy-start(f32[16,72,128]{2,1,0:T(8,128)S(1)} %collective-permute-done.3.chip_ref.refs_4_) | copy-start | bytes 1769476
  14.4 11.3 %collective-permute-start.4 = (f32[240,128]{1,0:T(8,128)S(1)}, f32[240,128]{1,0:T(8,128)S(1)}, u32[]{:S(2)}, u32[]{:S(2)}) collective-permute-start(f32[240,128]{1,0:T(8,128)S(1)} %get-tuple-element.22), channel_id=1, source_target_pairs={{0,32},{64,96},{128,160},{192,224},{32,0},{96,64},{160,128},{224,1... | collective-permute-start | bytes 368648 | tf_op jit(solution)/shard_map/ppermute | solution.py:784
  15.7 9.9 %collective-permute-start.5 = (f32[240,128]{1,0:T(8,128)S(1)}, f32[240,128]{1,0:T(8,128)S(1)}, u32[]{:S(2)}, u32[]{:S(2)}) collective-permute-start(f32[240,128]{1,0:T(8,128)S(1)} %get-tuple-element.23), channel_id=1, source_target_pairs={{32,64},{96,128},{160,192},{64,32},{128,96},{192,160},{33,65},{97,... | collective-permute-start | bytes 368648 | tf_op jit(solution)/shard_map/ppermute | solution.py:785
  25.6 6.3 %copy-start.2 = (f32[4,144,128]{2,1,0:T(8,128)}, f32[4,144,128]{2,1,0:T(8,128)S(1)}, u32[]{:S(2)}) copy-start(f32[4,144,128]{2,1,0:T(8,128)S(1)} %collective-permute-done.a_ref.refs_5_) | copy-start | bytes 884740
  25.7 6.3 %copy-start.3 = (f32[4,144,128]{2,1,0:T(8,128)}, f32[4,144,128]{2,1,0:T(8,128)S(1)}, u32[]{:S(2)}) copy-start(f32[4,144,128]{2,1,0:T(8,128)S(1)} %collective-permute-done.1.b_ref.refs_6_) | copy-start | bytes 884740
  25.7 36.0 %copy-start.7 = (s32[16,2]{0,1:T(2,128)S(1)}, s32[16,2]{0,1:T(2,128)}, u32[]{:S(2)}) copy-start(s32[16,2]{0,1:T(2,128)} %param.9) | copy-start | bytes 388
  32.0 1.4 %collective-permute-start.6 = (f32[32,128]{1,0:T(8,128)S(1)}, f32[32,128]{1,0:T(8,128)S(1)}, u32[]{:S(2)}, u32[]{:S(2)}) collective-permute-start(f32[32,128]{1,0:T(8,128)S(1)} %get-tuple-element.29), channel_id=1, source_target_pairs={{0,1},{2,3},{4,5},{6,7},{8,9},{10,11},{12,13},{14,15},{16,17},{18,... | collective-permute-start | bytes 49160 | tf_op jit(solution)/shard_map/ppermute | solution.py:788
  52.7 16.3 %all-to-all-start.1 = ((f32[16,32,128]{2,1,0:T(8,128)}), f32[16,32,128]{2,1,0:T(8,128)S(1)}, u32[]{:S(2)}, u32[]{:S(2)}) async-start(f32[16,32,128]{2,1,0:T(8,128)} %broadcast_in_dim.5), calls=%async_computation.1 | async-start | bytes 524288 | tf_op jit(solution)/shard_map/all_to_all | solution.py:767
  69.0 0.7 copy-start.6

commit v4 on v3

v4 whole, which is shorter than its diff:
```python
import math

import jax
import jax.numpy as jnp
from jax import lax
from jax.experimental import pallas as pl
from jax.experimental.pallas import tpu as pltpu
from jax.sharding import PartitionSpec as P

SHIFT = 12.0
F = 16
LANES = 128
HALO = 4
HIGHEST = lax.Precision.HIGHEST
V0, V1, V2, E0, E1, V3, E2 = 0, 32, 64, 96, 112, 144, 176
KEPT, ALL_ROWS = 144, 208
WIDE = 10 * LANES
MB = 2**20


def tile_at(y):
    return slice(y * F, (y + 1) * F)


def run_copies(pairs, sems, first=0):
    copies = [
        pltpu.make_async_copy(s, d, sems.at[first + i]) for i, (s, d) in enumerate(pairs)
    ]
    for c in copies:
        c.start()
    return copies


def wait_all(copies):
    for c in copies:
        c.wait()


def odd(axis):
    return lax.rem(lax.axis_index(axis), 2) == 1


PARTS = 4


def pack_kernel(
    bg_hbm, cond_hbm, pert_hbm, elec_hbm, wide_ref, core_ref, chip_ref, a_ref, b_ref, ids_ref,
    bg, cond_v, pert_v, elec, sems,
):
    size_x, size_y = cond_v.shape[0], cond_v.shape[1]
    each = size_x // PARTS
    pairs = [(cond_hbm, cond_v), (pert_hbm, pert_v), (elec_hbm, elec)]
    for i in range(PARTS):
        planes = pl.ds(i * each, each)
        pairs.append((bg_hbm.at[:, planes], bg.at[:, planes]))
    copies = run_copies(pairs, sems)

    def fill(top_ref, bottom_ref):
        wait_all(copies[:3])

        def plane(x, carry):
            for y in range(size_y):
                tile = bg[:, x, y, :]
                wide_ref[x + HALO, tile_at(y + HALO), :] = tile
                if y >= size_y - HALO:
                    top_ref[x, tile_at(y - size_y + HALO), :] = tile
                if y < HALO:
                    bottom_ref[x, tile_at(y), :] = tile
            cond, pert = cond_v[x], pert_v[x]
            wide_ref[x + HALO, 256:264, :] = cond
            wide_ref[x + HALO, 264:272, :] = pert
            top_ref[x, 64:72, :] = jnp.concatenate([cond[4:8], pert[4:8]], axis=0)
            bottom_ref[x, 64:72, :] = jnp.concatenate([cond[0:4], pert[0:4]], axis=0)
            return carry

        for i in range(PARTS):
            copies[3 + i].wait()
            lax.fori_loop(i * each, (i + 1) * each, plane, 0, unroll=each)

    @pl.when(odd("gy"))
    def _():
        fill(chip_ref, core_ref)

    @pl.when(jnp.logical_not(odd("gy")))
    def _():
        fill(core_ref, chip_ref)

    sub = lax.broadcasted_iota(jnp.int32, (F, LANES), 0)
    ids = jnp.zeros((F, LANES), jnp.int32)
    for e in range(F):
        ids = jnp.where(sub == e, elec[e], ids)
    ids_ref[...] = ids - lane_ids(F)

    for out, up in ((a_ref, jnp.logical_not(odd("gx"))), (b_ref, odd("gx"))):
        for dx in range(1, HALO + 1):
            x = HALO + jnp.where(up, size_x - dx, dx - 1)
            out[dx - 1, 0:128, :] = wide_ref[x, 64:192, :]
            out[dx - 1, 128:144, :] = wide_ref[x, 256:272, :]


def pack(background, conductivity, perturbation, electrodes):
    shape = jax.ShapeDtypeStruct
    inputs = [
        pltpu.with_memory_space_constraint(v, pltpu.HBM)
        for v in (background, conductivity, perturbation, electrodes)
    ]
    return pl.pallas_call(
        pack_kernel,
        out_shape=(
            shape((24, 288, LANES), jnp.float32),
            shape((16, 72, LANES), jnp.float32),
            shape((16, 72, LANES), jnp.float32),
            shape((HALO, 144, LANES), jnp.float32),
            shape((HALO, 144, LANES), jnp.float32),
            shape((F, LANES), jnp.int32),
        ),
        in_specs=[pl.BlockSpec(memory_space=pltpu.HBM)] * 4,
        scratch_shapes=[
            pltpu.VMEM((16, 16, 8, LANES), jnp.float32),
            pltpu.VMEM((16, 8, LANES), jnp.float32),
            pltpu.VMEM((16, 8, LANES), jnp.float32),
            pltpu.SMEM((F,), jnp.int32),
            pltpu.SemaphoreType.DMA((3 + PARTS,)),
        ],
        compiler_params=pltpu.CompilerParams(vmem_limit_bytes=16 * MB),
        name="pack_y",
    )(*inputs)


def corner_layout():
    table, at = [], 0
    for dx in range(1, HALO):
        rows = (HALO - dx) * F
        table.append((dx, rows, at))
        at += 2 * rows + 16
    return table, at


CORNERS, CORNER_ROWS = corner_layout()


def pack_corners_kernel(core_ref, chip_ref, a_ref, b_ref):
    def send(left_ref, right_ref):
        for out, up in ((a_ref, jnp.logical_not(odd("gx"))), (b_ref, odd("gx"))):
            for dx, rows, at in CORNERS:
                x = jnp.where(up, left_ref.shape[0] - dx, dx - 1)
                out[at : at + rows, :] = left_ref[x, 64 - rows : 64, :]
                out[at + rows : at + 2 * rows, :] = right_ref[x, 0:rows, :]
                at += 2 * rows
                out[at : at + 8, :] = left_ref[x, 64:72, :]
                out[at + 8 : at + 16, :] = right_ref[x, 64:72, :]

    @pl.when(odd("gy"))
    def _():
        send(core_ref, chip_ref)

    @pl.when(jnp.logical_not(odd("gy")))
    def _():
        send(chip_ref, core_ref)


def pack_corners(core, chip):
    shape = jax.ShapeDtypeStruct((CORNER_ROWS, LANES), jnp.float32)
    return pl.pallas_call(
        pack_corners_kernel,
        out_shape=(shape, shape),
        compiler_params=pltpu.CompilerParams(vmem_limit_bytes=16 * MB),
        name="pack_corners",
    )(core, chip)


def lane_ids(rows):
    return lax.broadcasted_iota(jnp.int32, (rows, LANES), 1)


def faces(wide, x, ccoef, pcoef):
    lane = lane_ids(16)
    last = lane == LANES - 1
    edge = (lane == 0) | last

    def cells(x):
        own, left, right = wide[x, 256:272, :], wide[x, 272:280, :], wide[x, 280:288, :]
        return (
            jnp.concatenate([left[0:4], own[0:8], right[0:4]], axis=0),
            jnp.concatenate([left[4:8], own[8:16], right[4:8]], axis=0),
        )

    before, now, then = cells(jnp.maximum(x - 1, 0)), cells(x), cells(x + 1)
    for which, coef, half in ((0, ccoef, 0.5), (1, pcoef, -0.5)):
        c, n = now[which], then[which]
        fx, fy, fu, fd, dd = coef
        east = half * (c + n)
        south = half * (c + pltpu.roll(c, 15, 0))
        up = jnp.where(last, 0.0, half * (c + pltpu.roll(c, LANES - 1, 1)))
        down = pltpu.roll(up, 1, 1)
        rest = jnp.where(edge, half * c, 0.0)
        if which == 0:
            west = half * (c + before[0])
            sides = (east + west) + (south + pltpu.roll(south, 1, 0)) + (up + down)
            rest = (0.05 - SHIFT) + rest + sides
        fx[x], fy[x], fu[x], fd[x], dd[x] = east, south, up, down, rest


def source_plane(get, coeffs, x, y0, y1, mask_x, mask_y, emit):
    fx, fy, fu, fd, dd = coeffs
    q = get(x, y0)
    flux = fy[x, y0 - 1 : y0, :] * (q - get(x, y0 - 1))
    for y in range(y0, y1):
        nxt = get(x, y + 1)
        row = slice(y, y + 1)
        later = fy[x, row, :] * (nxt - q)
        out = dd[x, row, :] * q + (flux - later)
        out = out + fx[x - 1, row, :] * (q - get(x - 1, y))
        out = out - fx[x, row, :] * (get(x + 1, y) - q)
        out = out + fd[x, row, :] * (q - pltpu.roll(q, 1, 1))
        out = out - fu[x, row, :] * (pltpu.roll(q, LANES - 1, 1) - q)
        emit(y, masked(out, y, mask_x, mask_y))
        flux, q = later, nxt


def operator_plane(get, coeffs, x, y0, y1, mask_x, mask_y, emit):
    fx, fy, fu, fd, dd = coeffs
    before, q = get(x, y0 - 1), get(x, y0)
    north = fy[x, y0 - 1 : y0, :]
    for y in range(y0, y1):
        nxt = get(x, y + 1)
        row = slice(y, y + 1)
        south = fy[x, row, :]
        out = dd[x, row, :] * q - north * before - south * nxt
        across = fx[x - 1, row, :] * get(x - 1, y) + fx[x, row, :] * get(x + 1, y)
        depth = fd[x, row, :] * pltpu.roll(q, 1, 1) + fu[x, row, :] * pltpu.roll(q, LANES - 1, 1)
        emit(y, masked(out - (across + depth), y, mask_x, mask_y))
        before, q, north = q, nxt, south


def masked(out, y, mask_x, mask_y):
    mask = mask_x
    if y < 4:
        mask = mask_y[0] if mask is None else mask * mask_y[0]
    elif y >= 12:
        mask = mask_y[1] if mask is None else mask * mask_y[1]
    return out if mask is None else out * mask


def tiles(ref):
    return lambda x, y: ref[x, tile_at(y), :]


def put_split(s_ref, i, row, y, value, exact=False):
    lanes = slice((y - 3) * LANES, (y - 2) * LANES)
    hi = value.astype(jnp.bfloat16)
    s_ref[i, row : row + F, lanes] = hi
    if not exact:
        lo = (value - hi.astype(jnp.float32)).astype(jnp.bfloat16)
        s_ref[i, row + F : row + 2 * F, lanes] = lo


def grid_masks():
    one, zero = jnp.float32(1), jnp.float32(0)
    masks = []
    for axis in ("gx", "gy"):
        i = lax.axis_index(axis)
        low, high = i > 0, i < lax.axis_size(axis) - 1
        masks.append((jnp.where(low, one, zero), jnp.where(high, one, zero)))
    return masks


def unit_plane(ids, at_x, e0, i, s_ref, s_at):
    size_x, size_y = 16 * lax.axis_size("gx"), 8 * lax.axis_size("gy")
    good_x = (at_x >= 0) & (at_x < size_x)
    for y in range(2, 14):
        at_y = lax.axis_index("gy") * 8 + y - 4
        good = good_x & (at_y >= 0) & (at_y < size_y)
        here = jnp.where(good, (at_x * size_y + at_y) * LANES, -(2**20))
        value = jnp.where(ids == here, 1.0, 0.0)
        e0[i, tile_at(y), :] = value
        if 3 <= y < 13:
            put_split(s_ref, s_at, E0, y, value, exact=True)


def gram_of(s_ref, i):
    return lax.dot_general(
        s_ref[i, 0:KEPT, LANES : 9 * LANES],
        s_ref[i, :, LANES : 9 * LANES],
        (((1,), (1,)), ((), ())),
        preferred_element_type=jnp.float32,
    )


def inner_kernel(
    ids_ref, wide_in, core_ref, chip_ref,
    wide, v0, v1, v2, side_ref, gram_ref, s_hbm,
    e0, e1, s_ref, cx, cy, cu, cd, cr, px, py, pu, pd, pr, out_sems,
):
    del wide_in

    def fill(left_ref, right_ref):
        def plane(x, carry):
            wide[x + HALO, 0:64, :] = left_ref[x, 0:64, :]
            wide[x + HALO, 192:256, :] = right_ref[x, 0:64, :]
            wide[x + HALO, 272:280, :] = left_ref[x, 64:72, :]
            wide[x + HALO, 280:288, :] = right_ref[x, 64:72, :]
            return carry

        lax.fori_loop(0, 16, plane, 0, unroll=4)

    @pl.when(odd("gy"))
    def _():
        fill(core_ref, chip_ref)

    @pl.when(jnp.logical_not(odd("gy")))
    def _():
        fill(chip_ref, core_ref)

    gx = lax.axis_index("gx")
    _, mask_y = grid_masks()
    ids = ids_ref[...]
    ccoef, pcoef = (cx, cy, cu, cd, cr), (px, py, pu, pd, pr)

    def prepare(x, carry):
        faces(wide, x, ccoef, pcoef)
        return carry

    lax.fori_loop(4, 19, prepare, 0, unroll=3)

    def units(x, carry):
        unit_plane(ids, gx * 16 + x - HALO, e0, x, s_ref, x - HALO)
        return carry

    lax.fori_loop(6, 18, units, 0, unroll=2)
    outs = []

    def hand_on(src, dst):
        outs.extend(run_copies([(src, dst)], out_sems, len(outs)))

    def sweep(stencil, src, dst, coeffs, first, reach, row, keep):
        def plane(x, carry):
            def emit(y, out):
                if dst is not None:
                    dst[x, tile_at(y), :] = out
                if keep[0] <= y < keep[1]:
                    put_split(s_ref, x - HALO, row, y, out)

            stencil(tiles(src), coeffs, x, 4 - reach, 12 + reach, None, mask_y, emit)
            return carry

        lax.fori_loop(HALO + first, HALO + 16 - first, plane, 0, unroll=2)

    sweep(source_plane, wide, v0, pcoef, 1, 3, V0, (3, 13))
    sweep(operator_plane, v0, v1, ccoef, 2, 2, V1, (3, 13))
    sweep(operator_plane, v1, v2, ccoef, 3, 1, V2, (3, 13))
    hand_on(s_ref.at[pl.ds(1, 3), pl.ds(0, 96)], side_ref.at[pl.ds(0, 3)])
    hand_on(s_ref.at[pl.ds(12, 3), pl.ds(0, 96)], side_ref.at[pl.ds(3, 3)])
    sweep(operator_plane, e0, e1, ccoef, 3, 1, E1, (3, 13))
    hand_on(s_ref.at[pl.ds(4, 8), pl.ds(0, KEPT)], s_hbm)
    sweep(operator_plane, v2, None, ccoef, 4, 0, V3, (4, 12))
    sweep(operator_plane, e1, None, ccoef, 4, 0, E2, (4, 12))

    gram_ref[...] = gram_of(s_ref, 4)

    def gram_step(x, carry):
        gram_ref[...] += gram_of(s_ref, x)
        return carry

    lax.fori_loop(5, 12, gram_step, 0, unroll=7)
    wait_all(outs)


FIELD = (24, 256, LANES)
COEFF = (24, 16, LANES)


def inner(ids, wide, core, chip):
    vmem = pl.BlockSpec(memory_space=pltpu.VMEM)
    shape = jax.ShapeDtypeStruct
    field = shape(FIELD, jnp.float32)
    return pl.pallas_call(
        inner_kernel,
        out_shape=(
            shape((24, 288, LANES), jnp.float32),
            field, field, field,
            shape((6, 96, WIDE), jnp.bfloat16),
            shape((KEPT, ALL_ROWS), jnp.float32),
            pltpu.HBM((8, KEPT, WIDE), jnp.bfloat16),
        ),
        in_specs=[vmem] * 4,
        out_specs=(vmem,) * 6 + (pl.BlockSpec(memory_space=pltpu.HBM),),
        scratch_shapes=[pltpu.VMEM(FIELD, jnp.float32)] * 2
        + [pltpu.VMEM((16, ALL_ROWS, WIDE), jnp.bfloat16)]
        + [pltpu.VMEM(COEFF, jnp.float32)] * 10
        + [pltpu.SemaphoreType.DMA((3,))],
        input_output_aliases={1: 0},
        compiler_params=pltpu.CompilerParams(vmem_limit_bytes=VMEM_INNER * MB),
        cost_estimate=pl.CostEstimate(
            flops=4 * 10**9, bytes_accessed=16 * 10**6, transcendentals=0
        ),
        name="inner",
    )(ids, wide, core, chip)


VMEM_INNER = 36
VMEM_EDGE = 36


def edge_kernel(
    ids_ref, a_ref, b_ref, a_corner, b_corner, wide_in, v0_in, v1_in, v2_in, side_ref, first_gram,
    wide, v0, v1, v2, pay_ref, s_hbm, bg_hbm,
    e0, e1, s_ref, gram, cx, cy, cu, cd, cr, px, py, pu, pd, pr, out_sems,
):
    del wide_in, v0_in, v1_in, v2_in
    gx = lax.axis_index("gx")
    mask_x, mask_y = grid_masks()
    ids = ids_ref[...]

    def halo_plane(high, dx):
        return jnp.where(high, 19 + dx, HALO - dx)

    sides = ((a_ref, a_corner, jnp.logical_not(odd("gx"))), (b_ref, b_corner, odd("gx")))
    for ref, corner, high in sides:
        for dx in range(1, HALO + 1):
            x = halo_plane(high, dx)
            wide[x, 64:192, :] = ref[dx - 1, 0:128, :]
            wide[x, 256:272, :] = ref[dx - 1, 128:144, :]
        for dx, rows, at in CORNERS:
            x = halo_plane(high, dx)
            wide[x, 64 - rows : 64, :] = corner[at : at + rows, :]
            wide[x, 192 : 192 + rows, :] = corner[at + rows : at + 2 * rows, :]
            wide[x, 272:288, :] = corner[at + 2 * rows : at + 2 * rows + 16, :]

    outs = run_copies([(wide.at[pl.ds(3, 18), pl.ds(48, 160)], bg_hbm)], out_sems)

    for i in range(3):
        rows = 96 - 32 * (2 - i)
        s_ref[2 + i, 0:rows, :] = side_ref[i, 0:rows, :]
        s_ref[7 - i, 0:rows, :] = side_ref[5 - i, 0:rows, :]

    ccoef, pcoef = (cx, cy, cu, cd, cr), (px, py, pu, pd, pr)

    def prepare(i, carry):
        faces(wide, jnp.where(i < 9, i, i + 5), ccoef, pcoef)
        return carry

    lax.fori_loop(0, 18, prepare, 0, unroll=3)

    def mirrored(low, count, body):
        for x in range(low, low + count):
            inside = -1 <= x <= 3
            body(HALO + x, x + 1 if inside else 10, mask_x[0])
            body(19 - x, 8 - x if inside else 10, mask_x[1])

    mirrored(-2, 8, lambda at, s_at, _: unit_plane(ids, gx * 16 + at - HALO, e0, at, s_ref, s_at))

    def sweep(stencil, src, dst, coeffs, row, low, count, near, keep):
        def body(at, s_at, mask):
            def emit(y, out):
                if dst is not None:
                    dst[at, tile_at(y), :] = out
                if keep[0] <= y < keep[1]:
                    put_split(s_ref, s_at, row, y, out)

            mask = mask if low < 0 else None
            stencil(tiles(src), coeffs, at, 4 - near, 12 + near, mask, mask_y, emit)

        mirrored(low, count, body)

    def save(row, rows):
        pair = (s_ref.at[pl.ds(0, 10), pl.ds(row, rows)], s_hbm.at[:, pl.ds(row, rows)])
        outs.extend(run_copies([pair], out_sems, len(outs)))

    none, block, both = (99, 99), (4, 12), (3, 13)
    sweep(operator_plane, e0, e1, ccoef, E1, -1, 1, 0, block)
    sweep(operator_plane, e0, e1, ccoef, E1, 0, 5, 1, both)
    save(E0, 48)
    sweep(source_plane, wide, v0, pcoef, V0, -3, 1, 0, none)
    sweep(source_plane, wide, v0, pcoef, V0, -2, 1, 1, none)
    sweep(source_plane, wide, v0, pcoef, V0, -1, 1, 2, both)
    sweep(source_plane, wide, v0, pcoef, V0, 0, 1, 3, both)
    save(V0, 32)
    sweep(operator_plane, v0, v1, ccoef, V1, -2, 1, 0, none)
    sweep(operator_plane, v0, v1, ccoef, V1, -1, 1, 1, both)
    sweep(operator_plane, v0, v1, ccoef, V1, 0, 2, 2, both)
    save(V1, 32)
    sweep(operator_plane, v1, v2, ccoef, V2, -1, 1, 0, block)
    sweep(operator_plane, v1, v2, ccoef, V2, 0, 3, 1, both)
    save(V2, 32)
    sweep(operator_plane, v2, None, ccoef, V3, 0, 4, 0, block)
    sweep(operator_plane, e1, None, ccoef, E2, 0, 4, 0, block)

    gram[...] = first_gram[...]

    def gram_step(i, carry):
        gram[...] += gram_of(s_ref, i)
        return carry

    lax.fori_loop(1, 9, gram_step, 0, unroll=8)

    def rows_of(row):
        if row == E0:
            return gram[row : row + F, :]
        return gram[row : row + F, :] + gram[row + F : row + 2 * F, :]

    summed = {row: rows_of(row) for row in (V0, V1, V2, E0, E1)}

    def block_of(row, col):
        rows = summed[row]
        if col == E0:
            return rows[:, col : col + F]
        return rows[:, col : col + F] + rows[:, col + F : col + 2 * F]

    order = [
        (V0, V0), (V0, V1), (V1, V1), (V1, V2), (V2, V2), (V2, V3), (V0, E0), (V1, E0),
        (V2, E0), (E0, V3), (E1, V3), (E0, E0), (E0, E1), (E1, E1), (E1, E2),
    ]
    blocks = [block_of(r, c) for r, c in order] + [jnp.zeros((F, F), jnp.float32)]
    pay_ref[0:16, :] = jnp.concatenate(blocks[:8], axis=1)
    pay_ref[16:32, :] = jnp.concatenate(blocks[8:], axis=1)
    wait_all(outs)


def edge(ids, a, b, a_corner, b_corner, wide, v0, v1, v2, side, gram):
    vmem = pl.BlockSpec(memory_space=pltpu.VMEM)
    hbm = pl.BlockSpec(memory_space=pltpu.HBM)
    shape = jax.ShapeDtypeStruct
    field = shape(FIELD, jnp.float32)
    outs = pl.pallas_call(
        edge_kernel,
        out_shape=(
            shape((24, 288, LANES), jnp.float32),
            field, field, field,
            shape((32, LANES), jnp.float32),
            pltpu.HBM((10, KEPT, WIDE), jnp.bfloat16),
            pltpu.HBM((18, 160, LANES), jnp.float32),
        ),
        in_specs=[vmem] * 11,
        out_specs=(vmem,) * 5 + (hbm,) * 2,
        scratch_shapes=[pltpu.VMEM(FIELD, jnp.float32)] * 2
        + [
            pltpu.VMEM((11, ALL_ROWS, WIDE), jnp.bfloat16),
            pltpu.VMEM((KEPT, ALL_ROWS), jnp.float32),
        ]
        + [pltpu.VMEM(COEFF, jnp.float32)] * 10
        + [pltpu.SemaphoreType.DMA((5,))],
        input_output_aliases={5: 0, 6: 1, 7: 2, 8: 3},
        compiler_params=pltpu.CompilerParams(vmem_limit_bytes=VMEM_EDGE * MB),
        name="edge",
    )(ids, a, b, a_corner, b_corner, wide, v0, v1, v2, side, gram)
    return outs[4:]


def matmul(a, b, dims=((1,), (0,))):
    return lax.dot_general(
        a, b, (dims, ((), ())), precision=HIGHEST, preferred_element_type=jnp.float32
    )


def galerkin(m0, m1, m2, m3):
    a12 = m2 + SHIFT * m1
    work = jnp.concatenate(
        [
            jnp.concatenate([m1 + SHIFT * m0, a12, m0], axis=1),
            jnp.concatenate([a12, m3 + SHIFT * m2, m1], axis=1),
        ],
        axis=0,
    )
    work = jnp.concatenate([work, jnp.zeros((2 * F, LANES - 3 * F), jnp.float32)], axis=1)
    return eliminate(work)[:, 2 * F : 3 * F]


def eliminate(work, size=8):
    count = work.shape[0]
    sub = lax.broadcasted_iota(jnp.int32, work.shape, 0)

    def column(k):
        return jnp.take_along_axis(work, jnp.full(work.shape, k, jnp.int32), axis=1)

    def row(v, k):
        return jnp.broadcast_to(v[k : k + 1, :], (8, LANES))

    def tall(v):
        return jnp.concatenate([v] * (count // 8), axis=0)

    for k in range(0, count, size):
        cols = [column(k + j) for j in range(size)]
        rows = [row(work, k + i) for i in range(size)]
        p = [[row(cols[j], k + i) for j in range(size)] for i in range(size)]
        for s in range(0, size, 2):
            a, b, c, d = p[s][s], p[s][s + 1], p[s + 1][s], p[s + 1][s + 1]
            inverse = 1.0 / (a * d - b * c)
            a, b, c, d = d * inverse, -(b * inverse), -(c * inverse), a * inverse
            rows[s], rows[s + 1] = a * rows[s] + b * rows[s + 1], c * rows[s] + d * rows[s + 1]
            for j in range(s + 2, size):
                u, v = p[s][j], p[s + 1][j]
                p[s][j], p[s + 1][j] = a * u + b * v, c * u + d * v
            for i in range(size):
                if i in (s, s + 1):
                    continue
                u, v = p[i][s], p[i][s + 1]
                rows[i] = rows[i] - u * rows[s] - v * rows[s + 1]
                for j in range(s + 2, size):
                    p[i][j] = p[i][j] - u * p[s][j] - v * p[s + 1][j]
        for j in range(size):
            work = work - cols[j] * tall(rows[j])
        for j in range(size):
            work = jnp.where(sub == k + j, tall(rows[j]), work)
    return work


def final_kernel(
    pattern_ref, parts_ref, bg_hbm, mid_hbm, edge_hbm,
    out_ref, sens_ref, bg, adj, s_ref, mix_ref, sems, *, damping,
):
    pairs = [
        (edge_hbm.at[pl.ds(0, 5)], s_ref.at[pl.ds(0, 5)]),
        (mid_hbm, s_ref.at[pl.ds(5, 8)]),
        (edge_hbm.at[pl.ds(5, 5)], s_ref.at[pl.ds(13, 5)]),
        (bg_hbm, bg),
    ]
    copies = [pltpu.make_async_copy(s, d, sems.at[i]) for i, (s, d) in enumerate(pairs)]

    @pl.when(lax.axis_index("gx") >= 0)
    def _():
        for c in copies:
            c.start()

    total = jnp.sum(parts_ref[...], axis=0)

    def part(k):
        r, c = (k // 8) * F, (k % 8) * F
        return total[r : r + F, c : c + F]

    m = [part(k) for k in range(6)]
    p = [part(6), part(7), part(8), part(9).T, part(10).T]
    e = [part(k) for k in range(11, 15)]
    y = galerkin(*m[:4])

    lane = lax.broadcasted_iota(jnp.int32, (F, F), 1)
    sub = lax.broadcasted_iota(jnp.int32, (F, F), 0)
    first, second = jnp.zeros((F, F), jnp.int32), jnp.zeros((F, F), jnp.int32)
    for i in range(F):
        first = jnp.where(sub == i, pattern_ref[i, 0], first)
        second = jnp.where(sub == i, pattern_ref[i, 1], second)
    pairing = jnp.where(lane == first, 1.0, 0.0) - jnp.where(lane == second, 1.0, 0.0)
    w = matmul(8.0 * matmul(pairing, pairing, ((0,), (0,))), jnp.concatenate(p[:2], axis=0), ((1,), (1,)))
    forms = []
    for k in range(4):
        inside = jnp.concatenate(
            [
                jnp.concatenate([m[k], m[k + 1]], axis=1),
                jnp.concatenate([m[k + 1], m[k + 2]], axis=1),
            ],
            axis=0,
        )
        across = matmul(jnp.concatenate([p[k], p[k + 1]], axis=0), w)
        local = matmul(w, matmul(e[k], w), ((0,), (0,)))
        forms.append(damping * (damping * inside + across + across.T) + local)
    hy = matmul(jnp.concatenate(forms, axis=0), y)
    moments = [matmul(y, hy[32 * k : 32 * (k + 1)], ((0,), (0,))) for k in range(4)]
    z = jnp.concatenate([damping * y, matmul(w, y)], axis=0)
    q = galerkin(*moments)
    z0, z1 = matmul(z, q[0:F]), matmul(z, q[F:])
    none = jnp.zeros((F, F), jnp.float32)
    mix = [
        jnp.concatenate([y[0:F], z0[0:F]], axis=1),
        jnp.concatenate([y[F:], z0[F : 2 * F] + z1[0:F]], axis=1),
        jnp.concatenate([none, z1[F : 2 * F]], axis=1),
        jnp.concatenate([none, z0[2 * F :]], axis=1),
        jnp.concatenate([none, z1[2 * F :]], axis=1),
    ]
    mix = [mix[i] for i in (0, 0, 1, 1, 2, 2, 3, 4, 4)]
    mix = jnp.concatenate(mix, axis=0).T
    hi = mix.astype(jnp.bfloat16)
    mix_ref[0:32, :] = hi
    mix_ref[32:64, :] = (mix - hi.astype(jnp.float32)).astype(jnp.bfloat16)
    wait_all(copies)
    both = mix_ref[...]

    def combine(x, lanes):
        out = jnp.dot(both, s_ref[x, :, lanes], preferred_element_type=jnp.float32)
        return out[0:32] + out[32:64]

    def store(x, out):
        for k in range(10):
            cols = slice(k * LANES, (k + 1) * LANES)
            if 0 < k < 9:
                out_ref[pl.ds(x * 8 + k - 9, F, stride=128), :] = out[0:F, cols]
            adj[x, tile_at(k), :] = out[F:, cols]

    def store_end(x, out):
        for k in range(8):
            adj[x, tile_at(k + 1), :] = out[F:, k * LANES : (k + 1) * LANES]

    lane = lane_ids(F)

    def sens_plane(x):
        b, a = bg[x, tile_at(1), :], adj[x, tile_at(1), :]
        before = (b - bg[x, tile_at(0), :]) * (a - adj[x, tile_at(0), :])
        for k in range(1, 9):
            bn, an = bg[x, tile_at(k + 1), :], adj[x, tile_at(k + 1), :]
            after = (bn - b) * (an - a)
            total = before + after
            for s in (x - 1, x + 1):
                total = total + (bg[s, tile_at(k), :] - b) * (adj[s, tile_at(k), :] - a)
            bu = jnp.where(lane == LANES - 1, 0.0, pltpu.roll(b, LANES - 1, 1))
            au = jnp.where(lane == LANES - 1, 0.0, pltpu.roll(a, LANES - 1, 1))
            bd = jnp.where(lane == 0, 0.0, pltpu.roll(b, 1, 1))
            ad = jnp.where(lane == 0, 0.0, pltpu.roll(a, 1, 1))
            total = total + (bu - b) * (au - a) + (bd - b) * (ad - a)
            sens_ref[x - 1, k - 1 : k, :] = -0.5 * jnp.sum(total, axis=0, keepdims=True)
            before, b, a = after, bn, an

    ends = slice(LANES, 9 * LANES)
    store_end(0, combine(0, ends))
    store(1, combine(1, slice(0, WIDE)))
    store(2, combine(2, slice(0, WIDE)))

    def plane(x, carry):
        out = combine(x + 2, slice(0, WIDE))
        sens_plane(x)
        store(x + 2, out)
        return carry

    lax.fori_loop(1, 15, plane, 0, unroll=7)
    out = combine(17, ends)
    sens_plane(15)
    store_end(17, out)
    sens_plane(16)


def final(pattern, parts, bg, mid, edges, damping):
    vmem = pl.BlockSpec(memory_space=pltpu.VMEM)
    hbm = pl.BlockSpec(memory_space=pltpu.HBM)

    def kernel(*refs):
        final_kernel(*refs, damping=damping)

    return pl.pallas_call(
        kernel,
        out_shape=(
            jax.ShapeDtypeStruct((2048, LANES), jnp.float32),
            jax.ShapeDtypeStruct((16, 8, LANES), jnp.float32),
        ),
        in_specs=[pl.BlockSpec(memory_space=pltpu.SMEM), vmem] + [hbm] * 3,
        scratch_shapes=[
            pltpu.VMEM((18, 160, LANES), jnp.float32),
            pltpu.VMEM((18, 160, LANES), jnp.float32),
            pltpu.VMEM((18, KEPT, WIDE), jnp.bfloat16),
            pltpu.VMEM((64, KEPT), jnp.bfloat16),
            pltpu.SemaphoreType.DMA((4,)),
        ],
        compiler_params=pltpu.CompilerParams(vmem_limit_bytes=56 * MB),
        name="final",
    )(pattern, parts, bg, mid, edges)


def spread(block, axis, count, groups=None):
    copies = jnp.broadcast_to(block[None], (count,) + block.shape)
    return lax.all_to_all(copies, axis, 0, 0, axis_index_groups=groups)


def swaps(first, count):
    lows = range(first, count - 1, 2)
    return [(i, i + 1) for i in lows] + [(i + 1, i) for i in lows]


def on_device(background, conductivity, perturbation, electrodes, pattern):
    size_x, size_y, size_z = conductivity.shape
    count_x, count_y = lax.axis_size("gx"), lax.axis_size("gy")
    wide, core, chip, a, b, ids = pack(background, conductivity, perturbation, electrodes)
    a = lax.ppermute(a, "gx", swaps(0, count_x))
    b = lax.ppermute(b, "gx", swaps(1, count_x))
    chip = lax.ppermute(chip, "gy", swaps(1, count_y))
    core = lax.ppermute(core, "gy", swaps(0, count_y))
    a_corner, b_corner = pack_corners(core, chip)
    a_corner = lax.ppermute(a_corner, "gx", swaps(0, count_x))
    b_corner = lax.ppermute(b_corner, "gx", swaps(1, count_x))
    wide, v0, v1, v2, side, gram, mid = inner(ids, wide, core, chip)
    pay, edges, bg = edge(
        ids, a, b, a_corner, b_corner, wide, v0, v1, v2, side, gram
    )
    pay = pay + lax.ppermute(pay, "gy", swaps(0, count_y))
    pay = jnp.sum(spread(pay, "gx", count_x), axis=0)
    chips = count_y // 2
    groups = [[2 * i + c for i in range(chips)] for c in range(2)]
    parts = spread(pay, "gy", chips, groups)
    cells = size_x * size_y * size_z * count_x * count_y
    damping = 80.0 / math.sqrt(cells)
    tangent, sens = final(pattern, parts, bg, mid, edges, damping)
    return tangent.reshape(background.shape), sens


def solution(mesh):
    in_specs = (P(None, "gx", "gy", None), P("gx", "gy", None), P("gx", "gy", None), P(), P())
    out_specs = (P(None, "gx", "gy", None), P("gx", "gy", None))
    return jax.shard_map(
        on_device, mesh=mesh, in_specs=in_specs, out_specs=out_specs, check_vma=False
    )
```

time: 80.8 us -> 76.3 us (0.944)
  Pallas kernels: 27.7 us -> 23.3 us
    pallas_call x1, Pallas kernels: 10.5 us -> 8.22 us  [final(): pl.pallas_call(kernel, out_shape=(jax.ShapeDtypeStruct((2048, LANES), jnp...]
    pallas_call x4, Pallas kernels: 17.2 us -> 15.1 us  [the longest x1 8.21 us: inner(): pl.pallas_call(inner_kernel, out_shape=(shape((24, 288, LANES), jnp.float...]
where the time goes in v4:
time: 76.3 us; the launch traced here: 75.9 us
  Pallas kernels  23.3 us (31%)
  blocking collectives  18.5 us (24%)
  starting transfers between devices  16.9 us (22%)
  waiting for transfers between devices  14.1 us (18%)
  local copies, waits for them, and re-layouts  2.15 us (3%)
  between operations  0.91 us (1%)
    all_to_all x1, blocking collectives, spread(): return lax.all_to_all(copies, axis, 0, 0, axis_index_groups=groups)  18.5 us
    all_to_all x1, starting transfers between devices, spread(): return lax.all_to_all(copies, axis, 0, 0, axis_index_groups=groups)  9.04 us
    pallas_call x1, Pallas kernels, final(): pl.pallas_call(kernel, out_shape=(jax.ShapeDtypeStruct((2048, LANES), jnp...  8.22 us
    pallas_call x1, Pallas kernels, inner(): pl.pallas_call(inner_kernel, out_shape=(shape((24, 288, LANES), jnp.float...  8.21 us
    all_to_all x1, waiting for transfers between devices, spread(): return lax.all_to_all(copies, axis, 0, 0, axis_index_groups=groups)  6.65 us
    ppermute x1, waiting for transfers between devices, on_device(): chip = lax.ppermute(chip, 'gy', swaps(1, count_y))  6.6 us
    pallas_call x1, Pallas kernels, edge(): pl.pallas_call(edge_kernel, out_shape=(shape((24, 288, LANES), jnp.float3...  5.13 us
    ppermute x1, starting transfers between devices, on_device(): chip = lax.ppermute(chip, 'gy', swaps(1, count_y))  4.27 us
  transfers between devices with their start and end apart: 8, of which 3 were waited for; matrix products, arithmetic and copies ran while one was open for 1% of the time, Pallas kernels for 11%

profile of v4, /device:TPU:2, one launch (start us, length us, event | category | flops | bytes accessed | tf_op | source)
XLA Modules:
  0.0 75.9 jit_solution(17946288217262966561)
XLA Ops:
  0.6 1.8 %pack_y.1 = (f32[24,288,128]{2,1,0:T(8,128)S(1)}, f32[16,72,128]{2,1,0:T(8,128)S(1)}, f32[16,72,128]{2,1,0:T(8,128)S(1)}, f32[4,144,128]{2,1,0:T(8,128)S(1)}, f3...) custom-call(f32[16,16,8,128]{3,2,1,0:T(8,128)} %bg_hbm.1, f32[16,8,128]{2,1,0:T(8,128)} %cond_hbm.1, ...), custom_call_target="tpu_custom_call" | custom-call | tf_op jit(solution)/shard_map/pack_y/pallas_call | solution.py:107
  2.4 0.1 collective-permute-start.2
  2.5 4.3 %collective-permute-start.3 = (f32[16,72,128]{2,1,0:T(8,128)S(1)}, f32[16,72,128]{2,1,0:T(8,128)S(1)}, u32[]{:S(2)}, u32[]{:S(2)}) collective-permute-start(f32[16,72,128]{2,1,0:T(8,128)S(1)} %get-tuple-element.26), channel_id=1, source_target_pairs={{1,2},{3,4},{5,6},{7,8},{9,10},{11,12},{13,14},{15,16},{17,18},{19... | collective-permute-start | bytes 1769480 | tf_op jit(solution)/shard_map/ppermute | solution.py:771
  6.8 0.3 collective-permute-start
  7.1 0.7 collective-permute-start.1
  7.7 0.0 collective-permute-done.2.core_ref
  7.7 6.6 %collective-permute-done.3.chip_ref = f32[16,72,128]{2,1,0:T(8,128)S(1)} collective-permute-done((f32[16,72,128]{2,1,0:T(8,128)S(1)}, f32[16,72,128]{2,1,0:T(8,128)S(1)}, u32[]{:S(2)}, u32[]{:S(2)}) %collective-permute-start.3) | collective-permute-done | bytes 589856 | tf_op jit(solution)/shard_map/ppermute | solution.py:771
  14.4 1.4 %collective-permute-start.4 = (f32[240,128]{1,0:T(8,128)S(1)}, f32[240,128]{1,0:T(8,128)S(1)}, u32[]{:S(2)}, u32[]{:S(2)}) collective-permute-start(f32[240,128]{1,0:T(8,128)S(1)} %get-tuple-element.27), channel_id=1, source_target_pairs={{0,32},{64,96},{128,160},{192,224},{32,0},{96,64},{160,128},{224,1... | collective-permute-start | bytes 368648 | tf_op jit(solution)/shard_map/ppermute | solution.py:774
  15.7 0.7 collective-permute-start.5
  16.4 8.2 %inner.1 = (f32[24,288,128]{2,1,0:T(8,128)S(1)}, f32[24,256,128]{2,1,0:T(8,128)S(1)}, f32[24,256,128]{2,1,0:T(8,128)S(1)}, f32[24,256,128]{2,1,0:T(8,128)S(1)}, ...) custom-call(s32[16,128]{1,0:T(8,128)S(1)} %get-tuple-element.22.ids_, ...), custom_call_target="tpu_custom_call", output_to_operand_aliasing={{0}: (1, {})} | custom-call | flops 4000000000 | bytes 16000000 | tf_op jit(solution)/shard_map/inner/pallas_call | solution.py:377
  24.6 0.0 collective-permute-done.a_ref
  24.6 0.0 collective-permute-done.1.b_ref
  24.6 0.0 collective-permute-done.4.a_corner
  24.6 0.0 collective-permute-done.5.b_corner
  24.7 0.0 copy-start.1
  24.7 5.1 %edge.1 = (f32[24,288,128]{2,1,0:T(8,128)S(1)}, f32[24,256,128]{2,1,0:T(8,128)S(1)}, f32[24,256,128]{2,1,0:T(8,128)S(1)}, f32[24,256,128]{2,1,0:T(8,128)S(1)}, f...) custom-call(s32[16,128]{1,0:T(8,128)S(1)} %get-tuple-element.22.ids_, ...), custom_call_target="tpu_custom_call", output_to_operand_aliasing={{0}: (5, {}), {1}: (6, {}), {2}: (7, {}), {3}: (8, {})} | custom-call | tf_op jit(solution)/shard_map/edge/pallas_call | solution.py:525
  29.8 0.6 collective-permute-start.6
  30.4 0.8 %collective-permute-done.6 = f32[32,128]{1,0:T(8,128)S(1)} collective-permute-done((f32[32,128]{1,0:T(8,128)S(1)}, f32[32,128]{1,0:T(8,128)S(1)}, u32[]{:S(2)}, u32[]{:S(2)}) %collective-permute-start.6) | collective-permute-done | bytes 16416 | tf_op jit(solution)/shard_map/ppermute | solution.py:780
  31.2 18.5 %all_to_all.10 = f32[8,32,128]{2,1,0:T(8,128)S(1)} all-to-all(f32[8,32,128]{2,1,0:T(8,128)S(1)} %broadcast_in_dim.4), channel_id=1, replica_groups=mesh['gx'=8,'gy'=32] {'gx'}, dimensions={0} | all-to-all | bytes 262144 | tf_op jit(solution)/shard_map/all_to_all | solution.py:757
  49.7 0.7 broadcast_in_dim.5
  50.5 9.0 %all-to-all-start.1 = ((f32[16,32,128]{2,1,0:T(8,128)}), f32[16,32,128]{2,1,0:T(8,128)S(1)}, u32[]{:S(2)}, u32[]{:S(2)}) async-start(f32[16,32,128]{2,1,0:T(8,128)} %broadcast_in_dim.5), calls=%async_computation.1 | async-start | bytes 524288 | tf_op jit(solution)/shard_map/all_to_all | solution.py:757
  59.5 0.0 copy-done.1
  59.5 0.7 copy.13.refs_0_
  60.2 6.6 %all-to-all-done.1.refs_1_ = f32[16,32,128]{2,1,0:T(8,128)S(1)} async-done(((f32[16,32,128]{2,1,0:T(8,128)}), f32[16,32,128]{2,1,0:T(8,128)S(1)}, u32[]{:S(2)}, u32[]{:S(2)}) %all-to-all-start.1) | async-done | bytes 262176 | tf_op jit(solution)/shard_map/all_to_all | solution.py:757
  66.8 0.0 copy-start
  66.8 0.7 copy-done
  67.6 8.2 %final.1 = (f32[2048,128]{1,0:T(8,128)}, f32[16,8,128]{2,1,0:T(8,128)}) custom-call(s32[16,2]{1,0:T(8,128)} %copy.13.refs_0_, f32[16,32,128]{2,1,0:T(8,128)} %copy-done, f32[18,160,128]{2,1,0:T(8,128)} %get-tuple-element.37.refs_2_, bf16[8,144,1280]{2,1,0:T(8,128)(2,1)} %get-tuple-element.38.refs_3_, bf16[10,144,1280]{2,1,0:T(8,128)(2,1)} %get-tuple-element.39.refs_4_), custom_call_target="tpu_custom_call" | custom-call | tf_op jit(solution)/shard_map/final/pallas_call | solution.py:736
  (4 shorter events, 0.0 us)
Async XLA Ops:
  2.4 5.3 %collective-permute-start.2 = (f32[16,72,128]{2,1,0:T(8,128)S(1)}, f32[16,72,128]{2,1,0:T(8,128)S(1)}, u32[]{:S(2)}, u32[]{:S(2)}) collective-permute-start(f32[16,72,128]{2,1,0:T(8,128)S(1)} %get-tuple-element.25), channel_id=1, source_target_pairs={{0,1},{2,3},{4,5},{6,7},{8,9},{10,11},{12,13},{14,15},{16,17},{18,... | collective-permute-start | bytes 1769480 | tf_op jit(solution)/shard_map/ppermute | solution.py:772
  2.5 11.8 %collective-permute-start.3 = (f32[16,72,128]{2,1,0:T(8,128)S(1)}, f32[16,72,128]{2,1,0:T(8,128)S(1)}, u32[]{:S(2)}, u32[]{:S(2)}) collective-permute-start(f32[16,72,128]{2,1,0:T(8,128)S(1)} %get-tuple-element.26), channel_id=1, source_target_pairs={{1,2},{3,4},{5,6},{7,8},{9,10},{11,12},{13,14},{15,16},{17,18},{19... | collective-permute-start | bytes 1769480 | tf_op jit(solution)/shard_map/ppermute | solution.py:771
  6.8 17.8 %collective-permute-start = (f32[4,144,128]{2,1,0:T(8,128)S(1)}, f32[4,144,128]{2,1,0:T(8,128)S(1)}, u32[]{:S(2)}, u32[]{:S(2)}) collective-permute-start(f32[4,144,128]{2,1,0:T(8,128)S(1)} %get-tuple-element.23), channel_id=1, source_target_pairs={{0,32},{64,96},{128,160},{192,224},{32,0},{96,64},{160,128},{224,1... | collective-permute-start | bytes 884744 | tf_op jit(solution)/shard_map/ppermute | solution.py:769
  7.1 17.6 %collective-permute-start.1 = (f32[4,144,128]{2,1,0:T(8,128)S(1)}, f32[4,144,128]{2,1,0:T(8,128)S(1)}, u32[]{:S(2)}, u32[]{:S(2)}) collective-permute-start(f32[4,144,128]{2,1,0:T(8,128)S(1)} %get-tuple-element.24), channel_id=1, source_target_pairs={{32,64},{96,128},{160,192},{64,32},{128,96},{192,160},{33,65},{97,... | collective-permute-start | bytes 884744 | tf_op jit(solution)/shard_map/ppermute | solution.py:770
  14.4 10.3 %collective-permute-start.4 = (f32[240,128]{1,0:T(8,128)S(1)}, f32[240,128]{1,0:T(8,128)S(1)}, u32[]{:S(2)}, u32[]{:S(2)}) collective-permute-start(f32[240,128]{1,0:T(8,128)S(1)} %get-tuple-element.27), channel_id=1, source_target_pairs={{0,32},{64,96},{128,160},{192,224},{32,0},{96,64},{160,128},{224,1... | collective-permute-start | bytes 368648 | tf_op jit(solution)/shard_map/ppermute | solution.py:774
  15.7 8.9 %collective-permute-start.5 = (f32[240,128]{1,0:T(8,128)S(1)}, f32[240,128]{1,0:T(8,128)S(1)}, u32[]{:S(2)}, u32[]{:S(2)}) collective-permute-start(f32[240,128]{1,0:T(8,128)S(1)} %get-tuple-element.28), channel_id=1, source_target_pairs={{32,64},{96,128},{160,192},{64,32},{128,96},{192,160},{33,65},{97,... | collective-permute-start | bytes 368648 | tf_op jit(solution)/shard_map/ppermute | solution.py:775
  24.7 34.8 %copy-start.1 = (s32[16,2]{0,1:T(2,128)S(1)}, s32[16,2]{0,1:T(2,128)}, u32[]{:S(2)}) copy-start(s32[16,2]{0,1:T(2,128)} %param.9) | copy-start | bytes 388
  29.8 1.4 %collective-permute-start.6 = (f32[32,128]{1,0:T(8,128)S(1)}, f32[32,128]{1,0:T(8,128)S(1)}, u32[]{:S(2)}, u32[]{:S(2)}) collective-permute-start(f32[32,128]{1,0:T(8,128)S(1)} %get-tuple-element.36), channel_id=1, source_target_pairs={{0,1},{2,3},{4,5},{6,7},{8,9},{10,11},{12,13},{14,15},{16,17},{18,... | collective-permute-start | bytes 49160 | tf_op jit(solution)/shard_map/ppermute | solution.py:780
  50.5 16.4 %all-to-all-start.1 = ((f32[16,32,128]{2,1,0:T(8,128)}), f32[16,32,128]{2,1,0:T(8,128)S(1)}, u32[]{:S(2)}, u32[]{:S(2)}) async-start(f32[16,32,128]{2,1,0:T(8,128)} %broadcast_in_dim.5), calls=%async_computation.1 | async-start | bytes 524288 | tf_op jit(solution)/shard_map/all_to_all | solution.py:757
  66.8 0.7 copy-start

commit v5 on v4

--- a/solution.py
+++ b/solution.py
@@ -16,6 +16,8 @@
 KEPT, ALL_ROWS = 144, 208
 WIDE = 10 * LANES
 MB = 2**20
+FIELD = (24, 256, LANES)
+COEFF = (24, 16, LANES)
 
 
 def tile_at(y):
@@ -44,20 +46,30 @@
 
 
 def pack_kernel(
-    bg_hbm, cond_hbm, pert_hbm, elec_hbm, wide_ref, core_ref, chip_ref, a_ref, b_ref, ids_ref,
-    bg, cond_v, pert_v, elec, sems,
+    bg_hbm, cond_hbm, pert_hbm, elec_hbm, pattern_hbm,
+    wide_ref, core_ref, chip_ref, a_ref, b_ref, ids_ref, pairing_ref,
+    bg, cond_v, pert_v, elec, pattern, pairing, sems,
 ):
     size_x, size_y = cond_v.shape[0], cond_v.shape[1]
     each = size_x // PARTS
-    pairs = [(cond_hbm, cond_v), (pert_hbm, pert_v), (elec_hbm, elec)]
+    pairs = [(cond_hbm, cond_v), (pert_hbm, pert_v), (elec_hbm, elec), (pattern_hbm, pattern)]
     for i in range(PARTS):
         planes = pl.ds(i * each, each)
         pairs.append((bg_hbm.at[:, planes], bg.at[:, planes]))
     copies = run_copies(pairs, sems)
 
+    wait_all(copies[:4])
+    sub = lax.broadcasted_iota(jnp.int32, (F, LANES), 0)
+    ids = jnp.zeros((F, LANES), jnp.int32)
+    for e in range(F):
+        ids = jnp.where(sub == e, elec[e], ids)
+    ids_ref[...] = ids - lane_ids(F)
+    sub = lax.broadcasted_iota(jnp.int32, (F, F), 0)
+    first = jnp.where(sub == pattern[0:1, :], 1.0, 0.0)
+    pairing[:, 0:F] = first - jnp.where(sub == pattern[1:2, :], 1.0, 0.0)
+    outs = run_copies([(pairing, pairing_ref)], sems, 4 + PARTS)
+
     def fill(top_ref, bottom_ref):
-        wait_all(copies[:3])
-
         def plane(x, carry):
             for y in range(size_y):
                 tile = bg[:, x, y, :]
@@ -74,7 +86,7 @@
             return carry
 
         for i in range(PARTS):
-            copies[3 + i].wait()
+            copies[4 + i].wait()
             lax.fori_loop(i * each, (i + 1) * each, plane, 0, unroll=each)
 
     @pl.when(odd("gy"))
@@ -84,25 +96,20 @@
     @pl.when(jnp.logical_not(odd("gy")))
     def _():
         fill(core_ref, chip_ref)
-
-    sub = lax.broadcasted_iota(jnp.int32, (F, LANES), 0)
-    ids = jnp.zeros((F, LANES), jnp.int32)
-    for e in range(F):
-        ids = jnp.where(sub == e, elec[e], ids)
-    ids_ref[...] = ids - lane_ids(F)
 
     for out, up in ((a_ref, jnp.logical_not(odd("gx"))), (b_ref, odd("gx"))):
         for dx in range(1, HALO + 1):
             x = HALO + jnp.where(up, size_x - dx, dx - 1)
             out[dx - 1, 0:128, :] = wide_ref[x, 64:192, :]
             out[dx - 1, 128:144, :] = wide_ref[x, 256:272, :]
-
-
-def pack(background, conductivity, perturbation, electrodes):
+    wait_all(outs)
+
+
+def pack(background, conductivity, perturbation, electrodes, pattern):
     shape = jax.ShapeDtypeStruct
     inputs = [
         pltpu.with_memory_space_constraint(v, pltpu.HBM)
-        for v in (background, conductivity, perturbation, electrodes)
+        for v in (background, conductivity, perturbation, electrodes, pattern.T)
     ]
     return pl.pallas_call(
         pack_kernel,
@@ -113,14 +120,19 @@
             shape((HALO, 144, LANES), jnp.float32),
             shape((HALO, 144, LANES), jnp.float32),
             shape((F, LANES), jnp.int32),
+            pltpu.HBM((F, LANES), jnp.float32),
         ),
-        in_specs=[pl.BlockSpec(memory_space=pltpu.HBM)] * 4,
+        in_specs=[pl.BlockSpec(memory_space=pltpu.HBM)] * 5,
+        out_specs=(pl.BlockSpec(memory_space=pltpu.VMEM),) * 6
+        + (pl.BlockSpec(memory_space=pltpu.HBM),),
         scratch_shapes=[
             pltpu.VMEM((16, 16, 8, LANES), jnp.float32),
             pltpu.VMEM((16, 8, LANES), jnp.float32),
             pltpu.VMEM((16, 8, LANES), jnp.float32),
             pltpu.SMEM((F,), jnp.int32),
-            pltpu.SemaphoreType.DMA((3 + PARTS,)),
+            pltpu.VMEM((2, F), jnp.int32),
+            pltpu.VMEM((F, LANES), jnp.float32),
+            pltpu.SemaphoreType.DMA((5 + PARTS,)),
         ],
         compiler_params=pltpu.CompilerParams(vmem_limit_bytes=16 * MB),
         name="pack_y",
@@ -287,12 +299,79 @@
     )
 
 
+def prepare_planes(wide, ccoef, pcoef):
+    def prepare(x, carry):
+        faces(wide, x, ccoef, pcoef)
+        return carry
+
+    lax.fori_loop(HALO, HALO + 15, prepare, 0, unroll=3)
+
+
+def sweep_planes(stencil, src, dst, coeffs, first, ranges, mask_y, s_ref, row, keep, unroll=2):
+    def plane(x, carry):
+        def emit(y, out):
+            if dst is not None:
+                dst[x, tile_at(y), :] = out
+            if keep[0] <= y < keep[1]:
+                put_split(s_ref, x - HALO, row, y, out)
+
+        for y0, y1 in ranges:
+            stencil(tiles(src), coeffs, x, y0, y1, None, mask_y, emit)
+        return carry
+
+    lax.fori_loop(HALO + first, HALO + 16 - first, plane, 0, unroll=unroll)
+
+
+BLOCK, BOTH = (4, 12), (3, 13)
+
+
+def early_kernel(
+    ids_ref, wide, v0, v1, v2, e0, e1, s_ref, cx, cy, cu, cd, cr, px, py, pu, pd, pr
+):
+    gx = lax.axis_index("gx")
+    ids = ids_ref[...]
+    ccoef, pcoef = (cx, cy, cu, cd, cr), (px, py, pu, pd, pr)
+    prepare_planes(wide, ccoef, pcoef)
+
+    def units(x, carry):
+        unit_plane(ids, gx * 16 + x - HALO, e0, x, s_ref, x - HALO)
+        return carry
+
+    lax.fori_loop(6, 18, units, 0, unroll=2)
+
+    def sweep(stencil, src, dst, coeffs, first, rows, row):
+        sweep_planes(stencil, src, dst, coeffs, first, [rows], None, s_ref, row, rows)
+
+    sweep(source_plane, wide, v0, pcoef, 1, (5, 11), V0)
+    sweep(operator_plane, v0, v1, ccoef, 2, (6, 10), V1)
+    sweep(operator_plane, v1, v2, ccoef, 3, (7, 9), V2)
+    sweep(operator_plane, e0, e1, ccoef, 3, (5, 11), E1)
+    sweep(operator_plane, e1, None, ccoef, 4, (6, 10), E2)
+
+
+def early(ids, wide):
+    vmem = pl.BlockSpec(memory_space=pltpu.VMEM)
+    field = jax.ShapeDtypeStruct(FIELD, jnp.float32)
+    return pl.pallas_call(
+        early_kernel,
+        out_shape=(field,) * 5 + (jax.ShapeDtypeStruct((16, ALL_ROWS, WIDE), jnp.bfloat16),),
+        in_specs=[vmem] * 2,
+        out_specs=(vmem,) * 6,
+        scratch_shapes=[pltpu.VMEM(COEFF, jnp.float32)] * 10,
+        compiler_params=pltpu.CompilerParams(vmem_limit_bytes=10 * MB),
+        cost_estimate=pl.CostEstimate(
+            flops=10**9, bytes_accessed=8 * 10**6, transcendentals=0
+        ),
+        name="early",
+    )(ids, wide)
+
+
 def inner_kernel(
-    ids_ref, wide_in, core_ref, chip_ref,
-    wide, v0, v1, v2, side_ref, gram_ref, s_hbm,
-    e0, e1, s_ref, cx, cy, cu, cd, cr, px, py, pu, pd, pr, out_sems,
+    wide_in, v0_in, v1_in, v2_in, e0_in, e1_in, s_in, core_ref, chip_ref,
+    wide, v0, v1, v2, e0, e1, s_ref, side_ref, gram_ref, s_hbm,
+    cx, cy, cu, cd, cr, px, py, pu, pd, pr, out_sems,
 ):
-    del wide_in
+    del wide_in, v0_in, v1_in, v2_in, e0_in, e1_in, s_in
 
     def fill(left_ref, right_ref):
         def plane(x, carry):
@@ -312,49 +391,28 @@
     def _():
         fill(chip_ref, core_ref)
 
-    gx = lax.axis_index("gx")
     _, mask_y = grid_masks()
-    ids = ids_ref[...]
     ccoef, pcoef = (cx, cy, cu, cd, cr), (px, py, pu, pd, pr)
-
-    def prepare(x, carry):
-        faces(wide, x, ccoef, pcoef)
-        return carry
-
-    lax.fori_loop(4, 19, prepare, 0, unroll=3)
-
-    def units(x, carry):
-        unit_plane(ids, gx * 16 + x - HALO, e0, x, s_ref, x - HALO)
-        return carry
-
-    lax.fori_loop(6, 18, units, 0, unroll=2)
+    prepare_planes(wide, ccoef, pcoef)
     outs = []
 
     def hand_on(src, dst):
         outs.extend(run_copies([(src, dst)], out_sems, len(outs)))
 
-    def sweep(stencil, src, dst, coeffs, first, reach, row, keep):
-        def plane(x, carry):
-            def emit(y, out):
-                if dst is not None:
-                    dst[x, tile_at(y), :] = out
-                if keep[0] <= y < keep[1]:
-                    put_split(s_ref, x - HALO, row, y, out)
-
-            stencil(tiles(src), coeffs, x, 4 - reach, 12 + reach, None, mask_y, emit)
-            return carry
-
-        lax.fori_loop(HALO + first, HALO + 16 - first, plane, 0, unroll=2)
-
-    sweep(source_plane, wide, v0, pcoef, 1, 3, V0, (3, 13))
-    sweep(operator_plane, v0, v1, ccoef, 2, 2, V1, (3, 13))
-    sweep(operator_plane, v1, v2, ccoef, 3, 1, V2, (3, 13))
+    def sweep(stencil, src, dst, coeffs, first, reach, done, row, keep):
+        y0, y1 = 4 - reach, 12 + reach
+        ranges = [(y0, done[0]), (done[1], y1)] if done else [(y0, y1)]
+        sweep_planes(stencil, src, dst, coeffs, first, ranges, mask_y, s_ref, row, keep)
+
+    sweep(source_plane, wide, v0, pcoef, 1, 3, (5, 11), V0, BOTH)
+    sweep(operator_plane, v0, v1, ccoef, 2, 2, (6, 10), V1, BOTH)
+    sweep(operator_plane, v1, v2, ccoef, 3, 1, (7, 9), V2, BOTH)
     hand_on(s_ref.at[pl.ds(1, 3), pl.ds(0, 96)], side_ref.at[pl.ds(0, 3)])
     hand_on(s_ref.at[pl.ds(12, 3), pl.ds(0, 96)], side_ref.at[pl.ds(3, 3)])
-    sweep(operator_plane, e0, e1, ccoef, 3, 1, E1, (3, 13))
+    sweep(operator_plane, e0, e1, ccoef, 3, 1, (5, 11), E1, BOTH)
     hand_on(s_ref.at[pl.ds(4, 8), pl.ds(0, KEPT)], s_hbm)
-    sweep(operator_plane, v2, None, ccoef, 4, 0, V3, (4, 12))
-    sweep(operator_plane, e1, None, ccoef, 4, 0, E2, (4, 12))
+    sweep(operator_plane, v2, None, ccoef, 4, 0, None, V3, BLOCK)
+    sweep(operator_plane, e1, None, ccoef, 4, 0, (6, 10), E2, BLOCK)
 
     gram_ref[...] = gram_of(s_ref, 4)
 
@@ -366,11 +424,7 @@
     wait_all(outs)
 
 
-FIELD = (24, 256, LANES)
-COEFF = (24, 16, LANES)
-
-
-def inner(ids, wide, core, chip):
+def inner(wide, fields, core, chip):
     vmem = pl.BlockSpec(memory_space=pltpu.VMEM)
     shape = jax.ShapeDtypeStruct
     field = shape(FIELD, jnp.float32)
@@ -378,36 +432,30 @@
         inner_kernel,
         out_shape=(
             shape((24, 288, LANES), jnp.float32),
-            field, field, field,
+            field, field, field, field, field,
+            shape((16, ALL_ROWS, WIDE), jnp.bfloat16),
             shape((6, 96, WIDE), jnp.bfloat16),
             shape((KEPT, ALL_ROWS), jnp.float32),
             pltpu.HBM((8, KEPT, WIDE), jnp.bfloat16),
-        ),
-        in_specs=[vmem] * 4,
-        out_specs=(vmem,) * 6 + (pl.BlockSpec(memory_space=pltpu.HBM),),
-        scratch_shapes=[pltpu.VMEM(FIELD, jnp.float32)] * 2
-        + [pltpu.VMEM((16, ALL_ROWS, WIDE), jnp.bfloat16)]
-        + [pltpu.VMEM(COEFF, jnp.float32)] * 10
-        + [pltpu.SemaphoreType.DMA((3,))],
-        input_output_aliases={1: 0},
-        compiler_params=pltpu.CompilerParams(vmem_limit_bytes=VMEM_INNER * MB),
+        )
+        + (shape(COEFF, jnp.float32),) * 10,
+        in_specs=[vmem] * 9,
+        out_specs=(vmem,) * 9 + (pl.BlockSpec(memory_space=pltpu.HBM),) + (vmem,) * 10,
+        scratch_shapes=[pltpu.SemaphoreType.DMA((3,))],
+        input_output_aliases={i: i for i in range(7)},
+        compiler_params=pltpu.CompilerParams(vmem_limit_bytes=10 * MB),
         cost_estimate=pl.CostEstimate(
             flops=4 * 10**9, bytes_accessed=16 * 10**6, transcendentals=0
         ),
         name="inner",
-    )(ids, wide, core, chip)
-
-
-VMEM_INNER = 36
-VMEM_EDGE = 36
+    )(wide, *fields, core, chip)
 
 
 def edge_kernel(
-    ids_ref, a_ref, b_ref, a_corner, b_corner, wide_in, v0_in, v1_in, v2_in, side_ref, first_gram,
-    wide, v0, v1, v2, pay_ref, s_hbm, bg_hbm,
-    e0, e1, s_ref, gram, cx, cy, cu, cd, cr, px, py, pu, pd, pr, out_sems,
+    ids_ref, a_ref, b_ref, a_corner, b_corner, side_ref, first_gram, *refs
 ):
-    del wide_in, v0_in, v1_in, v2_in
+    wide, v0, v1, v2, *coeffs = refs[14:28]
+    pay_ref, s_hbm, bg_hbm, e0, e1, s_ref, gram, out_sems = refs[28:]
     gx = lax.axis_index("gx")
     mask_x, mask_y = grid_masks()
     ids = ids_ref[...]
@@ -434,13 +482,13 @@
         s_ref[2 + i, 0:rows, :] = side_ref[i, 0:rows, :]
         s_ref[7 - i, 0:rows, :] = side_ref[5 - i, 0:rows, :]
 
-    ccoef, pcoef = (cx, cy, cu, cd, cr), (px, py, pu, pd, pr)
+    ccoef, pcoef = coeffs[:5], coeffs[5:]
 
     def prepare(i, carry):
-        faces(wide, jnp.where(i < 9, i, i + 5), ccoef, pcoef)
+        faces(wide, jnp.where(i < 5, i, i + 14), ccoef, pcoef)
         return carry
 
-    lax.fori_loop(0, 18, prepare, 0, unroll=3)
+    lax.fori_loop(0, 9, prepare, 0, unroll=3)
 
     def mirrored(low, count, body):
         for x in range(low, low + count):
@@ -517,34 +565,32 @@
     wait_all(outs)
 
 
-def edge(ids, a, b, a_corner, b_corner, wide, v0, v1, v2, side, gram):
+def edge(ids, a, b, a_corner, b_corner, kept, side, gram):
     vmem = pl.BlockSpec(memory_space=pltpu.VMEM)
     hbm = pl.BlockSpec(memory_space=pltpu.HBM)
     shape = jax.ShapeDtypeStruct
-    field = shape(FIELD, jnp.float32)
+    count = len(kept)
     outs = pl.pallas_call(
         edge_kernel,
-        out_shape=(
-            shape((24, 288, LANES), jnp.float32),
-            field, field, field,
+        out_shape=tuple(shape(v.shape, v.dtype) for v in kept)
+        + (
             shape((32, LANES), jnp.float32),
             pltpu.HBM((10, KEPT, WIDE), jnp.bfloat16),
             pltpu.HBM((18, 160, LANES), jnp.float32),
         ),
-        in_specs=[vmem] * 11,
-        out_specs=(vmem,) * 5 + (hbm,) * 2,
+        in_specs=[vmem] * (7 + count),
+        out_specs=(vmem,) * (count + 1) + (hbm,) * 2,
         scratch_shapes=[pltpu.VMEM(FIELD, jnp.float32)] * 2
         + [
             pltpu.VMEM((11, ALL_ROWS, WIDE), jnp.bfloat16),
             pltpu.VMEM((KEPT, ALL_ROWS), jnp.float32),
-        ]
-        + [pltpu.VMEM(COEFF, jnp.float32)] * 10
-        + [pltpu.SemaphoreType.DMA((5,))],
-        input_output_aliases={5: 0, 6: 1, 7: 2, 8: 3},
-        compiler_params=pltpu.CompilerParams(vmem_limit_bytes=VMEM_EDGE * MB),
+            pltpu.SemaphoreType.DMA((5,)),
+        ],
+        input_output_aliases={7 + i: i for i in range(count)},
+        compiler_params=pltpu.CompilerParams(vmem_limit_bytes=24 * MB),
         name="edge",
-    )(ids, a, b, a_corner, b_corner, wide, v0, v1, v2, side, gram)
-    return outs[4:]
+    )(ids, a, b, a_corner, b_corner, side, gram, *kept)
+    return outs[count:]
 
 
 def matmul(a, b, dims=((1,), (0,))):
@@ -606,10 +652,12 @@
 
 
 def final_kernel(
-    pattern_ref, parts_ref, bg_hbm, mid_hbm, edge_hbm,
-    out_ref, sens_ref, bg, adj, s_ref, mix_ref, sems, *, damping,
+    pairing_hbm, parts_hbm, bg_hbm, mid_hbm, edge_hbm,
+    out_ref, sens_ref, pairing_ref, parts_ref, bg, adj, s_ref, mix_ref, sems, *, damping,
 ):
     pairs = [
+        (parts_hbm, parts_ref),
+        (pairing_hbm, pairing_ref),
         (edge_hbm.at[pl.ds(0, 5)], s_ref.at[pl.ds(0, 5)]),
         (mid_hbm, s_ref.at[pl.ds(5, 8)]),
         (edge_hbm.at[pl.ds(5, 5)], s_ref.at[pl.ds(13, 5)]),
@@ -621,6 +669,7 @@
     def _():
         for c in copies:
             c.start()
+        wait_all(copies[:2])
 
     total = jnp.sum(parts_ref[...], axis=0)
 
@@ -633,14 +682,8 @@
     e = [part(k) for k in range(11, 15)]
     y = galerkin(*m[:4])
 
-    lane = lax.broadcasted_iota(jnp.int32, (F, F), 1)
-    sub = lax.broadcasted_iota(jnp.int32, (F, F), 0)
-    first, second = jnp.zeros((F, F), jnp.int32), jnp.zeros((F, F), jnp.int32)
-    for i in range(F):
-        first = jnp.where(sub == i, pattern_ref[i, 0], first)
-        second = jnp.where(sub == i, pattern_ref[i, 1], second)
-    pairing = jnp.where(lane == first, 1.0, 0.0) - jnp.where(lane == second, 1.0, 0.0)
-    w = matmul(8.0 * matmul(pairing, pairing, ((0,), (0,))), jnp.concatenate(p[:2], axis=0), ((1,), (1,)))
+    pairing = pairing_ref[:, 0:F]
+    w = matmul(8.0 * matmul(pairing, pairing, ((1,), (1,))), jnp.concatenate(p[:2], axis=0), ((1,), (1,)))
     forms = []
     for k in range(4):
         inside = jnp.concatenate(
@@ -671,7 +714,7 @@
     hi = mix.astype(jnp.bfloat16)
     mix_ref[0:32, :] = hi
     mix_ref[32:64, :] = (mix - hi.astype(jnp.float32)).astype(jnp.bfloat16)
-    wait_all(copies)
+    wait_all(copies[2:])
     both = mix_ref[...]
 
     def combine(x, lanes):
@@ -726,7 +769,7 @@
     sens_plane(16)
 
 
-def final(pattern, parts, bg, mid, edges, damping):
+def final(pairing, parts, bg, mid, edges, damping):
     vmem = pl.BlockSpec(memory_space=pltpu.VMEM)
     hbm = pl.BlockSpec(memory_space=pltpu.HBM)
 
@@ -739,17 +782,19 @@
             jax.ShapeDtypeStruct((2048, LANES), jnp.float32),
             jax.ShapeDtypeStruct((16, 8, LANES), jnp.float32),
         ),
-        in_specs=[pl.BlockSpec(memory_space=pltpu.SMEM), vmem] + [hbm] * 3,
+        in_specs=[hbm] * 5,
         scratch_shapes=[
+            pltpu.VMEM((F, LANES), jnp.float32),
+            pltpu.VMEM((F, 32, LANES), jnp.float32),
             pltpu.VMEM((18, 160, LANES), jnp.float32),
             pltpu.VMEM((18, 160, LANES), jnp.float32),
             pltpu.VMEM((18, KEPT, WIDE), jnp.bfloat16),
             pltpu.VMEM((64, KEPT), jnp.bfloat16),
-            pltpu.SemaphoreType.DMA((4,)),
+            pltpu.SemaphoreType.DMA((6,)),
         ],
         compiler_params=pltpu.CompilerParams(vmem_limit_bytes=56 * MB),
         name="final",
-    )(pattern, parts, bg, mid, edges)
+    )(pairing, pltpu.with_memory_space_constraint(parts, pltpu.HBM), bg, mid, edges)
 
 
 def spread(block, axis, count, groups=None):
@@ -765,17 +810,20 @@
 def on_device(background, conductivity, perturbation, electrodes, pattern):
     size_x, size_y, size_z = conductivity.shape
     count_x, count_y = lax.axis_size("gx"), lax.axis_size("gy")
-    wide, core, chip, a, b, ids = pack(background, conductivity, perturbation, electrodes)
+    wide, core, chip, a, b, ids, pairing = pack(
+        background, conductivity, perturbation, electrodes, pattern
+    )
     a = lax.ppermute(a, "gx", swaps(0, count_x))
     b = lax.ppermute(b, "gx", swaps(1, count_x))
     chip = lax.ppermute(chip, "gy", swaps(1, count_y))
     core = lax.ppermute(core, "gy", swaps(0, count_y))
+    fields = early(ids, wide)
     a_corner, b_corner = pack_corners(core, chip)
     a_corner = lax.ppermute(a_corner, "gx", swaps(0, count_x))
     b_corner = lax.ppermute(b_corner, "gx", swaps(1, count_x))
-    wide, v0, v1, v2, side, gram, mid = inner(ids, wide, core, chip)
+    wide, v0, v1, v2, _, _, _, side, gram, mid, *coeffs = inner(wide, fields, core, chip)
     pay, edges, bg = edge(
-        ids, a, b, a_corner, b_corner, wide, v0, v1, v2, side, gram
+        ids, a, b, a_corner, b_corner, [wide, v0, v1, v2, *coeffs], side, gram
     )
     pay = pay + lax.ppermute(pay, "gy", swaps(0, count_y))
     pay = jnp.sum(spread(pay, "gx", count_x), axis=0)
@@ -784,7 +832,7 @@
     parts = spread(pay, "gy", chips, groups)
     cells = size_x * size_y * size_z * count_x * count_y
     damping = 80.0 / math.sqrt(cells)
-    tangent, sens = final(pattern, parts, bg, mid, edges, damping)
+    tangent, sens = final(pairing, parts, bg, mid, edges, damping)
     return tangent.reshape(background.shape), sens
 
 

time: 76.3 us -> 71.9 us (0.942)
  blocking collectives: 18.5 us -> 33.3 us
  waiting for transfers between devices: 14.1 us -> 3.29 us
  starting transfers between devices: 16.9 us -> 9.13 us
  local copies, waits for them, and re-layouts: 2.15 us -> 0.03 us
  Pallas kernels: 23.3 us -> 24.9 us
    all_to_all x1 -> x2, blocking collectives: 18.5 us -> 33.3 us  [spread(): return lax.all_to_all(copies, axis, 0, 0, axis_index_groups=groups)]
    all_to_all x1 -> x0, starting transfers between devices: 9.04 us -> none  [spread(): return lax.all_to_all(copies, axis, 0, 0, axis_index_groups=groups)]
    all_to_all x1 -> x0, waiting for transfers between devices: 6.65 us -> none  [spread(): return lax.all_to_all(copies, axis, 0, 0, axis_index_groups=groups)]
    ppermute x1, waiting for transfers between devices: 6.6 us -> 2.25 us  [on_device(): chip = lax.ppermute(chip, 'gy', swaps(1, count_y))]
    pallas_call x1 -> x2, Pallas kernels: 5.13 us -> 9.1 us  [the longest x1 4.77 us: edge(): pl.pallas_call(edge_kernel, out_shape=tuple((shape(v.shape, v.dtype) for...]
    pallas_call x1, Pallas kernels: 8.21 us -> 6.64 us  [inner(): pl.pallas_call(inner_kernel, out_shape=(shape((24, 288, LANES), jnp.float...]
    ppermute x1, starting transfers between devices: 1.38 us -> 2.94 us  [on_device(): a_corner = lax.ppermute(a_corner, 'gx', swaps(0, count_x))]
    unnamed x5 -> x0, local copies, waits for them, and re-layouts: 1.4 us -> none
  transfers between devices with their start and end apart: 8 -> 7, of which waited for: 3 -> 2; matrix products, arithmetic and copies ran while one was open for 1% -> 0% of each run, Pallas kernels for 11% -> 15%
where the time goes in v5:
time: 71.9 us; the launch traced here: 71.7 us
  blocking collectives  33.3 us (46%)
  Pallas kernels  24.9 us (35%)
  starting transfers between devices  9.13 us (13%)
  waiting for transfers between devices  3.29 us (5%)
  between operations  0.91 us (1%)
    all_to_all x2, blocking collectives, spread(): return lax.all_to_all(copies, axis, 0, 0, axis_index_groups=groups)  33.3 us
    pallas_call x1, Pallas kernels, final(): pl.pallas_call(kernel, out_shape=(jax.ShapeDtypeStruct((2048, LANES), jnp...  7.39 us
    pallas_call x1, Pallas kernels, inner(): pl.pallas_call(inner_kernel, out_shape=(shape((24, 288, LANES), jnp.float...  6.64 us
    pallas_call x1, Pallas kernels, edge(): pl.pallas_call(edge_kernel, out_shape=tuple((shape(v.shape, v.dtype) for...  4.77 us
    pallas_call x1, Pallas kernels, early(): pl.pallas_call(early_kernel, out_shape=(field,) * 5 + (jax.ShapeDtypeStru...  4.34 us
    ppermute x1, starting transfers between devices, on_device(): chip = lax.ppermute(chip, 'gy', swaps(1, count_y))  4.27 us
    ppermute x1, starting transfers between devices, on_device(): a_corner = lax.ppermute(a_corner, 'gx', swaps(0, count_x))  2.94 us
    ppermute x1, waiting for transfers between devices, on_device(): chip = lax.ppermute(chip, 'gy', swaps(1, count_y))  2.25 us
  transfers between devices with their start and end apart: 7, of which 2 were waited for; matrix products, arithmetic and copies ran while one was open for 0% of the time, Pallas kernels for 15%

profile of v5, /device:TPU:2, one launch (start us, length us, event | category | flops | bytes accessed | tf_op | source)
XLA Modules:
  0.0 71.7 jit_solution(16768619789170938671)
XLA Ops:
  0.6 1.8 %pack_y.1 = (f32[24,288,128]{2,1,0:T(8,128)S(1)}, f32[16,72,128]{2,1,0:T(8,128)S(1)}, f32[16,72,128]{2,1,0:T(8,128)S(1)}, f32[4,144,128]{2,1,0:T(8,128)S(1)}, f3...) custom-call(f32[16,16,8,128]{3,2,1,0:T(8,128)} %bg_hbm.1, f32[16,8,128]{2,1,0:T(8,128)} %cond_hbm.1, ...), custom_call_target="tpu_custom_call" | custom-call | tf_op jit(solution)/shard_map/pack_y/pallas_call | solution.py:114
  2.4 0.1 collective-permute-start.2
  2.5 4.3 %collective-permute-start.3 = (f32[16,72,128]{2,1,0:T(8,128)S(1)}, f32[16,72,128]{2,1,0:T(8,128)S(1)}, u32[]{:S(2)}, u32[]{:S(2)}) collective-permute-start(f32[16,72,128]{2,1,0:T(8,128)S(1)} %get-tuple-element.44), channel_id=1, source_target_pairs={{1,2},{3,4},{5,6},{7,8},{9,10},{11,12},{13,14},{15,16},{17,18},{19... | collective-permute-start | bytes 1769480 | tf_op jit(solution)/shard_map/ppermute | solution.py:818
  6.8 0.3 collective-permute-start
  7.1 0.7 collective-permute-start.1
  7.8 4.3 %early.1 = (f32[24,256,128]{2,1,0:T(8,128)S(1)}, f32[24,256,128]{2,1,0:T(8,128)S(1)}, f32[24,256,128]{2,1,0:T(8,128)S(1)}, f32[24,256,128]{2,1,0:T(8,128)S(1)}, ...) custom-call(s32[16,128]{1,0:T(8,128)S(1)} %get-tuple-element.40.ids_ref, ...), custom_call_target="tpu_custom_call" | custom-call | flops 1000000000 | bytes 8000000 | tf_op jit(solution)/shard_map/early/pallas_call | solution.py:355
  12.1 0.0 collective-permute-done.2.core_ref
  12.1 2.3 %collective-permute-done.3.chip_ref = f32[16,72,128]{2,1,0:T(8,128)S(1)} collective-permute-done((f32[16,72,128]{2,1,0:T(8,128)S(1)}, f32[16,72,128]{2,1,0:T(8,128)S(1)}, u32[]{:S(2)}, u32[]{:S(2)}) %collective-permute-start.3) | collective-permute-done | bytes 589856 | tf_op jit(solution)/shard_map/ppermute | solution.py:818
  14.4 2.9 %collective-permute-start.4 = (f32[240,128]{1,0:T(8,128)S(1)}, f32[240,128]{1,0:T(8,128)S(1)}, u32[]{:S(2)}, u32[]{:S(2)}) collective-permute-start(f32[240,128]{1,0:T(8,128)S(1)} %get-tuple-element.45), channel_id=1, source_target_pairs={{0,32},{64,96},{128,160},{192,224},{32,0},{96,64},{160,128},{224,1... | collective-permute-start | bytes 368648 | tf_op jit(solution)/shard_map/ppermute | solution.py:822
  17.3 0.7 collective-permute-start.5
  18.0 6.6 %inner.1 = (f32[24,288,128]{2,1,0:T(8,128)S(1)}, f32[24,256,128]{2,1,0:T(8,128)S(1)}, f32[24,256,128]{2,1,0:T(8,128)S(1)}, f32[24,256,128]{2,1,0:T(8,128)S(1)}, ...) custom-call(f32[24,288,128]{2,1,0:T(8,128)S(1)} %get-tuple-element.4, ...), custom_call_target="tpu_custom_call", output_to_operand_aliasing={{0}: (0, {}), {1}: (1, {}), {2}: (2, {}), {3}: (3, {}), {4}... | custom-call | flops 4000000000 | bytes 16000000 | tf_op jit(solution)/shard_map/inner/pallas_call | solution.py:431
  24.6 0.0 collective-permute-done.a_ref
  24.6 0.0 collective-permute-done.1.b_ref
  24.7 0.0 collective-permute-done.4.a_corner
  24.7 0.0 collective-permute-done.5.b_corner
  24.7 4.8 %edge.1 = (f32[24,288,128]{2,1,0:T(8,128)S(1)}, f32[24,256,128]{2,1,0:T(8,128)S(1)}, f32[24,256,128]{2,1,0:T(8,128)S(1)}, f32[24,256,128]{2,1,0:T(8,128)S(1)}, f...) custom-call(s32[16,128]{1,0:T(8,128)S(1)} %get-tuple-element.40.ids_, ...), custom_call_target="tpu_custom_call", output_to_operand_aliasing={{0}: (7, {}), {1}: (8, {}), {2}: (9, {}), {3}: (10, {}), {4... | custom-call | tf_op jit(solution)/shard_map/edge/pallas_call | solution.py:573
  29.5 0.2 collective-permute-start.6
  29.7 1.0 %collective-permute-done.6 = f32[32,128]{1,0:T(8,128)S(1)} collective-permute-done((f32[32,128]{1,0:T(8,128)S(1)}, f32[32,128]{1,0:T(8,128)S(1)}, u32[]{:S(2)}, u32[]{:S(2)}) %collective-permute-start.6) | collective-permute-done | bytes 16416 | tf_op jit(solution)/shard_map/ppermute | solution.py:828
  30.7 17.4 %all_to_all.10 = f32[8,32,128]{2,1,0:T(8,128)S(1)} all-to-all(f32[8,32,128]{2,1,0:T(8,128)S(1)} %broadcast_in_dim.4), channel_id=1, replica_groups=mesh['gx'=8,'gy'=32] {'gx'}, dimensions={0} | all-to-all | bytes 262144 | tf_op jit(solution)/shard_map/all_to_all | solution.py:802
  48.2 15.9 %all_to_all.11.refs_1_ = f32[16,32,128]{2,1,0:T(8,128)} all-to-all(f32[16,32,128]{2,1,0:T(8,128)S(1)} %broadcast_in_dim.5), channel_id=1, replica_groups={{0,2,4,6,8,10,12,14,16,18,20,22,24,26,28,30},{1,3,5,7,9,11,13,15,17,19,..., dimensions={0} | all-to-all | bytes 524288 | tf_op jit(solution)/shard_map/all_to_all | solution.py:802
  64.1 7.4 %final.1 = (f32[2048,128]{1,0:T(8,128)}, f32[16,8,128]{2,1,0:T(8,128)}) custom-call(f32[16,128]{1,0:T(8,128)} %get-tuple-element.39.refs_0_, f32[16,32,128]{2,1,0:T(8,128)} %all_to_all.11.refs_1_, f32[18,160,128]{2,1,0:T(8,128)} %get-tuple-element.71.refs_2_, bf16[8,144,1280]{2,1,0:T(8,128)(2,1)} %get-tuple-element.72.refs_3_, ...), custom_call_target="tpu_custom_call" | custom-call | tf_op jit(solution)/shard_map/final/pallas_call | solution.py:779
  (5 shorter events, 0.1 us)
Async XLA Ops:
  2.4 9.7 %collective-permute-start.2 = (f32[16,72,128]{2,1,0:T(8,128)S(1)}, f32[16,72,128]{2,1,0:T(8,128)S(1)}, u32[]{:S(2)}, u32[]{:S(2)}) collective-permute-start(f32[16,72,128]{2,1,0:T(8,128)S(1)} %get-tuple-element.43), channel_id=1, source_target_pairs={{0,1},{2,3},{4,5},{6,7},{8,9},{10,11},{12,13},{14,15},{16,17},{18,... | collective-permute-start | bytes 1769480 | tf_op jit(solution)/shard_map/ppermute | solution.py:819
  2.5 11.8 %collective-permute-start.3 = (f32[16,72,128]{2,1,0:T(8,128)S(1)}, f32[16,72,128]{2,1,0:T(8,128)S(1)}, u32[]{:S(2)}, u32[]{:S(2)}) collective-permute-start(f32[16,72,128]{2,1,0:T(8,128)S(1)} %get-tuple-element.44), channel_id=1, source_target_pairs={{1,2},{3,4},{5,6},{7,8},{9,10},{11,12},{13,14},{15,16},{17,18},{19... | collective-permute-start | bytes 1769480 | tf_op jit(solution)/shard_map/ppermute | solution.py:818
  6.8 17.8 %collective-permute-start = (f32[4,144,128]{2,1,0:T(8,128)S(1)}, f32[4,144,128]{2,1,0:T(8,128)S(1)}, u32[]{:S(2)}, u32[]{:S(2)}) collective-permute-start(f32[4,144,128]{2,1,0:T(8,128)S(1)} %get-tuple-element.41), channel_id=1, source_target_pairs={{0,32},{64,96},{128,160},{192,224},{32,0},{96,64},{160,128},{224,1... | collective-permute-start | bytes 884744 | tf_op jit(solution)/shard_map/ppermute | solution.py:816
  7.1 17.6 %collective-permute-start.1 = (f32[4,144,128]{2,1,0:T(8,128)S(1)}, f32[4,144,128]{2,1,0:T(8,128)S(1)}, u32[]{:S(2)}, u32[]{:S(2)}) collective-permute-start(f32[4,144,128]{2,1,0:T(8,128)S(1)} %get-tuple-element.42), channel_id=1, source_target_pairs={{32,64},{96,128},{160,192},{64,32},{128,96},{192,160},{33,65},{97,... | collective-permute-start | bytes 884744 | tf_op jit(solution)/shard_map/ppermute | solution.py:817
  14.4 10.3 %collective-permute-start.4 = (f32[240,128]{1,0:T(8,128)S(1)}, f32[240,128]{1,0:T(8,128)S(1)}, u32[]{:S(2)}, u32[]{:S(2)}) collective-permute-start(f32[240,128]{1,0:T(8,128)S(1)} %get-tuple-element.45), channel_id=1, source_target_pairs={{0,32},{64,96},{128,160},{192,224},{32,0},{96,64},{160,128},{224,1... | collective-permute-start | bytes 368648 | tf_op jit(solution)/shard_map/ppermute | solution.py:822
  17.3 7.3 %collective-permute-start.5 = (f32[240,128]{1,0:T(8,128)S(1)}, f32[240,128]{1,0:T(8,128)S(1)}, u32[]{:S(2)}, u32[]{:S(2)}) collective-permute-start(f32[240,128]{1,0:T(8,128)S(1)} %get-tuple-element.46), channel_id=1, source_target_pairs={{32,64},{96,128},{160,192},{64,32},{128,96},{192,160},{33,65},{97,... | collective-permute-start | bytes 368648 | tf_op jit(solution)/shard_map/ppermute | solution.py:823
  29.5 1.3 %collective-permute-start.6 = (f32[32,128]{1,0:T(8,128)S(1)}, f32[32,128]{1,0:T(8,128)S(1)}, u32[]{:S(2)}, u32[]{:S(2)}) collective-permute-start(f32[32,128]{1,0:T(8,128)S(1)} %get-tuple-element.70), channel_id=1, source_target_pairs={{0,1},{2,3},{4,5},{6,7},{8,9},{10,11},{12,13},{14,15},{16,17},{18,... | collective-permute-start | bytes 49160 | tf_op jit(solution)/shard_map/ppermute | solution.py:828

commit v6 on v5

--- a/solution.py
+++ b/solution.py
@@ -304,10 +304,10 @@
         faces(wide, x, ccoef, pcoef)
         return carry
 
-    lax.fori_loop(HALO, HALO + 15, prepare, 0, unroll=3)
-
-
-def sweep_planes(stencil, src, dst, coeffs, first, ranges, mask_y, s_ref, row, keep, unroll=2):
+    lax.fori_loop(HALO, HALO + 15, prepare, 0, unroll=15)
+
+
+def sweep_planes(stencil, src, dst, coeffs, first, ranges, mask_y, s_ref, row, keep, unroll):
     def plane(x, carry):
         def emit(y, out):
             if dst is not None:
@@ -340,7 +340,8 @@
     lax.fori_loop(6, 18, units, 0, unroll=2)
 
     def sweep(stencil, src, dst, coeffs, first, rows, row):
-        sweep_planes(stencil, src, dst, coeffs, first, [rows], None, s_ref, row, rows)
+        count = 16 - 2 * first
+        sweep_planes(stencil, src, dst, coeffs, first, [rows], None, s_ref, row, rows, count)
 
     sweep(source_plane, wide, v0, pcoef, 1, (5, 11), V0)
     sweep(operator_plane, v0, v1, ccoef, 2, (6, 10), V1)
@@ -402,7 +403,8 @@
     def sweep(stencil, src, dst, coeffs, first, reach, done, row, keep):
         y0, y1 = 4 - reach, 12 + reach
         ranges = [(y0, done[0]), (done[1], y1)] if done else [(y0, y1)]
-        sweep_planes(stencil, src, dst, coeffs, first, ranges, mask_y, s_ref, row, keep)
+        half = 8 - first
+        sweep_planes(stencil, src, dst, coeffs, first, ranges, mask_y, s_ref, row, keep, half)
 
     sweep(source_plane, wide, v0, pcoef, 1, 3, (5, 11), V0, BOTH)
     sweep(operator_plane, v0, v1, ccoef, 2, 2, (6, 10), V1, BOTH)
@@ -488,7 +490,7 @@
         faces(wide, jnp.where(i < 5, i, i + 14), ccoef, pcoef)
         return carry
 
-    lax.fori_loop(0, 9, prepare, 0, unroll=3)
+    lax.fori_loop(0, 9, prepare, 0, unroll=9)
 
     def mirrored(low, count, body):
         for x in range(low, low + count):

time: 71.9 us -> 69.8 us (0.971)
  Pallas kernels: 24.9 us -> 20.5 us
  waiting for transfers between devices: 3.29 us -> 5.44 us
  blocking collectives: 33.3 us -> 34.7 us
  starting transfers between devices: 9.13 us -> 7.92 us
    ppermute x1, waiting for transfers between devices: 2.25 us -> 4.58 us  [on_device(): chip = lax.ppermute(chip, 'gy', swaps(1, count_y))]
    pallas_call x1, Pallas kernels: 4.34 us -> 2.01 us  [early(): pl.pallas_call(early_kernel, out_shape=(field,) * 5 + (jax.ShapeDtypeStru...]
    pallas_call x1, Pallas kernels: 6.64 us -> 4.93 us  [inner(): pl.pallas_call(inner_kernel, out_shape=(shape((24, 288, LANES), jnp.float...]
    ppermute x1, starting transfers between devices: 2.94 us -> 1.38 us  [on_device(): a_corner = lax.ppermute(a_corner, 'gx', swaps(0, count_x))]
    all_to_all x2, blocking collectives: 33.3 us -> 34.7 us  [spread(): return lax.all_to_all(copies, axis, 0, 0, axis_index_groups=groups)]
  transfers between devices with their start and end apart: 7 -> 7, of which waited for: 2 -> 2; matrix products, arithmetic and copies ran while one was open for 0% -> 0% of each run, Pallas kernels for 15% -> 10%
where the time goes in v6:
time: 69.8 us; the launch traced here: 69.5 us
  blocking collectives  34.7 us (50%)
  Pallas kernels  20.5 us (29%)
  starting transfers between devices  7.92 us (11%)
  waiting for transfers between devices  5.44 us (8%)
  between operations  0.91 us (1%)
    all_to_all x2, blocking collectives, spread(): return lax.all_to_all(copies, axis, 0, 0, axis_index_groups=groups)  34.7 us
    pallas_call x1, Pallas kernels, final(): pl.pallas_call(kernel, out_shape=(jax.ShapeDtypeStruct((2048, LANES), jnp...  7.38 us
    pallas_call x1, Pallas kernels, inner(): pl.pallas_call(inner_kernel, out_shape=(shape((24, 288, LANES), jnp.float...  4.93 us
    ppermute x1, waiting for transfers between devices, on_device(): chip = lax.ppermute(chip, 'gy', swaps(1, count_y))  4.58 us
    pallas_call x1, Pallas kernels, edge(): pl.pallas_call(edge_kernel, out_shape=tuple((shape(v.shape, v.dtype) for...  4.38 us
    ppermute x1, starting transfers between devices, on_device(): chip = lax.ppermute(chip, 'gy', swaps(1, count_y))  4.27 us
    pallas_call x1, Pallas kernels, early(): pl.pallas_call(early_kernel, out_shape=(field,) * 5 + (jax.ShapeDtypeStru...  2.01 us
    pallas_call x1, Pallas kernels, pack(): pl.pallas_call(pack_kernel, out_shape=(shape((24, 288, LANES), jnp.float3...  1.79 us
  transfers between devices with their start and end apart: 7, of which 2 were waited for; matrix products, arithmetic and copies ran while one was open for 0% of the time, Pallas kernels for 10%

profile of v6, /device:TPU:2, one launch (start us, length us, event | category | flops | bytes accessed | tf_op | source)
XLA Modules:
  0.0 69.5 jit_solution(14647854941987558467)
XLA Ops:
  0.6 1.8 %pack_y.1 = (f32[24,288,128]{2,1,0:T(8,128)S(1)}, f32[16,72,128]{2,1,0:T(8,128)S(1)}, f32[16,72,128]{2,1,0:T(8,128)S(1)}, f32[4,144,128]{2,1,0:T(8,128)S(1)}, f3...) custom-call(f32[16,16,8,128]{3,2,1,0:T(8,128)} %bg_hbm.1, f32[16,8,128]{2,1,0:T(8,128)} %cond_hbm.1, ...), custom_call_target="tpu_custom_call" | custom-call | tf_op jit(solution)/shard_map/pack_y/pallas_call | solution.py:114
  2.4 0.1 collective-permute-start.2
  2.5 4.3 %collective-permute-start.3 = (f32[16,72,128]{2,1,0:T(8,128)S(1)}, f32[16,72,128]{2,1,0:T(8,128)S(1)}, u32[]{:S(2)}, u32[]{:S(2)}) collective-permute-start(f32[16,72,128]{2,1,0:T(8,128)S(1)} %get-tuple-element.44), channel_id=1, source_target_pairs={{1,2},{3,4},{5,6},{7,8},{9,10},{11,12},{13,14},{15,16},{17,18},{19... | collective-permute-start | bytes 1769480 | tf_op jit(solution)/shard_map/ppermute | solution.py:820
  6.8 0.3 collective-permute-start
  7.1 0.7 collective-permute-start.1
  7.8 2.0 %early.1 = (f32[24,256,128]{2,1,0:T(8,128)S(1)}, f32[24,256,128]{2,1,0:T(8,128)S(1)}, f32[24,256,128]{2,1,0:T(8,128)S(1)}, f32[24,256,128]{2,1,0:T(8,128)S(1)}, ...) custom-call(s32[16,128]{1,0:T(8,128)S(1)} %get-tuple-element.40.ids_ref, ...), custom_call_target="tpu_custom_call" | custom-call | flops 1000000000 | bytes 8000000 | tf_op jit(solution)/shard_map/early/pallas_call | solution.py:356
  9.8 0.0 collective-permute-done.2.core_ref
  9.8 4.6 %collective-permute-done.3.chip_ref = f32[16,72,128]{2,1,0:T(8,128)S(1)} collective-permute-done((f32[16,72,128]{2,1,0:T(8,128)S(1)}, f32[16,72,128]{2,1,0:T(8,128)S(1)}, u32[]{:S(2)}, u32[]{:S(2)}) %collective-permute-start.3) | collective-permute-done | bytes 589856 | tf_op jit(solution)/shard_map/ppermute | solution.py:820
  14.4 1.4 %collective-permute-start.4 = (f32[240,128]{1,0:T(8,128)S(1)}, f32[240,128]{1,0:T(8,128)S(1)}, u32[]{:S(2)}, u32[]{:S(2)}) collective-permute-start(f32[240,128]{1,0:T(8,128)S(1)} %get-tuple-element.45), channel_id=1, source_target_pairs={{0,32},{64,96},{128,160},{192,224},{32,0},{96,64},{160,128},{224,1... | collective-permute-start | bytes 368648 | tf_op jit(solution)/shard_map/ppermute | solution.py:824
  15.8 0.7 collective-permute-start.5
  16.4 4.9 %inner.1 = (f32[24,288,128]{2,1,0:T(8,128)S(1)}, f32[24,256,128]{2,1,0:T(8,128)S(1)}, f32[24,256,128]{2,1,0:T(8,128)S(1)}, f32[24,256,128]{2,1,0:T(8,128)S(1)}, ...) custom-call(f32[24,288,128]{2,1,0:T(8,128)S(1)} %get-tuple-element.4, ...), custom_call_target="tpu_custom_call", output_to_operand_aliasing={{0}: (0, {}), {1}: (1, {}), {2}: (2, {}), {3}: (3, {}), {4}... | custom-call | flops 4000000000 | bytes 16000000 | tf_op jit(solution)/shard_map/inner/pallas_call | solution.py:433
  21.4 0.0 collective-permute-done.a_ref
  21.4 0.0 collective-permute-done.1.b_ref
  21.4 0.0 collective-permute-done.4.a_corner
  21.4 0.0 collective-permute-done.5.b_corner
  21.4 4.4 %edge.1 = (f32[24,288,128]{2,1,0:T(8,128)S(1)}, f32[24,256,128]{2,1,0:T(8,128)S(1)}, f32[24,256,128]{2,1,0:T(8,128)S(1)}, f32[24,256,128]{2,1,0:T(8,128)S(1)}, f...) custom-call(s32[16,128]{1,0:T(8,128)S(1)} %get-tuple-element.40.ids_, ...), custom_call_target="tpu_custom_call", output_to_operand_aliasing={{0}: (7, {}), {1}: (8, {}), {2}: (9, {}), {3}: (10, {}), {4... | custom-call | tf_op jit(solution)/shard_map/edge/pallas_call | solution.py:575
  25.8 0.6 collective-permute-start.6
  26.4 0.8 %collective-permute-done.6 = f32[32,128]{1,0:T(8,128)S(1)} collective-permute-done((f32[32,128]{1,0:T(8,128)S(1)}, f32[32,128]{1,0:T(8,128)S(1)}, u32[]{:S(2)}, u32[]{:S(2)}) %collective-permute-start.6) | collective-permute-done | bytes 16416 | tf_op jit(solution)/shard_map/ppermute | solution.py:830
  27.2 19.8 %all_to_all.10 = f32[8,32,128]{2,1,0:T(8,128)S(1)} all-to-all(f32[8,32,128]{2,1,0:T(8,128)S(1)} %broadcast_in_dim.4), channel_id=1, replica_groups=mesh['gx'=8,'gy'=32] {'gx'}, dimensions={0} | all-to-all | bytes 262144 | tf_op jit(solution)/shard_map/all_to_all | solution.py:804
  47.0 15.0 %all_to_all.11.refs_1_ = f32[16,32,128]{2,1,0:T(8,128)} all-to-all(f32[16,32,128]{2,1,0:T(8,128)S(1)} %broadcast_in_dim.5), channel_id=1, replica_groups={{0,2,4,6,8,10,12,14,16,18,20,22,24,26,28,30},{1,3,5,7,9,11,13,15,17,19,..., dimensions={0} | all-to-all | bytes 524288 | tf_op jit(solution)/shard_map/all_to_all | solution.py:804
  62.0 7.4 %final.1 = (f32[2048,128]{1,0:T(8,128)}, f32[16,8,128]{2,1,0:T(8,128)}) custom-call(f32[16,128]{1,0:T(8,128)} %get-tuple-element.39.refs_0_, f32[16,32,128]{2,1,0:T(8,128)} %all_to_all.11.refs_1_, f32[18,160,128]{2,1,0:T(8,128)} %get-tuple-element.71.refs_2_, bf16[8,144,1280]{2,1,0:T(8,128)(2,1)} %get-tuple-element.72.refs_3_, ...), custom_call_target="tpu_custom_call" | custom-call | tf_op jit(solution)/shard_map/final/pallas_call | solution.py:781
  (5 shorter events, 0.1 us)
Async XLA Ops:
  2.4 7.3 %collective-permute-start.2 = (f32[16,72,128]{2,1,0:T(8,128)S(1)}, f32[16,72,128]{2,1,0:T(8,128)S(1)}, u32[]{:S(2)}, u32[]{:S(2)}) collective-permute-start(f32[16,72,128]{2,1,0:T(8,128)S(1)} %get-tuple-element.43), channel_id=1, source_target_pairs={{0,1},{2,3},{4,5},{6,7},{8,9},{10,11},{12,13},{14,15},{16,17},{18,... | collective-permute-start | bytes 1769480 | tf_op jit(solution)/shard_map/ppermute | solution.py:821
  2.5 11.8 %collective-permute-start.3 = (f32[16,72,128]{2,1,0:T(8,128)S(1)}, f32[16,72,128]{2,1,0:T(8,128)S(1)}, u32[]{:S(2)}, u32[]{:S(2)}) collective-permute-start(f32[16,72,128]{2,1,0:T(8,128)S(1)} %get-tuple-element.44), channel_id=1, source_target_pairs={{1,2},{3,4},{5,6},{7,8},{9,10},{11,12},{13,14},{15,16},{17,18},{19... | collective-permute-start | bytes 1769480 | tf_op jit(solution)/shard_map/ppermute | solution.py:820
  6.8 14.6 %collective-permute-start = (f32[4,144,128]{2,1,0:T(8,128)S(1)}, f32[4,144,128]{2,1,0:T(8,128)S(1)}, u32[]{:S(2)}, u32[]{:S(2)}) collective-permute-start(f32[4,144,128]{2,1,0:T(8,128)S(1)} %get-tuple-element.41), channel_id=1, source_target_pairs={{0,32},{64,96},{128,160},{192,224},{32,0},{96,64},{160,128},{224,1... | collective-permute-start | bytes 884744 | tf_op jit(solution)/shard_map/ppermute | solution.py:818
  7.1 14.3 %collective-permute-start.1 = (f32[4,144,128]{2,1,0:T(8,128)S(1)}, f32[4,144,128]{2,1,0:T(8,128)S(1)}, u32[]{:S(2)}, u32[]{:S(2)}) collective-permute-start(f32[4,144,128]{2,1,0:T(8,128)S(1)} %get-tuple-element.42), channel_id=1, source_target_pairs={{32,64},{96,128},{160,192},{64,32},{128,96},{192,160},{33,65},{97,... | collective-permute-start | bytes 884744 | tf_op jit(solution)/shard_map/ppermute | solution.py:819
  14.4 7.0 %collective-permute-start.4 = (f32[240,128]{1,0:T(8,128)S(1)}, f32[240,128]{1,0:T(8,128)S(1)}, u32[]{:S(2)}, u32[]{:S(2)}) collective-permute-start(f32[240,128]{1,0:T(8,128)S(1)} %get-tuple-element.45), channel_id=1, source_target_pairs={{0,32},{64,96},{128,160},{192,224},{32,0},{96,64},{160,128},{224,1... | collective-permute-start | bytes 368648 | tf_op jit(solution)/shard_map/ppermute | solution.py:824
  15.8 5.6 %collective-permute-start.5 = (f32[240,128]{1,0:T(8,128)S(1)}, f32[240,128]{1,0:T(8,128)S(1)}, u32[]{:S(2)}, u32[]{:S(2)}) collective-permute-start(f32[240,128]{1,0:T(8,128)S(1)} %get-tuple-element.46), channel_id=1, source_target_pairs={{32,64},{96,128},{160,192},{64,32},{128,96},{192,160},{33,65},{97,... | collective-permute-start | bytes 368648 | tf_op jit(solution)/shard_map/ppermute | solution.py:825
  25.8 1.4 %collective-permute-start.6 = (f32[32,128]{1,0:T(8,128)S(1)}, f32[32,128]{1,0:T(8,128)S(1)}, u32[]{:S(2)}, u32[]{:S(2)}) collective-permute-start(f32[32,128]{1,0:T(8,128)S(1)} %get-tuple-element.70), channel_id=1, source_target_pairs={{0,1},{2,3},{4,5},{6,7},{8,9},{10,11},{12,13},{14,15},{16,17},{18,... | collective-permute-start | bytes 49160 | tf_op jit(solution)/shard_map/ppermute | solution.py:830

commit v7 on v6

--- a/solution.py
+++ b/solution.py
@@ -764,7 +764,7 @@
         store(x + 2, out)
         return carry
 
-    lax.fori_loop(1, 15, plane, 0, unroll=7)
+    lax.fori_loop(1, 15, plane, 0, unroll=14)
     out = combine(17, ends)
     sens_plane(15)
     store_end(17, out)

time: 69.8 us -> 69.5 us (level)
  no operation moved by 1% of the time
where the time goes in v7:
time: 69.5 us; the launch traced here: 69.3 us
  blocking collectives  34.7 us (50%)
  Pallas kernels  20.2 us (29%)
  starting transfers between devices  7.92 us (11%)
  waiting for transfers between devices  5.44 us (8%)
  between operations  0.91 us (1%)
    all_to_all x2, blocking collectives, spread(): return lax.all_to_all(copies, axis, 0, 0, axis_index_groups=groups)  34.7 us
    pallas_call x1, Pallas kernels, final(): pl.pallas_call(kernel, out_shape=(jax.ShapeDtypeStruct((2048, LANES), jnp...  7.12 us
    pallas_call x1, Pallas kernels, inner(): pl.pallas_call(inner_kernel, out_shape=(shape((24, 288, LANES), jnp.float...  4.93 us
    ppermute x1, waiting for transfers between devices, on_device(): chip = lax.ppermute(chip, 'gy', swaps(1, count_y))  4.58 us
    pallas_call x1, Pallas kernels, edge(): pl.pallas_call(edge_kernel, out_shape=tuple((shape(v.shape, v.dtype) for...  4.38 us
    ppermute x1, starting transfers between devices, on_device(): chip = lax.ppermute(chip, 'gy', swaps(1, count_y))  4.27 us
    pallas_call x1, Pallas kernels, early(): pl.pallas_call(early_kernel, out_shape=(field,) * 5 + (jax.ShapeDtypeStru...  2.01 us
    pallas_call x1, Pallas kernels, pack(): pl.pallas_call(pack_kernel, out_shape=(shape((24, 288, LANES), jnp.float3...  1.79 us
  transfers between devices with their start and end apart: 7, of which 2 were waited for; matrix products, arithmetic and copies ran while one was open for 0% of the time, Pallas kernels for 10%

profile of v7, /device:TPU:2, one launch (start us, length us, event | category | flops | bytes accessed | tf_op | source)
XLA Modules:
  0.0 69.3 jit_solution(13118512895188232327)
XLA Ops:
  0.6 1.8 %pack_y.1 = (f32[24,288,128]{2,1,0:T(8,128)S(1)}, f32[16,72,128]{2,1,0:T(8,128)S(1)}, f32[16,72,128]{2,1,0:T(8,128)S(1)}, f32[4,144,128]{2,1,0:T(8,128)S(1)}, f3...) custom-call(f32[16,16,8,128]{3,2,1,0:T(8,128)} %bg_hbm.1, f32[16,8,128]{2,1,0:T(8,128)} %cond_hbm.1, ...), custom_call_target="tpu_custom_call" | custom-call | tf_op jit(solution)/shard_map/pack_y/pallas_call | solution.py:114
  2.4 0.1 collective-permute-start.2
  2.5 4.3 %collective-permute-start.3 = (f32[16,72,128]{2,1,0:T(8,128)S(1)}, f32[16,72,128]{2,1,0:T(8,128)S(1)}, u32[]{:S(2)}, u32[]{:S(2)}) collective-permute-start(f32[16,72,128]{2,1,0:T(8,128)S(1)} %get-tuple-element.44), channel_id=1, source_target_pairs={{1,2},{3,4},{5,6},{7,8},{9,10},{11,12},{13,14},{15,16},{17,18},{19... | collective-permute-start | bytes 1769480 | tf_op jit(solution)/shard_map/ppermute | solution.py:820
  6.8 0.3 collective-permute-start
  7.1 0.7 collective-permute-start.1
  7.8 2.0 %early.1 = (f32[24,256,128]{2,1,0:T(8,128)S(1)}, f32[24,256,128]{2,1,0:T(8,128)S(1)}, f32[24,256,128]{2,1,0:T(8,128)S(1)}, f32[24,256,128]{2,1,0:T(8,128)S(1)}, ...) custom-call(s32[16,128]{1,0:T(8,128)S(1)} %get-tuple-element.40.ids_ref, ...), custom_call_target="tpu_custom_call" | custom-call | flops 1000000000 | bytes 8000000 | tf_op jit(solution)/shard_map/early/pallas_call | solution.py:356
  9.8 0.0 collective-permute-done.2.core_ref
  9.8 4.6 %collective-permute-done.3.chip_ref = f32[16,72,128]{2,1,0:T(8,128)S(1)} collective-permute-done((f32[16,72,128]{2,1,0:T(8,128)S(1)}, f32[16,72,128]{2,1,0:T(8,128)S(1)}, u32[]{:S(2)}, u32[]{:S(2)}) %collective-permute-start.3) | collective-permute-done | bytes 589856 | tf_op jit(solution)/shard_map/ppermute | solution.py:820
  14.4 1.4 %collective-permute-start.4 = (f32[240,128]{1,0:T(8,128)S(1)}, f32[240,128]{1,0:T(8,128)S(1)}, u32[]{:S(2)}, u32[]{:S(2)}) collective-permute-start(f32[240,128]{1,0:T(8,128)S(1)} %get-tuple-element.45), channel_id=1, source_target_pairs={{0,32},{64,96},{128,160},{192,224},{32,0},{96,64},{160,128},{224,1... | collective-permute-start | bytes 368648 | tf_op jit(solution)/shard_map/ppermute | solution.py:824
  15.8 0.7 collective-permute-start.5
  16.4 4.9 %inner.1 = (f32[24,288,128]{2,1,0:T(8,128)S(1)}, f32[24,256,128]{2,1,0:T(8,128)S(1)}, f32[24,256,128]{2,1,0:T(8,128)S(1)}, f32[24,256,128]{2,1,0:T(8,128)S(1)}, ...) custom-call(f32[24,288,128]{2,1,0:T(8,128)S(1)} %get-tuple-element.4, ...), custom_call_target="tpu_custom_call", output_to_operand_aliasing={{0}: (0, {}), {1}: (1, {}), {2}: (2, {}), {3}: (3, {}), {4}... | custom-call | flops 4000000000 | bytes 16000000 | tf_op jit(solution)/shard_map/inner/pallas_call | solution.py:433
  21.4 0.0 collective-permute-done.a_ref
  21.4 0.0 collective-permute-done.1.b_ref
  21.4 0.0 collective-permute-done.4.a_corner
  21.4 0.0 collective-permute-done.5.b_corner
  21.4 4.4 %edge.1 = (f32[24,288,128]{2,1,0:T(8,128)S(1)}, f32[24,256,128]{2,1,0:T(8,128)S(1)}, f32[24,256,128]{2,1,0:T(8,128)S(1)}, f32[24,256,128]{2,1,0:T(8,128)S(1)}, f...) custom-call(s32[16,128]{1,0:T(8,128)S(1)} %get-tuple-element.40.ids_, ...), custom_call_target="tpu_custom_call", output_to_operand_aliasing={{0}: (7, {}), {1}: (8, {}), {2}: (9, {}), {3}: (10, {}), {4... | custom-call | tf_op jit(solution)/shard_map/edge/pallas_call | solution.py:575
  25.8 0.6 collective-permute-start.6
  26.4 0.8 %collective-permute-done.6 = f32[32,128]{1,0:T(8,128)S(1)} collective-permute-done((f32[32,128]{1,0:T(8,128)S(1)}, f32[32,128]{1,0:T(8,128)S(1)}, u32[]{:S(2)}, u32[]{:S(2)}) %collective-permute-start.6) | collective-permute-done | bytes 16416 | tf_op jit(solution)/shard_map/ppermute | solution.py:830
  27.2 19.8 %all_to_all.10 = f32[8,32,128]{2,1,0:T(8,128)S(1)} all-to-all(f32[8,32,128]{2,1,0:T(8,128)S(1)} %broadcast_in_dim.4), channel_id=1, replica_groups=mesh['gx'=8,'gy'=32] {'gx'}, dimensions={0} | all-to-all | bytes 262144 | tf_op jit(solution)/shard_map/all_to_all | solution.py:804
  47.0 15.0 %all_to_all.11.refs_1_ = f32[16,32,128]{2,1,0:T(8,128)} all-to-all(f32[16,32,128]{2,1,0:T(8,128)S(1)} %broadcast_in_dim.5), channel_id=1, replica_groups={{0,2,4,6,8,10,12,14,16,18,20,22,24,26,28,30},{1,3,5,7,9,11,13,15,17,19,..., dimensions={0} | all-to-all | bytes 524288 | tf_op jit(solution)/shard_map/all_to_all | solution.py:804
  62.0 7.1 %final.1 = (f32[2048,128]{1,0:T(8,128)}, f32[16,8,128]{2,1,0:T(8,128)}) custom-call(f32[16,128]{1,0:T(8,128)} %get-tuple-element.39.refs_0_, f32[16,32,128]{2,1,0:T(8,128)} %all_to_all.11.refs_1_, f32[18,160,128]{2,1,0:T(8,128)} %get-tuple-element.71.refs_2_, bf16[8,144,1280]{2,1,0:T(8,128)(2,1)} %get-tuple-element.72.refs_3_, ...), custom_call_target="tpu_custom_call" | custom-call | tf_op jit(solution)/shard_map/final/pallas_call | solution.py:781
  (5 shorter events, 0.1 us)
Async XLA Ops:
  2.4 7.3 %collective-permute-start.2 = (f32[16,72,128]{2,1,0:T(8,128)S(1)}, f32[16,72,128]{2,1,0:T(8,128)S(1)}, u32[]{:S(2)}, u32[]{:S(2)}) collective-permute-start(f32[16,72,128]{2,1,0:T(8,128)S(1)} %get-tuple-element.43), channel_id=1, source_target_pairs={{0,1},{2,3},{4,5},{6,7},{8,9},{10,11},{12,13},{14,15},{16,17},{18,... | collective-permute-start | bytes 1769480 | tf_op jit(solution)/shard_map/ppermute | solution.py:821
  2.5 11.8 %collective-permute-start.3 = (f32[16,72,128]{2,1,0:T(8,128)S(1)}, f32[16,72,128]{2,1,0:T(8,128)S(1)}, u32[]{:S(2)}, u32[]{:S(2)}) collective-permute-start(f32[16,72,128]{2,1,0:T(8,128)S(1)} %get-tuple-element.44), channel_id=1, source_target_pairs={{1,2},{3,4},{5,6},{7,8},{9,10},{11,12},{13,14},{15,16},{17,18},{19... | collective-permute-start | bytes 1769480 | tf_op jit(solution)/shard_map/ppermute | solution.py:820
  6.8 14.6 %collective-permute-start = (f32[4,144,128]{2,1,0:T(8,128)S(1)}, f32[4,144,128]{2,1,0:T(8,128)S(1)}, u32[]{:S(2)}, u32[]{:S(2)}) collective-permute-start(f32[4,144,128]{2,1,0:T(8,128)S(1)} %get-tuple-element.41), channel_id=1, source_target_pairs={{0,32},{64,96},{128,160},{192,224},{32,0},{96,64},{160,128},{224,1... | collective-permute-start | bytes 884744 | tf_op jit(solution)/shard_map/ppermute | solution.py:818
  7.1 14.3 %collective-permute-start.1 = (f32[4,144,128]{2,1,0:T(8,128)S(1)}, f32[4,144,128]{2,1,0:T(8,128)S(1)}, u32[]{:S(2)}, u32[]{:S(2)}) collective-permute-start(f32[4,144,128]{2,1,0:T(8,128)S(1)} %get-tuple-element.42), channel_id=1, source_target_pairs={{32,64},{96,128},{160,192},{64,32},{128,96},{192,160},{33,65},{97,... | collective-permute-start | bytes 884744 | tf_op jit(solution)/shard_map/ppermute | solution.py:819
  14.4 7.0 %collective-permute-start.4 = (f32[240,128]{1,0:T(8,128)S(1)}, f32[240,128]{1,0:T(8,128)S(1)}, u32[]{:S(2)}, u32[]{:S(2)}) collective-permute-start(f32[240,128]{1,0:T(8,128)S(1)} %get-tuple-element.45), channel_id=1, source_target_pairs={{0,32},{64,96},{128,160},{192,224},{32,0},{96,64},{160,128},{224,1... | collective-permute-start | bytes 368648 | tf_op jit(solution)/shard_map/ppermute | solution.py:824
  15.8 5.6 %collective-permute-start.5 = (f32[240,128]{1,0:T(8,128)S(1)}, f32[240,128]{1,0:T(8,128)S(1)}, u32[]{:S(2)}, u32[]{:S(2)}) collective-permute-start(f32[240,128]{1,0:T(8,128)S(1)} %get-tuple-element.46), channel_id=1, source_target_pairs={{32,64},{96,128},{160,192},{64,32},{128,96},{192,160},{33,65},{97,... | collective-permute-start | bytes 368648 | tf_op jit(solution)/shard_map/ppermute | solution.py:825
  25.8 1.4 %collective-permute-start.6 = (f32[32,128]{1,0:T(8,128)S(1)}, f32[32,128]{1,0:T(8,128)S(1)}, u32[]{:S(2)}, u32[]{:S(2)}) collective-permute-start(f32[32,128]{1,0:T(8,128)S(1)} %get-tuple-element.70), channel_id=1, source_target_pairs={{0,1},{2,3},{4,5},{6,7},{8,9},{10,11},{12,13},{14,15},{16,17},{18,... | collective-permute-start | bytes 49160 | tf_op jit(solution)/shard_map/ppermute | solution.py:830
